TPU v7x, 32 devices: a whole 2x2x4 slice. The times are simulated.
32 devices in a mesh: grp: 8 (over y, x, core), hd: 4 (over z).
Axes of the slice: x: 2, y: 2, z: 4, core: 2. Of those that a mesh axis runs over, the one named last changes fastest.
Arguments:
- pixels: bfloat16 [96, 256, 1024], P(('grp', 'hd')), may hold values from -6 to 6
- latents: bfloat16 [96, 256, 1024], P(('grp', 'hd')), may hold values from -6 to 6
- skip: bfloat16 [96, 256, 1024], P(('grp', 'hd')), may hold values from -6 to 6
- counts: int32 [96], P('grp'), may hold values from 1 to 256, as said below
- cotangent: bfloat16 [96, 256, 1024], P(('grp', 'hd')), may hold values from -6 to 6
- attn_in: float32 [6, 1024, 1024], P(None, None, ('grp', 'hd')), may hold values from -0.1875 to 0.1875
- attn_out: float32 [2, 1024, 1024], P(None, None, ('grp', 'hd')), may hold values from -2 to 2
- w_in: float32 [1024, 4096], P(None, ('grp', 'hd')), may hold values from -0.1875 to 0.1875
- w_out: float32 [4096, 1024], P(None, ('grp', 'hd')), may hold values from -0.09375 to 0.09375
- gains: float32 [4, 1024], P(None, ('grp', 'hd')), may hold values from 0.5 to 1.5
- attn_in_first: float32 [6, 1024, 1024], P(None, None, ('grp', 'hd')), may hold values from -896 to 896
- attn_in_second: float32 [6, 1024, 1024], P(None, None, ('grp', 'hd')), may hold values from 12288 to 196608
- attn_out_first: float32 [2, 1024, 1024], P(None, None, ('grp', 'hd')), may hold values from -80 to 80
- attn_out_second: float32 [2, 1024, 1024], P(None, None, ('grp', 'hd')), may hold values from 96 to 1536
- w_in_first: float32 [1024, 4096], P(None, ('grp', 'hd')), may hold values from -256 to 256
- w_in_second: float32 [1024, 4096], P(None, ('grp', 'hd')), may hold values from 1117 to 17873
- w_out_first: float32 [4096, 1024], P(None, ('grp', 'hd')), may hold values from -512 to 512
- w_out_second: float32 [4096, 1024], P(None, ('grp', 'hd')), may hold values from 4423 to 70778
- gains_first: float32 [4, 1024], P(None, ('grp', 'hd')), may hold values from -7524.8325 to 7524.8325
- gains_second: float32 [4, 1024], P(None, ('grp', 'hd')), may hold values from 12288 to 14155776, as said below
Outputs:
- latents_out: bfloat16 [96, 256, 1024], P(('grp', 'hd'))
- pixels_grad: float32 [96, 256, 1024], P(('grp', 'hd'))
- latents_grad: float32 [96, 256, 1024], P(('grp', 'hd'))
- attn_in_moment: float32 [6, 1024, 1024], P(None, None, ('grp', 'hd'))
- attn_in_square: float32 [6, 1024, 1024], P(None, None, ('grp', 'hd'))
- attn_in_new: float32 [6, 1024, 1024], P(None, None, ('grp', 'hd'))
- attn_out_moment: float32 [2, 1024, 1024], P(None, None, ('grp', 'hd'))
- attn_out_square: float32 [2, 1024, 1024], P(None, None, ('grp', 'hd'))
- attn_out_new: float32 [2, 1024, 1024], P(None, None, ('grp', 'hd'))
- w_in_moment: float32 [1024, 4096], P(None, ('grp', 'hd'))
- w_in_square: float32 [1024, 4096], P(None, ('grp', 'hd'))
- w_in_new: float32 [1024, 4096], P(None, ('grp', 'hd'))
- w_out_moment: float32 [4096, 1024], P(None, ('grp', 'hd'))
- w_out_square: float32 [4096, 1024], P(None, ('grp', 'hd'))
- w_out_new: float32 [4096, 1024], P(None, ('grp', 'hd'))
- gains_moment: float32 [4, 1024], P(None, ('grp', 'hd'))
- gains_square: float32 [3, 1024], P(None, ('grp', 'hd'))
- mlp_gain_square: float32 [1024], P(('grp', 'hd'))
- gains_new: float32 [4, 1024], P(None, ('grp', 'hd'))
Inputs may be any that keep to these rules, and one draw needn't show every extreme that they name: The first counts[i] input rows of image i are visible, the rest are padding; some image has all 256 rows visible. `gains_second`: entries are positive.
All inputs are finite; a program needn't handle non-finite values.
Results may differ from a plain program's by a relative error of at most 0.029.
Values may be sent and summed in bfloat16 or wider, within the bound.
No kernel may reach another device: no remote copies, remote signals or barrier semaphores. Data moves between devices by JAX's collectives and lax.ppermute only.
A program may use at most 320 MiB of HBM per device.

v0:
```python
import jax
import jax.numpy as jnp
from jax import lax
from jax.sharding import PartitionSpec as P

NH = 8
STEP = 5


def normed(row_block, gain_row):
    return (
        row_block
        * lax.rsqrt(jnp.mean(row_block * row_block, axis=-1, keepdims=True) + 1e-06)
        * gain_row
    )


def norm_back(row_block, gain_row, upstream):
    outputs, pull_back = jax.vjp(normed, row_block, gain_row)
    return pull_back(upstream)


def project(row_block, matrix):
    return jnp.einsum("bnd,de->bne", row_block, matrix, preferred_element_type=jnp.float32)


def project_back(grad_rows, matrix):
    return jnp.einsum("bne,de->bnd", grad_rows, matrix, preferred_element_type=jnp.float32)


def weight_grad(row_block, grad_rows):
    return jnp.einsum("bnd,bne->de", row_block, grad_rows, preferred_element_type=jnp.float32)


def split_heads(row_block, heads):
    return row_block.reshape(row_block.shape[0], row_block.shape[1], heads, -1)


def owner_view(grad, dim, outer, inner):
    shape = grad.shape
    return grad.reshape(
        shape[:dim] + (outer, inner, shape[dim] // (outer * inner)) + shape[dim + 1 :]
    )


def owner_merge(grad, dim):
    shape = grad.shape
    return grad.reshape(shape[:dim] + (shape[dim + 2],) + shape[dim + 3 :])


def masked_scores(query_heads, key_heads, visible):
    score_scale = query_heads.shape[-1] ** (-0.5)
    scores = jnp.einsum(
        "bqhd,bkhd->bhqk", query_heads, key_heads, preferred_element_type=jnp.float32
    )
    return jnp.where(visible[:, None, None, :], scores * score_scale, -1e30)


def attend_forward(queries, key_rows, value_rows, visible, heads):
    query_heads = split_heads(queries, heads)
    scores = masked_scores(query_heads, split_heads(key_rows, heads), visible)
    highest = jnp.max(scores, axis=-1, keepdims=True)
    exponent = jnp.exp(scores - highest)
    row_total = jnp.sum(exponent, axis=-1, keepdims=True)
    weights = (exponent / row_total).astype(jnp.bfloat16)
    context = jnp.einsum(
        "bhqk,bkhd->bqhd",
        weights,
        split_heads(value_rows, heads),
        preferred_element_type=jnp.float32,
    )
    return (context.reshape(queries.shape).astype(jnp.bfloat16), highest + jnp.log(row_total))


def attend_backward(queries, key_rows, value_rows, visible, log_total, context_grad, heads):
    query_heads = split_heads(queries, heads)
    key_heads = split_heads(key_rows, heads)
    value_heads = split_heads(value_rows, heads)
    grad_heads = split_heads(context_grad, heads)
    score_scale = query_heads.shape[-1] ** (-0.5)
    probs = jnp.exp(masked_scores(query_heads, key_heads, visible) - log_total)
    prob_grad = jnp.einsum(
        "bqhd,bkhd->bhqk", grad_heads, value_heads, preferred_element_type=jnp.float32
    )
    value_grad = jnp.einsum(
        "bhqk,bqhd->bkhd",
        probs.astype(jnp.bfloat16),
        grad_heads,
        preferred_element_type=jnp.float32,
    )
    score_grad = probs * (prob_grad - jnp.sum(probs * prob_grad, axis=-1, keepdims=True))
    score_grad = score_grad.astype(jnp.bfloat16)
    query_grad = jnp.einsum(
        "bhqk,bkhd->bqhd", score_grad, key_heads, preferred_element_type=jnp.float32
    )
    key_grad = jnp.einsum(
        "bhqk,bqhd->bkhd", score_grad, query_heads, preferred_element_type=jnp.float32
    )
    query_grad = (query_grad * score_scale).reshape(queries.shape).astype(jnp.bfloat16)
    key_grad = (key_grad * score_scale).reshape(key_rows.shape).astype(jnp.bfloat16)
    return (query_grad, key_grad, value_grad.reshape(value_rows.shape).astype(jnp.bfloat16))


def adamw(weight, grad, first_old, second_old, learn_rate, decay):
    first_new = 0.5 * first_old + 0.5 * grad
    second_new = 0.5 * second_old + 0.5 * grad * grad
    correction = 1.0 - 0.5**STEP
    normed_step = first_new / correction / (jnp.sqrt(second_new / correction) + 1e-08)
    return (first_new, second_new, weight - learn_rate * (normed_step + decay * weight))


def local(
    pixels,
    latents,
    skip,
    counts,
    cotangent,
    attn_in,
    attn_out,
    w_in,
    w_out,
    gains,
    attn_in_first,
    attn_in_second,
    attn_out_first,
    attn_out_second,
    w_in_first,
    w_in_second,
    w_out_first,
    w_out_second,
    gains_first,
    gains_second,
):
    group_count = lax.axis_size("grp")
    head_devices = lax.axis_size("hd")
    mixing, outward, gain_all = (
        lax.all_gather(attn_in.astype(jnp.bfloat16), ("grp", "hd"), axis=2, tiled=True),
        lax.all_gather(attn_out.astype(jnp.bfloat16), ("grp", "hd"), axis=2, tiled=True),
        lax.all_gather(gains.astype(jnp.bfloat16), ("grp", "hd"), axis=1, tiled=True),
    )
    lift, lower = (
        lax.all_gather(w_in.astype(jnp.bfloat16), ("grp", "hd"), axis=1, tiled=True),
        lax.all_gather(w_out.astype(jnp.bfloat16), ("grp", "hd"), axis=1, tiled=True),
    )
    gain_rows = gain_all.astype(jnp.float32)
    pixel_f = pixels.astype(jnp.float32)
    latent_f = latents.astype(jnp.float32)
    pixel_norm = normed(pixel_f, gain_rows[0]).astype(jnp.bfloat16)
    latent_norm = normed(latent_f, gain_rows[1]).astype(jnp.bfloat16)
    queries = project(latent_norm, mixing[0]).astype(jnp.bfloat16)
    key_rows = project(pixel_norm, mixing[1]).astype(jnp.bfloat16)
    value_rows = project(pixel_norm, mixing[2]).astype(jnp.bfloat16)
    places = jnp.arange(pixels.shape[1])
    head_count = NH // head_devices
    query_group, key_group, value_group = (
        lax.all_to_all(queries, "hd", split_axis=2, concat_axis=0, tiled=True),
        lax.all_to_all(key_rows, "hd", split_axis=2, concat_axis=0, tiled=True),
        lax.all_to_all(value_rows, "hd", split_axis=2, concat_axis=0, tiled=True),
    )
    visible = places[None, :] < counts[:, None]
    context_group, log_total = attend_forward(
        query_group, key_group, value_group, visible, head_count
    )
    context = lax.all_to_all(context_group, "hd", split_axis=0, concat_axis=2, tiled=True)
    first_sum = latent_f + project(context, outward[0])
    self_norm = normed(first_sum, gain_rows[2]).astype(jnp.bfloat16)
    queries2 = project(self_norm, mixing[3]).astype(jnp.bfloat16)
    keys2 = project(self_norm, mixing[4]).astype(jnp.bfloat16)
    values2 = project(self_norm, mixing[5]).astype(jnp.bfloat16)
    all_keys = jnp.ones((latents.shape[0], latents.shape[1]), jnp.bool_)
    context2, log_total2 = attend_forward(queries2, keys2, values2, all_keys, NH)
    second_sum = first_sum + project(context2, outward[1])
    mlp_norm = normed(second_sum, gain_rows[3]).astype(jnp.bfloat16)
    hidden = project(mlp_norm, lift)
    active, gelu_pull = jax.vjp(jax.nn.gelu, hidden)
    active_low = active.astype(jnp.bfloat16)
    third_sum = second_sum + project(active_low, lower)
    latents_out = (third_sum + skip.astype(jnp.float32)).astype(jnp.bfloat16)
    third_grad = cotangent.astype(jnp.float32)
    lower_grad = weight_grad(active_low, cotangent)
    (hidden_grad,) = gelu_pull(project_back(cotangent, lower))
    hidden_low = hidden_grad.astype(jnp.bfloat16)
    lift_grad = weight_grad(mlp_norm, hidden_low)
    lift_view = owner_view(lift_grad, 1, group_count, head_devices)
    lower_view = owner_view(lower_grad, 1, group_count, head_devices)
    lift_section, lower_section = (
        lax.psum_scatter(
            lift_view.astype(jnp.bfloat16), "hd", scatter_dimension=2, tiled=True
        ).astype(jnp.float32),
        lax.psum_scatter(
            lower_view.astype(jnp.bfloat16), "hd", scatter_dimension=2, tiled=True
        ).astype(jnp.float32),
    )
    lift_sum, lower_sum = (
        lax.psum_scatter(
            lift_section.astype(jnp.bfloat16), "grp", scatter_dimension=1, tiled=True
        ).astype(jnp.float32),
        lax.psum_scatter(
            lower_section.astype(jnp.bfloat16), "grp", scatter_dimension=1, tiled=True
        ).astype(jnp.float32),
    )
    lift_part = owner_merge(lift_sum, 1)
    lower_part = owner_merge(lower_sum, 1)
    second_extra, gain3_grad = norm_back(second_sum, gain_rows[3], project_back(hidden_low, lift))
    second_grad = third_grad + second_extra
    second_low = second_grad.astype(jnp.bfloat16)
    outward1_grad = weight_grad(context2, second_low)
    context2_grad = project_back(second_low, outward[1]).astype(jnp.bfloat16)
    query2_grad, key2_grad, value2_grad = attend_backward(
        queries2, keys2, values2, all_keys, log_total2, context2_grad, NH
    )
    self_up = (
        project_back(query2_grad, mixing[3])
        + project_back(key2_grad, mixing[4])
        + project_back(value2_grad, mixing[5])
    )
    first_extra, gain2_grad = norm_back(first_sum, gain_rows[2], self_up)
    first_grad = second_grad + first_extra
    first_low = first_grad.astype(jnp.bfloat16)
    outward0_grad = weight_grad(context, first_low)
    context_grad = project_back(first_low, outward[0]).astype(jnp.bfloat16)
    context_grad_group = lax.all_to_all(context_grad, "hd", split_axis=2, concat_axis=0, tiled=True)
    query_part, key_part, value_part = attend_backward(
        query_group, key_group, value_group, visible, log_total, context_grad_group, head_count
    )
    query_grad, key_grad, value_grad = (
        lax.all_to_all(query_part, "hd", split_axis=0, concat_axis=2, tiled=True),
        lax.all_to_all(key_part, "hd", split_axis=0, concat_axis=2, tiled=True),
        lax.all_to_all(value_part, "hd", split_axis=0, concat_axis=2, tiled=True),
    )
    latent_up = project_back(query_grad, mixing[0])
    pixel_up = project_back(key_grad, mixing[1]) + project_back(value_grad, mixing[2])
    latent_extra, gain1_grad = norm_back(latent_f, gain_rows[1], latent_up)
    pixels_grad, gain0_grad = norm_back(pixel_f, gain_rows[0], pixel_up)
    latents_grad = first_grad + latent_extra
    mixing_grad = jnp.stack(
        [
            weight_grad(latent_norm, query_grad),
            weight_grad(pixel_norm, key_grad),
            weight_grad(pixel_norm, value_grad),
            weight_grad(self_norm, query2_grad),
            weight_grad(self_norm, key2_grad),
            weight_grad(self_norm, value2_grad),
        ]
    )
    outward_grad = jnp.stack([outward0_grad, outward1_grad])
    gains_grad = jnp.stack([gain0_grad, gain1_grad, gain2_grad, gain3_grad])
    mixing_view = owner_view(mixing_grad, 2, group_count, head_devices)
    outward_view = owner_view(outward_grad, 2, group_count, head_devices)
    gains_view = owner_view(gains_grad, 1, group_count, head_devices)
    mixing_section, outward_section, gains_section = (
        lax.psum_scatter(
            mixing_view.astype(jnp.bfloat16), "hd", scatter_dimension=3, tiled=True
        ).astype(jnp.float32),
        lax.psum_scatter(
            outward_view.astype(jnp.bfloat16), "hd", scatter_dimension=3, tiled=True
        ).astype(jnp.float32),
        lax.psum_scatter(
            gains_view.astype(jnp.bfloat16), "hd", scatter_dimension=2, tiled=True
        ).astype(jnp.float32),
    )
    mixing_sum, outward_sum, gains_sum = (
        lax.psum_scatter(
            mixing_section.astype(jnp.bfloat16), "grp", scatter_dimension=2, tiled=True
        ).astype(jnp.float32),
        lax.psum_scatter(
            outward_section.astype(jnp.bfloat16), "grp", scatter_dimension=2, tiled=True
        ).astype(jnp.float32),
        lax.psum_scatter(
            gains_section.astype(jnp.bfloat16), "grp", scatter_dimension=1, tiled=True
        ).astype(jnp.float32),
    )
    mixing_part = owner_merge(mixing_sum, 2)
    outward_part = owner_merge(outward_sum, 2)
    gains_part = owner_merge(gains_sum, 1)
    mix_first, mix_second, mix_new = adamw(
        attn_in, mixing_part, attn_in_first, attn_in_second, 0.05, 0.1
    )
    out_first, out_second, out_new = adamw(
        attn_out, outward_part, attn_out_first, attn_out_second, 0.3, 0.1
    )
    lift_first, lift_second, lift_new = adamw(w_in, lift_part, w_in_first, w_in_second, 0.05, 0.1)
    lower_first, lower_second, lower_new = adamw(
        w_out, lower_part, w_out_first, w_out_second, 0.03, 0.1
    )
    gain_first, gain_second, gain_new = adamw(
        gains, gains_part, gains_first, gains_second, 0.4, 0.0
    )
    return (
        latents_out,
        pixels_grad,
        latents_grad,
        mix_first,
        mix_second,
        mix_new,
        out_first,
        out_second,
        out_new,
        lift_first,
        lift_second,
        lift_new,
        lower_first,
        lower_second,
        lower_new,
        gain_first,
        gain_second[:3],
        gain_second[3],
        gain_new,
    )


def solution(mesh):
    return jax.shard_map(
        local,
        mesh=mesh,
        in_specs=(
            P(("grp", "hd"), None, None),
            P(("grp", "hd"), None, None),
            P(("grp", "hd"), None, None),
            P("grp"),
            P(("grp", "hd"), None, None),
            P(None, None, ("grp", "hd")),
            P(None, None, ("grp", "hd")),
            P(None, ("grp", "hd")),
            P(None, ("grp", "hd")),
            P(None, ("grp", "hd")),
            P(None, None, ("grp", "hd")),
            P(None, None, ("grp", "hd")),
            P(None, None, ("grp", "hd")),
            P(None, None, ("grp", "hd")),
            P(None, ("grp", "hd")),
            P(None, ("grp", "hd")),
            P(None, ("grp", "hd")),
            P(None, ("grp", "hd")),
            P(None, ("grp", "hd")),
            P(None, ("grp", "hd")),
        ),
        out_specs=(
            P(("grp", "hd"), None, None),
            P(("grp", "hd"), None, None),
            P(("grp", "hd"), None, None),
            P(None, None, ("grp", "hd")),
            P(None, None, ("grp", "hd")),
            P(None, None, ("grp", "hd")),
            P(None, None, ("grp", "hd")),
            P(None, None, ("grp", "hd")),
            P(None, None, ("grp", "hd")),
            P(None, ("grp", "hd")),
            P(None, ("grp", "hd")),
            P(None, ("grp", "hd")),
            P(None, ("grp", "hd")),
            P(None, ("grp", "hd")),
            P(None, ("grp", "hd")),
            P(None, ("grp", "hd")),
            P(None, ("grp", "hd")),
            P(("grp", "hd")),
            P(None, ("grp", "hd")),
        ),
        check_vma=False,
    )
```

profile of v0, /device:TPU:0, one launch (start us, length us, event | category | flops | bytes accessed | tf_op | source)
XLA Modules:
  0.0 2056.6 jit_solution(5335321008325618984)
XLA Ops:
  13.1 70.5 %all-gather = bf16[32,32,4]{1,2,0:T(4,128)(2,1)S(1)} all-gather(bf16[1,32,4]{1,2,0:T(4,128)(2,1)S(1)} %convert_bitcast_fusion.2), channel_id=1, replica_groups=mesh['grp'=8,'hd'=4] {'grp','hd'}, dimensions={0}, use_global_device_ids=true | all-gather | bytes 8448 | tf_op jit(solution)/shard_map/all_gather | solution.py:139
  84.2 26.2 %all-gather.6.cloned.1.call-done = bf16[6,1024,1024]{1,2,0:T(8,128)(2,1)} async-done(((bf16[6,1024,32]{1,2,0:T(8,128)(2,1)}), bf16[6,1024,1024]{1,2,0:T(8,128)(2,1)}) %all-gather.6.cloned.1.call-update) | async-done | bytes 12582928 | tf_op jit(solution)/shard_map/all_gather | solution.py:137
  110.4 4.6 fusion.82
  114.9 4.2 copy.294
  119.1 3.6 all-to-all-start.2
  125.4 5.1 fusion.83
  130.5 4.1 copy.290
  134.6 46.4 %all-to-all-done.2 = bf16[3,256,1024]{1,0,2:T(4,128)(2,1)S(1)} async-done(((bf16[3,256,1024]{1,0,2:T(4,128)(2,1)}), bf16[3,256,1024]{1,0,2:T(4,128)(2,1)S(1)}, u32[]{:S(2)}, u32[]{:S(2)}) %all-to-all-start.2) | async-done | bytes 1572896 | tf_op jit(solution)/shard_map/all_to_all | solution.py:157
  181.0 4.5 all-to-all-start.1
  185.5 5.1 fusion.84
  190.6 4.1 copy.287
  194.7 47.7 %all-to-all-done.1 = bf16[3,256,1024]{1,0,2:T(4,128)(2,1)} async-done(((bf16[3,256,1024]{1,0,2:T(4,128)(2,1)}), bf16[3,256,1024]{1,0,2:T(4,128)(2,1)}, u32[]{:S(2)}, u32[]{:S(2)}) %all-to-all-start.1) | async-done | bytes 1572896 | tf_op jit(solution)/shard_map/all_to_all | solution.py:156
  242.4 4.5 all-to-all-start
  249.9 79.0 %all-to-all-done = bf16[3,256,1024]{1,0,2:T(4,128)(2,1)} async-done(((bf16[3,256,1024]{1,0,2:T(4,128)(2,1)}), bf16[3,256,1024]{1,0,2:T(4,128)(2,1)}, u32[]{:S(2)}, u32[]{:S(2)}) %all-to-all-start) | async-done | bytes 1572896 | tf_op jit(solution)/shard_map/all_to_all | solution.py:158
  338.2 4.0 all-to-all-start.3
  342.2 9.9 fusion.135
  352.1 10.6 copy.419
  362.7 10.6 copy.415
  373.3 10.3 all-to-all-done.3
  387.0 4.4 multiply_reduce_fusion.8
  393.2 4.6 fusion.79
  400.5 5.0 fusion.80
  413.8 3.5 fusion.105
  419.5 3.5 multiply_reduce_fusion.7
  423.1 12.8 fusion.13
  436.0 19.8 fusion.6
  455.8 10.5 multiply_reduce_fusion.3
  476.4 5.9 fusion.76
  491.2 3.4 fusion.59
  494.6 3.6 fusion.61
  498.3 5.1 multiply_reduce_fusion.4
  511.4 3.8 all-to-all-start.4
  515.2 48.0 %all-to-all-done.4 = bf16[3,256,1024]{1,0,2:T(4,128)(2,1)S(1)} async-done(((bf16[3,256,1024]{1,0,2:T(4,128)(2,1)}), bf16[3,256,1024]{1,0,2:T(4,128)(2,1)S(1)}, u32[]{:S(2)}, u32[]{:S(2)}) %all-to-all-start.4) | async-done | bytes 1572896 | tf_op jit(solution)/shard_map/all_to_all | solution.py:222
  563.6 5.8 fusion.73
  569.3 4.5 all-to-all-start.6
  578.2 5.5 multiply_reduce_fusion
  590.2 20.1 all-to-all-done.6
  610.4 3.6 all-to-all-start.7
  614.0 4.7 fusion.93
  618.7 12.1 bitcast_convert_fusion.1
  633.1 17.2 all-to-all-done.7
  650.3 4.4 all-to-all-start.5
  655.0 4.5 fusion.94
  659.5 14.3 convert_element_type.267
  673.8 10.0 copy.355
  686.3 12.2 bitcast_convert_fusion
  698.5 3.7 copy.331
  722.2 4.8 bitcast_dynamic-update-slice_fusion.5
  727.1 3.3 bitcast_dynamic-update-slice_fusion.4
  730.4 3.2 bitcast_dynamic-update-slice_fusion.3
  744.5 3.5 fusion.53
  748.1 5.6 fusion.28
  753.9 5.8 fusion.26
  760.5 1093.8 %all-reduce.14.cloned.1.call-done = (bf16[6,1024,8,4,32]{1,4,3,2,0:T(8,128)(2,1)}, bf16[2,1024,8,4,32]{1,4,3,2,0:T(8,128)(2,1)}, bf16[1024,8,4,128]{3,0,2,1:T(8,128)(2,1)}, bf16[4096,8,4,32]{0,3,2,1:T(8,128)(2,1)}) async-done(((bf16[6,1024,8,4,32]{1,4,3,2,0:T(8,128)(2,1)}, bf16[2,1024,8,4,32]{1,4,3,2,0:T(8,128)(2,1)}, bf16[1024,8,4,128]{3,0,2,1:T(8,128)(2,1)}, bf16[4096,8,4,32]{0,3,2,1:T(8,128)(2,1)}), ...) | async-done | bytes 33554448
  1854.3 4.8 constant_dynamic-slice_fusion.4
  1862.1 3.7 constant_dynamic-slice_fusion.2
  1866.5 3.8 constant_dynamic-slice_fusion.1
  1870.3 14.9 add_convert_fusion
  1885.4 5.4 add_add_fusion.1
  1891.5 14.7 all-reduce.6
  1908.0 50.1 %all-reduce.12.cloned.1.call-done = (bf16[6,1024,8,1,32]{1,4,3,2,0:T(8,128)(2,1)}, bf16[2,1024,8,1,32]{1,4,3,2,0:T(8,128)(2,1)}) async-done(((bf16[6,1024,8,1,32]{1,4,3,2,0:T(8,128)(2,1)}, bf16[2,1024,8,1,32]{1,4,3,2,0:T(8,128)(2,1)}), (bf16[6,1024,8,1,32]{1,4,3,2,0:T(8,128)(2,1)}, bf16[2,1024,8,1,32]{1,4,3,2,0:T(8,128)(2,1)})) %all-reduce.12.cloned.1.call-update) | async-done | bytes 4194320
  1960.9 4.3 multiply_subtract_fusion
  1965.2 37.8 %reduce-scatter.22.cloned.1.call-done = bf16[1024,1,1,128]{3,0,2,1:T(8,128)(2,1)} async-done(((bf16[1024,8,1,128]{3,0,2,1:T(8,128)(2,1)}), bf16[1024,1,1,128]{3,0,2,1:T(8,128)(2,1)}) %reduce-scatter.22.cloned.1.call-update) | async-done | bytes 262160 | tf_op jit(solution)/shard_map/reduce_scatter | solution.py:195
  2005.3 42.2 %reduce-scatter.24.cloned.1.call-done = bf16[4096,1,1,32]{0,3,2,1:T(8,128)(2,1)} async-done(((bf16[4096,8,1,32]{0,3,2,1:T(8,128)(2,1)}), bf16[4096,1,1,32]{0,3,2,1:T(8,128)(2,1)}) %reduce-scatter.24.cloned.1.call-update) | async-done | bytes 262160 | tf_op jit(solution)/shard_map/reduce_scatter | solution.py:198
  (300 shorter events, 127.7 us)
Async XLA Ops:
  7.2 5.9 copy-start.81
  7.2 76.5 %copy-start.17 = (bf16[3,256,1024]{2,1,0:T(8,128)(2,1)S(1)}, bf16[3,256,1024]{2,1,0:T(8,128)(2,1)}, u32[]{:S(2)}) copy-start(bf16[3,256,1024]{2,1,0:T(8,128)(2,1)} %param.20) | copy-start | bytes 4718596
  7.2 103.1 %all-gather.6.cloned.1.call-start = ((), (), s32[]{:S(2)}) async-start(), calls=%async_computation.11 | async-start | bytes 12976128 | tf_op jit(solution)/shard_map/all_gather | solution.py:137
  9.3 332.9 %all-gather.8.cloned.1.call-start = ((), (), s32[]{:S(2)}) async-start(), calls=%async_computation.12 | async-start | bytes 4325376 | tf_op jit(solution)/shard_map/all_gather | solution.py:138
  11.2 411.9 %all-gather.10.cloned.1.call-start = ((), (), s32[]{:S(2)}) async-start(), calls=%async_computation.13 | async-start | bytes 8650752 | tf_op jit(solution)/shard_map/all_gather | solution.py:142
  84.1 30.9 %copy-start.61 = (f32[3,256]{1,0:T(4,128)}, f32[3,256]{1,0:T(4,128)S(1)}, u32[]{:S(2)}) copy-start(f32[3,256]{1,0:T(4,128)S(1)} %fusion.36) | copy-start | bytes 9220
  84.1 101.3 %copy-start.69 = (f32[3,256]{1,0:T(4,128)}, f32[3,256]{1,0:T(4,128)S(1)}, u32[]{:S(2)}) copy-start(f32[3,256]{1,0:T(4,128)S(1)} %fusion.120) | copy-start | bytes 9220
  84.1 41.2 %copy-start.75 = (f32[1,1024]{1,0:T(1,128)}, f32[1,1024]{1,0:T(1,128)S(1)}, u32[]{:S(2)}) copy-start(f32[1,1024]{1,0:T(1,128)S(1)} %get-tuple-element.56) | copy-start | bytes 12292
  84.2 101.3 %copy-start.78 = (f32[1,1024]{1,0:T(1,128)}, f32[1,1024]{1,0:T(1,128)S(1)}, u32[]{:S(2)}) copy-start(f32[1,1024]{1,0:T(1,128)S(1)} %get-tuple-element.57) | copy-start | bytes 12292
  84.2 382.2 %copy-start.67 = (f32[1,1024]{1,0:T(1,128)}, f32[1,1024]{1,0:T(1,128)S(1)}, u32[]{:S(2)}) copy-start(f32[1,1024]{1,0:T(1,128)S(1)} %get-tuple-element.54) | copy-start | bytes 12292
  114.9 7.9 copy-start.39
  119.1 61.8 %all-to-all-start.2 = ((bf16[3,256,1024]{1,0,2:T(4,128)(2,1)}), bf16[3,256,1024]{1,0,2:T(4,128)(2,1)S(1)}, u32[]{:S(2)}, u32[]{:S(2)}) async-start(bf16[3,256,1024]{1,0,2:T(4,128)(2,1)} %copy.294), calls=%async_computation.2 | async-start | bytes 4194304 | tf_op jit(solution)/shard_map/all_to_all | solution.py:157
  122.8 313.2 %all-gather.12.cloned.1.call-start = ((), (), s32[]{:S(2)}) async-start(), calls=%async_computation.14 | async-start | bytes 8650752 | tf_op jit(solution)/shard_map/all_gather | solution.py:143
  181.0 61.5 %all-to-all-start.1 = ((bf16[3,256,1024]{1,0,2:T(4,128)(2,1)}), bf16[3,256,1024]{1,0,2:T(4,128)(2,1)}, u32[]{:S(2)}, u32[]{:S(2)}) async-start(bf16[3,256,1024]{1,0,2:T(4,128)(2,1)} %copy.290), calls=%async_computation.1 | async-start | bytes 4194304 | tf_op jit(solution)/shard_map/all_to_all | solution.py:156
  190.6 56.3 %copy-start.88 = (s32[12]{0:T(128)S(1)}, s32[12]{0:T(128)}, u32[]{:S(2)}) copy-start(s32[12]{0:T(128)} %param.23) | copy-start | bytes 148
  242.4 86.4 %all-to-all-start = ((bf16[3,256,1024]{1,0,2:T(4,128)(2,1)}), bf16[3,256,1024]{1,0,2:T(4,128)(2,1)}, u32[]{:S(2)}, u32[]{:S(2)}) async-start(bf16[3,256,1024]{1,0,2:T(4,128)(2,1)} %copy.287), calls=%async_computation | async-start | bytes 4194304 | tf_op jit(solution)/shard_map/all_to_all | solution.py:158
  247.3 83.4 %copy-start.9 = (bf16[4,3,256,256]{2,3,1,0:T(8,128)(2,1)}, bf16[4,3,256,256]{2,3,1,0:T(8,128)(2,1)S(1)}, u32[]{:S(2)}) copy-start(bf16[4,3,256,256]{2,3,1,0:T(8,128)(2,1)S(1)} %copy.296) | copy-start | bytes 4718596
  249.9 83.2 %copy-start.7 = (bf16[4,3,256,256]{2,3,1,0:T(8,128)(2,1)}, bf16[4,3,256,256]{2,3,1,0:T(8,128)(2,1)S(1)}, u32[]{:S(2)}) copy-start(bf16[4,3,256,256]{2,3,1,0:T(8,128)(2,1)S(1)} %copy.292) | copy-start | bytes 4718596
  338.2 45.5 %all-to-all-start.3 = ((bf16[12,256,256]{1,2,0:T(8,128)(2,1)}), bf16[12,256,256]{1,2,0:T(8,128)(2,1)S(1)}, u32[]{:S(2)}, u32[]{:S(2)}) async-start(bf16[12,256,256]{1,2,0:T(8,128)(2,1)} %bitcast.21), calls=%async_computation.3 | async-start | bytes 3145728 | tf_op jit(solution)/shard_map/all_to_all | solution.py:164
  391.5 27.5 %copy-start.4 = (f32[3,256,1024]{2,1,0:T(8,128)}, f32[3,256,1024]{2,1,0:T(8,128)S(1)}, u32[]{:S(2)}) copy-start(f32[3,256,1024]{2,1,0:T(8,128)S(1)} %get-tuple-element.61) | copy-start | bytes 9437188
  411.2 6.1 copy-start
  423.1 43.3 %copy-start.65 = (f32[3,256]{1,0:T(4,128)}, f32[3,256]{1,0:T(4,128)S(1)}, u32[]{:S(2)}) copy-start(f32[3,256]{1,0:T(4,128)S(1)} %fusion.123) | copy-start | bytes 9220
  436.0 19.8 copy-start.31
  436.0 19.8 copy-start.89
  455.8 10.6 copy-start.43
  473.2 9.2 slice-start
  476.4 6.0 slice-start.1
  476.4 6.0 copy-start.6
  476.4 6.0 copy-start.34
  488.6 9.6 copy-start.29
  511.4 51.8 %all-to-all-start.4 = ((bf16[3,256,1024]{1,0,2:T(4,128)(2,1)}), bf16[3,256,1024]{1,0,2:T(4,128)(2,1)S(1)}, u32[]{:S(2)}, u32[]{:S(2)}) async-start(bf16[3,256,1024]{1,0,2:T(4,128)(2,1)} %copy.323), calls=%async_computation.4 | async-start | bytes 4194304 | tf_op jit(solution)/shard_map/all_to_all | solution.py:222
  563.6 5.8 copy-start.10
  569.3 41.0 %all-to-all-start.6 = ((bf16[12,256,256]{1,2,0:T(8,128)(2,1)}), bf16[12,256,256]{1,2,0:T(8,128)(2,1)}, u32[]{:S(2)}, u32[]{:S(2)}) async-start(bf16[12,256,256]{1,2,0:T(8,128)(2,1)} %bitcast.55), calls=%async_computation.6 | async-start | bytes 3145728 | tf_op jit(solution)/shard_map/all_to_all | solution.py:229
  575.4 8.3 slice-start.2
  590.2 23.7 %copy-start.45 = (bf16[3,256,1024]{2,1,0:T(8,128)(2,1)S(1)}, bf16[3,256,1024]{2,1,0:T(8,128)(2,1)}, u32[]{:S(2)}) copy-start(bf16[3,256,1024]{2,1,0:T(8,128)(2,1)} %all_to_all.108) | copy-start | bytes 4718596
  610.4 40.0 %all-to-all-start.7 = ((bf16[12,256,256]{1,2,0:T(8,128)(2,1)}), bf16[12,256,256]{1,2,0:T(8,128)(2,1)S(1)}, u32[]{:S(2)}, u32[]{:S(2)}) async-start(bf16[12,256,256]{1,2,0:T(8,128)(2,1)} %bitcast.59), calls=%async_computation.7 | async-start | bytes 3145728 | tf_op jit(solution)/shard_map/all_to_all | solution.py:227
  618.6 12.1 copy-start.3
  618.6 12.1 copy-start.8
  633.1 21.9 %copy-start.46 = (bf16[1024,3,256]{2,0,1:T(8,128)(2,1)S(1)}, bf16[1024,3,256]{2,0,1:T(8,128)(2,1)}, u32[]{:S(2)}) copy-start(bf16[1024,3,256]{2,0,1:T(8,128)(2,1)} %copy.352) | copy-start | bytes 4718596
  650.3 9.2 copy-start.27
  650.3 61.6 %all-to-all-start.5 = ((bf16[12,256,256]{1,2,0:T(8,128)(2,1)}), bf16[12,256,256]{1,2,0:T(8,128)(2,1)}, u32[]{:S(2)}, u32[]{:S(2)}) async-start(bf16[12,256,256]{1,2,0:T(8,128)(2,1)} %bitcast.51), calls=%async_computation.5 | async-start | bytes 3145728 | tf_op jit(solution)/shard_map/all_to_all | solution.py:228
  654.7 1199.6 %all-reduce.14.cloned.1.call-start = ((), (), s32[]{:S(2)}) async-start(), calls=%async_computation.19 | async-start | bytes 67108864
  673.8 10.0 copy-start.41
  673.8 10.0 copy-start.42
  711.9 8.2 copy-start.22
  743.1 1147.7 %reduce-scatter.26.cloned.1.call-start = ((), (), s32[]{:S(2)}) async-start(), calls=%async_computation.17 | async-start | bytes 40960 | tf_op jit(solution)/shard_map/reduce_scatter | solution.py:258
  748.1 5.7 copy-start.21
  760.4 1197.6 %all-reduce.12.cloned.1.call-start = ((), (), s32[]{:S(2)}) async-start(), calls=%async_computation.18 | async-start | bytes 8388608
  1862.1 140.9 %reduce-scatter.22.cloned.1.call-start = ((), (), s32[]{:S(2)}) async-start(), calls=%async_computation.15 | async-start | bytes 2359296 | tf_op jit(solution)/shard_map/reduce_scatter | solution.py:195
  1865.9 181.7 %reduce-scatter.24.cloned.1.call-start = ((), (), s32[]{:S(2)}) async-start(), calls=%async_computation.16 | async-start | bytes 2359296 | tf_op jit(solution)/shard_map/reduce_scatter | solution.py:198
  1870.3 14.9 copy-start.64
  1870.3 14.9 copy-start.62
  1870.3 15.0 copy-start.13
  1885.3 20.9 %copy-start.82 = (f32[4,32]{1,0:T(4,128)S(1)}, f32[4,32]{1,0:T(4,128)}, u32[]{:S(2)}) copy-start(f32[4,32]{1,0:T(4,128)} %param.29) | copy-start | bytes 1540
  1885.3 20.9 %copy-start.84 = (f32[4,32]{1,0:T(4,128)S(1)}, f32[4,32]{1,0:T(4,128)}, u32[]{:S(2)}) copy-start(f32[4,32]{1,0:T(4,128)} %param.39) | copy-start | bytes 1540
  1885.3 20.9 %copy-start.85 = (f32[4,32]{1,0:T(4,128)S(1)}, f32[4,32]{1,0:T(4,128)}, u32[]{:S(2)}) copy-start(f32[4,32]{1,0:T(4,128)} %param.38) | copy-start | bytes 1540
  1885.3 72.7 %copy-start.56 = (f32[2,1024,32]{1,2,0:T(8,128)S(1)}, f32[2,1024,32]{1,2,0:T(8,128)}, u32[]{:S(2)}) copy-start(f32[2,1024,32]{1,2,0:T(8,128)} %param.26) | copy-start | bytes 786436
  1907.5 57.7 %copy-start.87 = (f32[4,32]{1,0:T(4,128)}, f32[4,32]{1,0:T(4,128)S(1)}, u32[]{:S(2)}) copy-start(f32[4,32]{1,0:T(4,128)S(1)} %get-tuple-element.34) | copy-start | bytes 1540
  1958.1 44.9 %copy-start.38 = (f32[1024,128]{1,0:T(8,128)S(1)}, f32[1024,128]{1,0:T(8,128)}, u32[]{:S(2)}) copy-start(f32[1024,128]{1,0:T(8,128)} %param.27) | copy-start | bytes 1572868
  1958.1 44.9 %copy-start.57 = (f32[1024,128]{1,0:T(8,128)S(1)}, f32[1024,128]{1,0:T(8,128)}, u32[]{:S(2)}) copy-start(f32[1024,128]{1,0:T(8,128)} %param.35) | copy-start | bytes 1572868
  1958.1 44.9 %copy-start.58 = (f32[1024,128]{1,0:T(8,128)S(1)}, f32[1024,128]{1,0:T(8,128)}, u32[]{:S(2)}) copy-start(f32[1024,128]{1,0:T(8,128)} %param.34) | copy-start | bytes 1572868
  1960.9 86.6 %copy-start.40 = (f32[4096,32]{0,1:T(8,128)S(1)}, f32[4096,32]{0,1:T(8,128)}, u32[]{:S(2)}) copy-start(f32[4096,32]{0,1:T(8,128)} %param.28) | copy-start | bytes 1572868
  1960.9 86.6 %copy-start.59 = (f32[4096,32]{0,1:T(8,128)S(1)}, f32[4096,32]{0,1:T(8,128)}, u32[]{:S(2)}) copy-start(f32[4096,32]{0,1:T(8,128)} %param.37) | copy-start | bytes 1572868
  1960.9 86.6 %copy-start.60 = (f32[4096,32]{0,1:T(8,128)S(1)}, f32[4096,32]{0,1:T(8,128)}, u32[]{:S(2)}) copy-start(f32[4096,32]{0,1:T(8,128)} %param.36) | copy-start | bytes 1572868
  (50 other events, 179.0 us)
Sparse Core Ops, SparseCore 0:
  11.6 98.6 all-gather.5
  113.9 93.2 all-gather.7
  210.6 125.1 all-gather.9
  339.2 94.8 all-gather.11
  743.2 1111.0 all-reduce.13
  1857.1 17.7 reduce-scatter.25
  1878.2 79.8 all-reduce.11
  1961.7 41.2 reduce-scatter.21
  2006.3 41.1 reduce-scatter.23
where the time goes:
time: 2070 us; the launch traced here: 2060 us
  waiting for transfers between devices  1520 us (73%)
  matrix products  217 us (10%)
  local copies, waits for them, and re-layouts  148 us (7%)
  blocking collectives  85.2 us (4%)
  other arithmetic  37.8 us (2%)
  starting transfers between devices  33.5 us (2%)
    unnamed x11, waiting for transfers between devices  1140 us
    all_to_all x1, waiting for transfers between devices, local(): lax.all_to_all(value_rows, 'hd', split_axis=2, concat_axis=0, tiled=True)  79 us
    all_gather x1, blocking collectives, local(): lax.all_gather(gains.astype(jnp.bfloat16), ('grp', 'hd'), axis=1, tiled=T...  70.5 us
    dot_general x10, matrix products, project(): jnp.einsum('bnd,de->bne', row_block, matrix, preferred_element_type=jnp.f...  63.6 us
    dot_general x10, matrix products, project_back(): jnp.einsum('bne,de->bnd', grad_rows, matrix, preferred_element_type=jnp.f...  62.4 us
    dot_general x10, matrix products, weight_grad(): jnp.einsum('bnd,bne->de', row_block, grad_rows, preferred_element_type=jn...  54.2 us
    unnamed x203, local copies, waits for them, and re-layouts  52 us
    all_to_all x1, waiting for transfers between devices, local(): lax.all_to_all(context_grad, 'hd', split_axis=2, concat_axis=0, tiled=True)  48 us
  transfers between devices with their start and end apart: 17, of which 12 were waited for; matrix products, arithmetic and copies ran while one was open for 13% of the time, Pallas kernels for 0%

commit v1 on v0

v1 whole, which is shorter than its diff:
```python
import functools

import jax
import jax.numpy as jnp
from jax import lax
from jax.experimental import pallas as pl
from jax.experimental.pallas import tpu as pltpu
from jax.sharding import PartitionSpec as P

NH = 8
STEP = 5
AXES = ("grp", "hd")

MIB = 1 << 20
F32, LOW = jnp.float32, jnp.bfloat16
VMEM = pl.BlockSpec(memory_space=pltpu.VMEM)
SMEM = pl.BlockSpec(memory_space=pltpu.SMEM)


ANY = pl.BlockSpec(memory_space=pl.ANY)


def adamw(weight, grad, first_old, second_old, learn_rate, decay):
    first_new = 0.5 * first_old + 0.5 * grad
    second_new = 0.5 * second_old + 0.5 * grad * grad
    correction = 1.0 - 0.5**STEP
    normed_step = first_new / correction / (jnp.sqrt(second_new / correction) + 1e-08)
    return (first_new, second_new, weight - learn_rate * (normed_step + decay * weight))


def log2(n):
    return n.bit_length() - 1


def bit_orders(groups, depth):
    near = log2(depth)
    z_bits = list(range(near))[::-1]
    outer = list(range(near + 1, near + log2(groups)))
    half = (len(outer) + 1) // 2
    x_bits, y_bits = outer[:half][::-1], outer[half:][::-1]
    return {
        "xzy": x_bits + z_bits + y_bits,
        "yzx": y_bits + z_bits + x_bits,
        "zxy": z_bits + x_bits + y_bits,
        "zyx": z_bits + y_bits + x_bits,
    }


def swap(block, bit, total):
    return lax.ppermute(block, AXES, [(j, j ^ (1 << bit)) for j in range(total)])


def spread_of(order, core, total):
    bits = list(order) + [core]
    return [sum(((p >> t) & 1) << b for t, b in enumerate(bits)) for p in range(total)]


def gather_chain(shard, order, core, total):
    held = shard[None]
    for bit in order[:-1]:
        held = jnp.concatenate([held, swap(held, bit, total)], axis=0)
    came = swap(held, order[-1], total)
    return [held, came, swap(held, core, total), swap(came, core, total)]


def added(a, b):
    return (a.astype(jnp.float32) + b.astype(jnp.float32)).astype(jnp.bfloat16)


def scatter_chain(pieces, order, core, total):
    away = added(pieces[1], swap(pieces[3], core, total))
    held = added(pieces[0], swap(pieces[2], core, total))
    held = added(held, swap(away, order[-1], total))
    for bit in reversed(order[:-1]):
        half = held.shape[0] // 2
        held = added(held[:half], swap(held[half:], bit, total))
    return held[0]


def device_index():
    return lax.axis_index("grp") * lax.axis_size("hd") + lax.axis_index("hd")


def place_kernel(spreads, blocks_of, *refs):
    *refs, sems = refs
    count = 4 * len(spreads)
    pieces, wholes = refs[:count], refs[count:]
    me = device_index()
    for c, spread in enumerate(spreads):
        each = len(spread) // 4
        for p, mask in enumerate(spread):
            block = pieces[4 * c + p // each].at[p % each]
            for m, (part, place) in enumerate(blocks_of[c](block, wholes, me ^ mask)):
                pltpu.make_async_copy(part, place, sems.at[m]).start()
    for m, whole in enumerate(wholes):
        pltpu.make_async_copy(whole, whole, sems.at[m]).wait()


def cut_kernel(spreads, blocks_of, count, *refs):
    *refs, sems = refs
    wholes, pieces = refs[:count], refs[count:]
    me = device_index()
    for c, spread in enumerate(spreads):
        each = len(spread) // 4
        for p, mask in enumerate(spread):
            at = 4 * c + p // each
            for part, place in blocks_of[c](pieces[at].at[p % each], wholes, me ^ mask):
                pltpu.make_async_copy(place, part, sems.at[at]).start()
    for m, piece in enumerate(pieces):
        pltpu.make_async_copy(piece, piece, sems.at[m]).wait()


def row_blocks(rows, block, wholes, owner):
    start = pl.multiple_of(owner * rows, rows)
    return [
        (block.at[pl.ds(m * rows, rows), :], whole.at[pl.ds(start, rows), :])
        for m, whole in enumerate(wholes)
    ]


def row_half(rows, at, width, block, wholes, owner):
    start = pl.multiple_of(owner * rows, rows)
    return [(block, wholes[0].at[pl.ds(start, rows), pl.ds(at, width)])]


def column_half(columns, at, width, block, wholes, owner):
    start = pl.multiple_of(owner * columns, columns)
    return [(block, wholes[0].at[pl.ds(at, width), pl.ds(start, columns)])]


def place(pieces, spreads, blocks_of, shapes):
    return pl.pallas_call(
        functools.partial(place_kernel, spreads, blocks_of),
        out_shape=[jax.ShapeDtypeStruct(s, LOW) for s in shapes],
        in_specs=[ANY] * len(pieces),
        out_specs=[VMEM] * len(shapes),
        scratch_shapes=[pltpu.SemaphoreType.DMA((len(shapes),))],
        compiler_params=pltpu.CompilerParams(vmem_limit_bytes=20 * MIB),
    )(*pieces)


def cut(wholes, spreads, blocks_of, shapes):
    return pl.pallas_call(
        functools.partial(cut_kernel, spreads, blocks_of, len(wholes)),
        out_shape=[
            jax.ShapeDtypeStruct((len(spread) // 4,) + shape, LOW)
            for spread, shape in zip(spreads, shapes)
            for _ in range(4)
        ],
        in_specs=[VMEM] * len(wholes),
        out_specs=[ANY] * (4 * len(shapes)),
        scratch_shapes=[pltpu.SemaphoreType.DMA((4 * len(shapes),))],
        compiler_params=pltpu.CompilerParams(vmem_limit_bytes=20 * MIB),
    )(*wholes)


ATTENTION_CHAINS = (("xzy", (1, 2)), ("yzx", (0, 6)), ("zxy", (3, 4)), ("zyx", (5, 7)))
LOWER_CHAINS = ("xzy", "yzx")
LIFT_CHAINS = ("zxy", "zyx")


def gather_weights(attention, lower, lift, groups, depth):
    total, core = groups * depth, log2(depth)
    orders = bit_orders(groups, depth)
    rows = attention[0].shape[0]
    if rows % 16 or lift.shape[1] % 128:
        whole = [lax.all_gather(a, AXES, axis=0, tiled=True) for a in attention]
        return (
            whole,
            lax.all_gather(lower, AXES, axis=0, tiled=True),
            lax.all_gather(lift, AXES, axis=1, tiled=True),
        )
    matrices = [None] * 8
    for name, members in ATTENTION_CHAINS:
        shard = jnp.concatenate([attention[m] for m in members], axis=0)
        pieces = gather_chain(shard, orders[name], core, total)
        placed = place(
            pieces,
            [spread_of(orders[name], core, total)],
            [functools.partial(row_blocks, rows)],
            [(rows * total, attention[0].shape[1])] * len(members),
        )
        for m, whole in zip(members, placed):
            matrices[m] = whole
    (lower_whole,) = place(
        [p for h, name in enumerate(LOWER_CHAINS) for p in gather_chain(half_of(lower, 1, h), orders[name], core, total)],
        [spread_of(orders[name], core, total) for name in LOWER_CHAINS],
        [functools.partial(row_half, rows, h * lower.shape[1] // 2, lower.shape[1] // 2) for h in range(2)],
        [(rows * total, lower.shape[1])],
    )
    (lift_whole,) = place(
        [p for h, name in enumerate(LIFT_CHAINS) for p in gather_chain(half_of(lift, 0, h), orders[name], core, total)],
        [spread_of(orders[name], core, total) for name in LIFT_CHAINS],
        [functools.partial(column_half, lift.shape[1], h * lift.shape[0] // 2, lift.shape[0] // 2) for h in range(2)],
        [(lift.shape[0], lift.shape[1] * total)],
    )
    return matrices, lower_whole, lift_whole


def scatter_attention(grads, groups, depth):
    total, core = groups * depth, log2(depth)
    orders = bit_orders(groups, depth)
    rows = grads[0].shape[0] // total
    if rows % 16:
        return {
            m: lax.psum_scatter(g, AXES, scatter_dimension=0, tiled=True) for m, g in grads.items()
        }
    sums = {}
    for name, members in ATTENTION_CHAINS:
        pieces = cut(
            [grads[m] for m in members],
            [spread_of(orders[name], core, total)],
            [functools.partial(row_blocks, rows)],
            [(rows * len(members), grads[0].shape[1])],
        )
        own = scatter_chain(pieces, orders[name], core, total)
        for at, m in enumerate(members):
            sums[m] = own[at * rows : (at + 1) * rows]
    return sums


def scatter_mlp(lower_grad, lift_grad, groups, depth):
    total, core = groups * depth, log2(depth)
    orders = bit_orders(groups, depth)
    rows, columns = lower_grad.shape[0] // total, lift_grad.shape[1] // total
    if rows % 16 or columns % 128:
        return (
            lax.psum_scatter(lower_grad, AXES, scatter_dimension=0, tiled=True),
            lax.psum_scatter(lift_grad, AXES, scatter_dimension=1, tiled=True),
        )
    half = lift_grad.shape[0] // 2
    pieces = cut(
        [lift_grad],
        [spread_of(orders[name], core, total) for name in LIFT_CHAINS],
        [functools.partial(column_half, columns, h * half, half) for h in range(2)],
        [(half, columns)] * 2,
    )
    lift_sums = [
        scatter_chain(pieces[4 * h : 4 * h + 4], orders[name], core, total) for h, name in enumerate(LIFT_CHAINS)
    ]
    half = lower_grad.shape[1] // 2
    pieces = cut(
        [lower_grad],
        [spread_of(orders[name], core, total) for name in LOWER_CHAINS],
        [functools.partial(row_half, rows, h * half, half) for h in range(2)],
        [(rows, half)] * 2,
    )
    lower_sums = [
        scatter_chain(pieces[4 * h : 4 * h + 4], orders[name], core, total) for h, name in enumerate(LOWER_CHAINS)
    ]
    return jnp.concatenate(lower_sums, axis=1), jnp.concatenate(lift_sums, axis=0)


def half_of(array, along, which):
    half = array.shape[along] // 2
    return lax.slice_in_dim(array, which * half, (which + 1) * half, axis=along)


def block_matrix(spread, total):
    mine = jnp.array(spread, jnp.int32)[None, :] ^ device_index()
    return (lax.broadcasted_iota(jnp.int32, (total, total), 0) == mine).astype(F32)


def gather_gains(gains, groups, depth):
    total, core = groups * depth, log2(depth)
    if total > 32:
        return lax.all_gather(gains, AXES, axis=1, tiled=True).astype(F32)
    order = bit_orders(groups, depth)["xzy"]
    rows, columns = gains.shape
    held = gains.reshape(1, -1)
    for bit in (*order, core):
        held = jnp.concatenate([held, swap(held, bit, total)], axis=0)
    whole = jnp.dot(block_matrix(spread_of(order, core, total), total).astype(LOW), held, preferred_element_type=F32)
    return jnp.swapaxes(whole.reshape(total, rows, columns), 0, 1).reshape(rows, -1)


def scatter_gains(grads, groups, depth):
    total, core = groups * depth, log2(depth)
    if total > 32:
        return lax.psum_scatter(grads.astype(LOW), AXES, scatter_dimension=1, tiled=True).astype(F32)
    order = bit_orders(groups, depth)["xzy"]
    rows = grads.shape[0]
    blocks = jnp.swapaxes(grads.reshape(rows, total, -1), 0, 1).reshape(total, -1)
    held = jnp.dot(
        block_matrix(spread_of(order, core, total), total).T, blocks, precision=lax.Precision.HIGHEST
    )
    for bit in (core, *reversed(order)):
        half = held.shape[0] // 2
        held = held[:half] + swap(held[half:], bit, total)
    return held.reshape(rows, -1)


def dot_nn(a, b):
    return lax.dot_general(a, b, (((1,), (0,)), ((), ())), preferred_element_type=F32)


def dot_nt(a, b):
    return lax.dot_general(a, b, (((1,), (1,)), ((), ())), preferred_element_type=F32)


def dot_tn(a, b):
    return lax.dot_general(a, b, (((0,), (0,)), ((), ())), preferred_element_type=F32)


def unit_rows(rows):
    inverse = lax.rsqrt(jnp.mean(rows * rows, axis=-1, keepdims=True) + 1e-06)
    return rows * inverse, inverse


def norm_grad(rows, gain, upstream):
    unit, inverse = unit_rows(rows)
    scaled = upstream * gain
    inner = jnp.mean(scaled * unit, axis=-1, keepdims=True)
    return (scaled - unit * inner) * inverse, jnp.sum(upstream * unit, axis=0, keepdims=True)


def heads_probs(query, key, count, scale):
    scores = dot_nt(query, key) * scale
    if count is not None:
        place = lax.broadcasted_iota(jnp.int32, scores.shape, 1)
        scores = jnp.where(place < count, scores, -1e30)
    exponent = jnp.exp(scores - jnp.max(scores, axis=-1, keepdims=True))
    return exponent / jnp.sum(exponent, axis=-1, keepdims=True)


def attend_kernel(cross, images, size, *refs):
    if cross:
        counts, gains, source, target, *refs = refs
    else:
        gains, target, *refs = refs
        counts, source = None, target
    (wq, wk, wv, wo, q_out, k_out, v_out, context_out, sum_out, wq_v, wk_v, wv_v, wo_v, sems) = refs
    copies = []
    for at, (src, dst) in enumerate(((wk, wk_v), (wv, wv_v), (wq, wq_v), (wo, wo_v))):
        copies.append(pltpu.make_async_copy(src, dst, sems.at[at]))
        copies[-1].start()
    key_gain, query_gain = (0, 1) if cross else (2, 2)
    rows = source[...].astype(F32)
    normal = (unit_rows(rows)[0] * gains[key_gain : key_gain + 1, :]).astype(LOW)
    copies[0].wait()
    k_out[...] = dot_nt(normal, wk_v[...]).astype(LOW)
    copies[1].wait()
    v_out[...] = dot_nt(normal, wv_v[...]).astype(LOW)
    if cross:
        rows = target[...].astype(F32)
        normal = (unit_rows(rows)[0] * gains[query_gain : query_gain + 1, :]).astype(LOW)
    copies[2].wait()
    q_out[...] = dot_nt(normal, wq_v[...]).astype(LOW)
    width = q_out.shape[1] // NH
    scale = width ** (-0.5)

    def one_image(image, carry):
        span = pl.ds(pl.multiple_of(image * size, size), size)
        count = counts[image] if cross else None
        for h in range(NH):
            part = slice(h * width, (h + 1) * width)
            weights = heads_probs(q_out[span, part], k_out[span, part], count, scale).astype(LOW)
            context_out[span, part] = dot_nn(weights, v_out[span, part]).astype(LOW)
        return carry

    lax.fori_loop(0, images, one_image, 0)
    copies[3].wait()
    sum_out[...] = target[...].astype(F32) + dot_nt(context_out[...], wo_v[...])


def attend_block(gains, source, target, counts, weights, images):
    cross = source is not None
    rows, width = target.shape
    low = jax.ShapeDtypeStruct((rows, width), LOW)
    head = (counts, gains, source, target) if cross else (gains, target)
    return pl.pallas_call(
        functools.partial(attend_kernel, cross, images, rows // images),
        out_shape=[low] * 4 + [jax.ShapeDtypeStruct((rows, width), F32)],
        in_specs=([SMEM] if cross else []) + [VMEM] * (3 if cross else 2) + [ANY] * 4,
        out_specs=[VMEM] * 5,
        scratch_shapes=[pltpu.VMEM((width, width), LOW)] * 4 + [pltpu.SemaphoreType.DMA((4,))],
        compiler_params=pltpu.CompilerParams(vmem_limit_bytes=48 * MIB),
        cost_estimate=pl.CostEstimate(
            flops=8 * rows * width * width + 4 * rows * width * (rows // images),
            bytes_accessed=12 * rows * width + 8 * width * width,
            transcendentals=rows * NH * (rows // images),
        ),
    )(*head, *weights)


def attend_grad_kernel(cross, images, size, *refs):
    if cross:
        counts, gains, source, target, *refs = refs
    else:
        gains, target, *refs = refs
        counts, source = None, target
    (upstream, q_in, k_in, v_in, context_in, wq, wk, wv, wo, *refs) = refs
    outs = 2 if cross else 1
    grads_out, gain_outs, (gq_out, gk_out, gv_out, go_out) = refs[:outs], refs[outs : 2 * outs], refs[2 * outs : 2 * outs + 4]
    (dq, dk, dv, dc, wq_v, wk_v, wv_v, wo_v, sems) = refs[2 * outs + 4 :]
    copies = []
    for at, (src, dst) in enumerate(((wo, wo_v), (wq, wq_v), (wk, wk_v), (wv, wv_v))):
        copies.append(pltpu.make_async_copy(src, dst, sems.at[at]))
        copies[-1].start()
    up_low = upstream[...].astype(LOW)
    copies[0].wait()
    dc[...] = dot_nn(up_low, wo_v[...]).astype(LOW)
    go_out[...] = dot_tn(up_low, context_in[...]).astype(LOW)
    width = q_in.shape[1] // NH
    scale = width ** (-0.5)

    def one_image(image, carry):
        span = pl.ds(pl.multiple_of(image * size, size), size)
        count = counts[image] if cross else None
        for h in range(NH):
            part = slice(h * width, (h + 1) * width)
            query, key, value, grad = q_in[span, part], k_in[span, part], v_in[span, part], dc[span, part]
            probs = heads_probs(query, key, count, scale)
            prob_grad = dot_nt(grad, value)
            dv[span, part] = dot_tn(probs.astype(LOW), grad).astype(LOW)
            score_grad = probs * (prob_grad - jnp.sum(probs * prob_grad, axis=-1, keepdims=True))
            score_grad = score_grad.astype(LOW)
            dq[span, part] = (dot_nn(score_grad, key) * scale).astype(LOW)
            dk[span, part] = (dot_tn(score_grad, query) * scale).astype(LOW)
        return carry

    lax.fori_loop(0, images, one_image, 0)
    key_gain, query_gain = (0, 1) if cross else (2, 2)
    rows = target[...].astype(F32)
    gain = gains[query_gain : query_gain + 1, :]
    normal = (unit_rows(rows)[0] * gain).astype(LOW)
    gq_out[...] = dot_tn(dq[...], normal).astype(LOW)
    copies[1].wait()
    back = dot_nn(dq[...], wq_v[...])
    copies[2].wait()
    copies[3].wait()
    if cross:
        extra, gain_grad = norm_grad(rows, gain, back)
        grads_out[0][...] = upstream[...] + extra
        gain_outs[0][...] = gain_grad
        rows = source[...].astype(F32)
        gain = gains[key_gain : key_gain + 1, :]
        normal = (unit_rows(rows)[0] * gain).astype(LOW)
        back = dot_nn(dk[...], wk_v[...])
    else:
        back += dot_nn(dk[...], wk_v[...])
    back += dot_nn(dv[...], wv_v[...])
    gk_out[...] = dot_tn(dk[...], normal).astype(LOW)
    gv_out[...] = dot_tn(dv[...], normal).astype(LOW)
    extra, gain_grad = norm_grad(rows, gain, back)
    if cross:
        grads_out[1][...] = extra
    else:
        grads_out[0][...] = upstream[...] + extra
    gain_outs[-1][...] = gain_grad


def attend_grad(gains, source, target, counts, upstream, saved, weights, images):
    cross = source is not None
    rows, width = target.shape
    outs = 2 if cross else 1
    head = (counts, gains, source, target) if cross else (gains, target)
    result = pl.pallas_call(
        functools.partial(attend_grad_kernel, cross, images, rows // images),
        out_shape=[jax.ShapeDtypeStruct((rows, width), F32)] * outs
        + [jax.ShapeDtypeStruct((1, width), F32)] * outs
        + [jax.ShapeDtypeStruct((width, width), LOW)] * 4,
        in_specs=([SMEM] if cross else []) + [VMEM] * (3 if cross else 2) + [VMEM] * 5 + [ANY] * 4,
        out_specs=[VMEM] * (2 * outs + 4),
        scratch_shapes=[pltpu.VMEM((rows, width), LOW)] * 4
        + [pltpu.VMEM((width, width), LOW)] * 4
        + [pltpu.SemaphoreType.DMA((4,))],
        compiler_params=pltpu.CompilerParams(vmem_limit_bytes=60 * MIB),
        cost_estimate=pl.CostEstimate(
            flops=16 * rows * width * width + 10 * rows * width * (rows // images),
            bytes_accessed=20 * rows * width + 16 * width * width,
            transcendentals=rows * NH * (rows // images),
        ),
    )(*head, upstream, *saved, *weights)
    return result[:outs], result[outs : 2 * outs], result[2 * outs :]


def mlp_kernel(gain_row, second, cotangent, skip, lift, lower, out, second_grad, gain_grad, lift_grad, lower_grad, normal, normal_t, cot_t, total, back):
    step = pl.program_id(0)

    @pl.when(step == 0)
    def first():
        low = (unit_rows(second[...])[0] * gain_row[...]).astype(LOW)
        normal[...] = low
        normal_t[...] = low.T
        cot_t[...] = cotangent[...].T
        total[...] = second[...]
        back[...] = jnp.zeros_like(back)

    hidden = dot_nn(normal[...], lift[...])
    square = hidden * hidden
    root = 0.7978845608028654
    tanh = jnp.tanh(root * hidden * (1.0 + 0.044715 * square))
    half = 0.5 * (1.0 + tanh)
    active = (hidden * half).astype(LOW)
    slope = half + 0.5 * hidden * (1.0 - tanh * tanh) * (root * (1.0 + 3 * 0.044715 * square))
    lower_grad[...] = dot_nn(cot_t[...], active).astype(LOW)
    total[...] += dot_nt(active, lower[...])
    hidden_grad = (dot_nn(cotangent[...], lower[...]) * slope).astype(LOW)
    lift_grad[...] = dot_nn(normal_t[...], hidden_grad).astype(LOW)
    back[...] += dot_nt(hidden_grad, lift[...])

    @pl.when(step == pl.num_programs(0) - 1)
    def last():
        out[...] = (total[...] + skip[...].astype(F32)).astype(LOW)
        extra, gains = norm_grad(second[...], gain_row[...], back[...])
        second_grad[...] = cotangent[...].astype(F32) + extra
        gain_grad[...] = gains


def mlp_block(gain_row, second, cotangent, skip, lift, lower):
    rows, width = second.shape
    hidden, block = lift.shape[1], 512
    whole = lambda shape: pl.BlockSpec(shape, lambda f: (0, 0), pipeline_mode=pl.Buffered(1))
    once = lambda shape: pl.BlockSpec(shape, lambda f: (0, 0))
    chunk = pl.BlockSpec((width, block), lambda f: (0, f))
    return pl.pallas_call(
        mlp_kernel,
        grid=(hidden // block,),
        out_shape=[
            jax.ShapeDtypeStruct((rows, width), LOW),
            jax.ShapeDtypeStruct((rows, width), F32),
            jax.ShapeDtypeStruct((1, width), F32),
            jax.ShapeDtypeStruct((width, hidden), LOW),
            jax.ShapeDtypeStruct((width, hidden), LOW),
        ],
        in_specs=[whole((1, width))] + [whole((rows, width))] * 3 + [chunk] * 2,
        out_specs=[once((rows, width))] * 2 + [once((1, width))] + [chunk] * 2,
        scratch_shapes=[
            pltpu.VMEM((rows, width), LOW),
            pltpu.VMEM((width, rows), LOW),
            pltpu.VMEM((width, rows), LOW),
            pltpu.VMEM((rows, width), F32),
            pltpu.VMEM((rows, width), F32),
        ],
        compiler_params=pltpu.CompilerParams(vmem_limit_bytes=60 * MIB),
        cost_estimate=pl.CostEstimate(
            flops=12 * rows * width * hidden,
            bytes_accessed=8 * width * hidden + 16 * rows * width,
            transcendentals=rows * hidden,
        ),
    )(gain_row, second, cotangent, skip, lift, lower)


def local(
    pixels,
    latents,
    skip,
    counts,
    cotangent,
    attn_in,
    attn_out,
    w_in,
    w_out,
    gains,
    attn_in_first,
    attn_in_second,
    attn_out_first,
    attn_out_second,
    w_in_first,
    w_in_second,
    w_out_first,
    w_out_second,
    gains_first,
    gains_second,
):
    groups, depth = lax.axis_size("grp"), lax.axis_size("hd")
    gain_rows = gather_gains(gains.astype(LOW), groups, depth)
    attn_in_t = jnp.swapaxes(attn_in, 1, 2).astype(LOW)
    attn_out_t = jnp.swapaxes(attn_out, 1, 2).astype(LOW)
    attention = [attn_in_t[m] for m in range(6)] + [attn_out_t[m] for m in range(2)]
    mats, lower, lift = gather_weights(attention, w_out.T.astype(LOW), w_in.astype(LOW), groups, depth)

    images, size, width = latents.shape
    flat = lambda rows: rows.reshape(-1, width)
    whole = lambda rows: rows.reshape(images, -1, width)
    pixel_rows, latent_rows = flat(pixels), flat(latents)
    own_counts = lax.dynamic_slice_in_dim(counts, lax.axis_index("hd") * images, images)
    cross, own = (mats[0], mats[1], mats[2], mats[6]), (mats[3], mats[4], mats[5], mats[7])
    *saved, first_sum = attend_block(gain_rows, pixel_rows, latent_rows, own_counts, cross, images)
    *saved2, second_sum = attend_block(gain_rows, None, first_sum, None, own, images)
    latents_out, second_grad, gain3_grad, lift_grad, lower_grad = mlp_block(
        gain_rows[3:], second_sum, flat(cotangent), flat(skip), lift, lower
    )
    lower_sum, lift_sum = scatter_mlp(lower_grad, lift_grad, groups, depth)
    (first_grad,), (gain2_grad,), grads2 = attend_grad(
        gain_rows, None, first_sum, None, second_grad, saved2, own, images
    )
    (latents_grad, pixels_grad), (gain1_grad, gain0_grad), grads = attend_grad(
        gain_rows, pixel_rows, latent_rows, own_counts, first_grad, saved, cross, images
    )
    sums = scatter_attention(
        dict(zip((3, 4, 5, 7, 0, 1, 2, 6), (*grads2, *grads))), groups, depth
    )
    gains_grad = jnp.concatenate([gain0_grad, gain1_grad, gain2_grad, gain3_grad], axis=0)
    gains_sum = scatter_gains(gains_grad, groups, depth)
    mixing_sum = jnp.swapaxes(jnp.stack([sums[m] for m in range(6)]), 1, 2).astype(F32)
    outward_sum = jnp.swapaxes(jnp.stack([sums[6], sums[7]]), 1, 2).astype(F32)
    mix = adamw(attn_in, mixing_sum, attn_in_first, attn_in_second, 0.05, 0.1)
    out = adamw(attn_out, outward_sum, attn_out_first, attn_out_second, 0.3, 0.1)
    lift_new = adamw(w_in, lift_sum.astype(F32), w_in_first, w_in_second, 0.05, 0.1)
    lower_new = adamw(w_out, lower_sum.T.astype(F32), w_out_first, w_out_second, 0.03, 0.1)
    gain_first, gain_second, gain_new = adamw(
        gains, gains_sum, gains_first, gains_second, 0.4, 0.0
    )
    return (
        whole(latents_out),
        whole(pixels_grad),
        whole(latents_grad),
        *mix,
        *out,
        *lift_new,
        *lower_new,
        gain_first,
        gain_second[:3],
        gain_second[3],
        gain_new,
    )


def solution(mesh):
    return jax.shard_map(
        local,
        mesh=mesh,
        in_specs=(
            P(("grp", "hd"), None, None),
            P(("grp", "hd"), None, None),
            P(("grp", "hd"), None, None),
            P("grp"),
            P(("grp", "hd"), None, None),
            P(None, None, ("grp", "hd")),
            P(None, None, ("grp", "hd")),
            P(None, ("grp", "hd")),
            P(None, ("grp", "hd")),
            P(None, ("grp", "hd")),
            P(None, None, ("grp", "hd")),
            P(None, None, ("grp", "hd")),
            P(None, None, ("grp", "hd")),
            P(None, None, ("grp", "hd")),
            P(None, ("grp", "hd")),
            P(None, ("grp", "hd")),
            P(None, ("grp", "hd")),
            P(None, ("grp", "hd")),
            P(None, ("grp", "hd")),
            P(None, ("grp", "hd")),
        ),
        out_specs=(
            P(("grp", "hd"), None, None),
            P(("grp", "hd"), None, None),
            P(("grp", "hd"), None, None),
            P(None, None, ("grp", "hd")),
            P(None, None, ("grp", "hd")),
            P(None, None, ("grp", "hd")),
            P(None, None, ("grp", "hd")),
            P(None, None, ("grp", "hd")),
            P(None, None, ("grp", "hd")),
            P(None, ("grp", "hd")),
            P(None, ("grp", "hd")),
            P(None, ("grp", "hd")),
            P(None, ("grp", "hd")),
            P(None, ("grp", "hd")),
            P(None, ("grp", "hd")),
            P(None, ("grp", "hd")),
            P(None, ("grp", "hd")),
            P(("grp", "hd")),
            P(None, ("grp", "hd")),
        ),
        check_vma=False,
    )
```

time: 2070 us -> 727 us (0.35)
  waiting for transfers between devices: 1520 us -> 326 us
  matrix products: 217 us -> 0.33 us
  Pallas kernels: 0 us -> 212 us
  blocking collectives: 85.2 us -> 0 us
  local copies, waits for them, and re-layouts: 148 us -> 65.2 us
  starting transfers between devices: 33.5 us -> 85.4 us
    unnamed x11 -> x0, waiting for transfers between devices: 1140 us -> none
    ppermute x0 -> x106, waiting for transfers between devices: none -> 326 us  [swap(): return lax.ppermute(block, AXES, [(j, j ^ 1 << bit) for j in range(total)])]
    all_to_all x8 -> x0, waiting for transfers between devices: 269 us -> none  [the longest x1 79 us: local(): lax.all_to_all(value_rows, 'hd', split_axis=2, concat_axis=0, tiled=True)]
    dot_general x42 -> x2, matrix products: 217 us -> 0.33 us  [the longest x1 0.2 us: scatter_gains(): jnp.dot(block_matrix(spread_of(order, core, total), total).T, blocks, pre...]
    pallas_call x0 -> x17, Pallas kernels: none -> 212 us  [the longest x2 71.4 us: attend_grad(): pl.pallas_call(functools.partial(attend_grad_kernel, cross, images, rows...]
    ppermute x0 -> x106, starting transfers between devices: none -> 85.4 us  [swap(): return lax.ppermute(block, AXES, [(j, j ^ 1 << bit) for j in range(total)])]
    reduce_scatter x3 -> x0, waiting for transfers between devices: 80 us -> none  [the longest x1 42.2 us: local(): lax.psum_scatter(lower_section.astype(jnp.bfloat16), 'grp', scatter_dimen...]
    all_gather x1 -> x0, blocking collectives: 70.5 us -> none  [local(): lax.all_gather(gains.astype(jnp.bfloat16), ('grp', 'hd'), axis=1, tiled=T...]
  transfers between devices with their start and end apart: 17 -> 106, of which waited for: 12 -> 37; matrix products, arithmetic and copies ran while one was open for 13% -> 4% of each run, Pallas kernels for 0% -> 12%
where the time goes in v1:
time: 727 us; the launch traced here: 721 us
  waiting for transfers between devices  326 us (45%)
  Pallas kernels  212 us (29%)
  starting transfers between devices  85.4 us (12%)
  local copies, waits for them, and re-layouts  65.2 us (9%)
  other arithmetic  29.3 us (4%)
    ppermute x106, waiting for transfers between devices, swap(): return lax.ppermute(block, AXES, [(j, j ^ 1 << bit) for j in range(total)])  326 us
    ppermute x106, starting transfers between devices, swap(): return lax.ppermute(block, AXES, [(j, j ^ 1 << bit) for j in range(total)])  85.4 us
    pallas_call x2, Pallas kernels, attend_grad(): pl.pallas_call(functools.partial(attend_grad_kernel, cross, images, rows...  71.4 us
    unnamed x294, local copies, waits for them, and re-layouts  62.5 us
    pallas_call x1, Pallas kernels, mlp_block(): pl.pallas_call(mlp_kernel, grid=(hidden // block,), out_shape=[jax.ShapeD...  52.9 us
    pallas_call x2, Pallas kernels, attend_block(): pl.pallas_call(functools.partial(attend_kernel, cross, images, rows // im...  35.1 us
    pallas_call x6, Pallas kernels, place(): pl.pallas_call(functools.partial(place_kernel, spreads, blocks_of), out_s...  27.7 us
    pallas_call x6, Pallas kernels, cut(): pl.pallas_call(functools.partial(cut_kernel, spreads, blocks_of, len(whol...  25.2 us
  transfers between devices with their start and end apart: 106, of which 37 were waited for; matrix products, arithmetic and copies ran while one was open for 4% of the time, Pallas kernels for 12%

profile of v1, /device:TPU:0, one launch (start us, length us, event | category | flops | bytes accessed | tf_op | source)
XLA Modules:
  0.0 721.4 jit_solution(12135860746462896800)
XLA Ops:
  1.5 2.9 collective-permute-start
  5.6 2.7 collective-permute-start.35
  12.0 2.7 collective-permute-start.1
  14.6 5.4 collective-permute-done.1
  20.7 2.9 collective-permute-done.2
  25.3 2.1 collective-permute-done.3
  27.3 2.0 collective-permute-start.17
  32.7 2.1 collective-permute-start.48
  34.8 11.9 %collective-permute-done.23 = bf16[1,64,1024]{2,1,0:T(8,128)(2,1)S(1)} collective-permute-done((bf16[1,64,1024]{2,1,0:T(8,128)(2,1)S(1)}, bf16[1,64,1024]{2,1,0:T(8,128)(2,1)S(1)}, u32[]{:S(2)}, u32[]{:S(2)}) %collective-permute-start.23) | collective-permute-done | bytes 131104 | tf_op jit(solution)/shard_map/ppermute | solution.py:50
  46.8 2.9 collective-permute-start.30
  49.9 2.9 collective-permute-start.6
  52.9 22.0 %collective-permute-done.42 = bf16[2,32,2048]{2,1,0:T(8,128)(2,1)S(1)} collective-permute-done((bf16[2,32,2048]{2,1,0:T(8,128)(2,1)S(1)}, bf16[2,32,2048]{2,1,0:T(8,128)(2,1)S(1)}, u32[]{:S(2)}, u32[]{:S(2)}) %collective-permute-start.42) | collective-permute-done | bytes 262176 | tf_op jit(solution)/shard_map/ppermute | solution.py:50
  74.9 5.7 collective-permute-done.12
  80.6 4.7 collective-permute-done.6
  85.4 5.5 collective-permute-done.24
  91.0 5.6 collective-permute-done.18
  98.0 26.5 %collective-permute-done.36 = bf16[2,512,128]{2,1,0:T(8,128)(2,1)S(1)} collective-permute-done((bf16[2,512,128]{2,1,0:T(8,128)(2,1)S(1)}, bf16[2,512,128]{2,1,0:T(8,128)(2,1)S(1)}, u32[]{:S(2)}, u32[]{:S(2)}) %collective-permute-start.36) | collective-permute-done | bytes 262176 | tf_op jit(solution)/shard_map/ppermute | solution.py:50
  124.6 2.1 collective-permute-start.43
  130.2 9.1 %collective-permute-done.49 = bf16[4,32,2048]{2,1,0:T(8,128)(2,1)S(1)} collective-permute-done((bf16[4,32,2048]{2,1,0:T(8,128)(2,1)S(1)}, bf16[4,32,2048]{2,1,0:T(8,128)(2,1)S(1)}, u32[]{:S(2)}, u32[]{:S(2)}) %collective-permute-start.49) | collective-permute-done | bytes 524320 | tf_op jit(solution)/shard_map/ppermute | solution.py:50
  139.3 10.3 %collective-permute-done.43 = bf16[4,32,2048]{2,1,0:T(8,128)(2,1)S(1)} collective-permute-done((bf16[4,32,2048]{2,1,0:T(8,128)(2,1)S(1)}, bf16[4,32,2048]{2,1,0:T(8,128)(2,1)S(1)}, u32[]{:S(2)}, u32[]{:S(2)}) %collective-permute-start.43) | collective-permute-done | bytes 524320 | tf_op jit(solution)/shard_map/ppermute | solution.py:50
  153.8 21.9 %collective-permute-done.26.refs_1_ = bf16[8,64,1024]{2,1,0:T(8,128)(2,1)S(1)} collective-permute-done((bf16[8,64,1024]{2,1,0:T(8,128)(2,1)S(1)}, bf16[8,64,1024]{2,1,0:T(8,128)(2,1)S(1)}, u32[]{:S(2)}, u32[]{:S(2)}) %collective-permute-start.26) | collective-permute-done | bytes 1048608 | tf_op jit(solution)/shard_map/ppermute | solution.py:50
  176.9 20.1 %collective-permute-done.8.refs_1_ = bf16[8,64,1024]{2,1,0:T(8,128)(2,1)S(1)} collective-permute-done((bf16[8,64,1024]{2,1,0:T(8,128)(2,1)S(1)}, bf16[8,64,1024]{2,1,0:T(8,128)(2,1)S(1)}, u32[]{:S(2)}, u32[]{:S(2)}) %collective-permute-start.8) | collective-permute-done | bytes 1048608 | tf_op jit(solution)/shard_map/ppermute | solution.py:50
  204.0 19.9 %collective-permute-done.32.refs_1_ = bf16[8,512,128]{2,1,0:T(8,128)(2,1)} collective-permute-done((bf16[8,512,128]{2,1,0:T(8,128)(2,1)S(1)}, bf16[8,512,128]{2,1,0:T(8,128)(2,1)}, u32[]{:S(2)}, u32[]{:S(2)}) %collective-permute-start.32) | collective-permute-done | bytes 1048608 | tf_op jit(solution)/shard_map/ppermute | solution.py:50
  239.3 5.7 shard_map.361
  247.7 5.5 shard_map.357
  255.9 5.5 shard_map.358
  264.1 5.5 shard_map.360
  273.3 3.0 shard_map.363.lift
  276.3 3.2 copy-done.1
  279.6 17.9 %shard_map.359 = (bf16[768,1024]{1,0:T(8,128)(2,1)S(1)}, bf16[768,1024]{1,0:T(8,128)(2,1)S(1)}, bf16[768,1024]{1,0:T(8,128)(2,1)S(1)}, bf16[768,1024]{1,0:T(8,128)(2,1)}, f32[768,1024]{1,0:T(8,128)}) custom-call(s32[3]{0:T(128)S(1)} %dynamic_slice.3.refs_0_, f32[4,1024]{1,0:T(4,128)S(1)} %reshape.100.refs_1_.refs_0_, bf16[768,1024]{1,0:T(8,128)(2,1)} %bitcast.87, ...), custom_call_target="tpu_custom_call" | custom-call | flops 7247757312 | bytes 17825792 | tf_op jit(solution)/shard_map/pallas_call | solution.py:371
  301.1 17.2 %shard_map.362 = (bf16[768,1024]{1,0:T(8,128)(2,1)S(1)}, bf16[768,1024]{1,0:T(8,128)(2,1)S(1)}, bf16[768,1024]{1,0:T(8,128)(2,1)S(1)}, bf16[768,1024]{1,0:T(8,128)(2,1)}, f32[768,1024]{1,0:T(8,128)}) custom-call(f32[4,1024]{1,0:T(4,128)S(1)} %reshape.100.refs_1_.refs_0_, f32[768,1024]{1,0:T(8,128)} %get-tuple-element.92.refs_1_, ...), custom_call_target="tpu_custom_call" | custom-call | flops 7247757312 | bytes 17825792 | tf_op jit(solution)/shard_map/pallas_call | solution.py:371
  321.9 2.4 shard_map.364.lower
  324.3 3.3 copy-done.2
  327.7 52.9 %shard_map.365 = (bf16[768,1024]{1,0:T(8,128)(2,1)}, f32[768,1024]{1,0:T(8,128)}, f32[1,1024]{1,0:T(1,128)}, bf16[1024,4096]{1,0:T(8,128)(2,1)}, bf16[1024,4096]{1,0:T(8,128)(2,1)}) custom-call(f32[1,1024]{1,0:T(1,128)} %slice.255.gain_row, f32[768,1024]{1,0:T(8,128)} %get-tuple-element.97.second, bf16[768,1024]{1,0:T(8,128)(2,1)} %bitcast.85, ...), custom_call_target="tpu_custom_call" | custom-call | flops 38654705664 | bytes 46137344 | tf_op jit(solution)/shard_map/pallas_call | solution.py:517
  380.5 35.2 %shard_map.366 = (f32[768,1024]{1,0:T(8,128)}, f32[1,1024]{1,0:T(1,128)}, bf16[1024,1024]{1,0:T(8,128)(2,1)}, bf16[1024,1024]{1,0:T(8,128)(2,1)}, bf16[1024,1024...) custom-call(f32[4,1024]{1,0:T(4,128)} %copy-done.70, f32[768,1024]{1,0:T(8,128)} %get-tuple-element.92.refs_1_, ...), custom_call_target="tpu_custom_call" | custom-call | flops 14898167808 | bytes 32505856 | tf_op jit(solution)/shard_map/pallas_call | solution.py:458
  415.8 36.2 %shard_map.367 = (f32[768,1024]{1,0:T(8,128)}, f32[768,1024]{1,0:T(8,128)}, f32[1,1024]{1,0:T(1,128)}, f32[1,1024]{1,0:T(1,128)}, bf16[1024,1024]{1,0:T(8,128)(2...) custom-call(s32[3]{0:T(128)} %copy-done.100, f32[4,1024]{1,0:T(4,128)} %copy-done.70, ...), custom_call_target="tpu_custom_call" | custom-call | flops 14898167808 | bytes 32505856 | tf_op jit(solution)/shard_map/pallas_call | solution.py:458
  458.8 4.1 shard_map.368
  465.2 3.5 collective-permute-done.103
  471.4 5.1 shard_map.369
  481.8 5.3 shard_map.370
  490.2 2.4 shard_map.372
  495.6 3.1 shard_map.373
  501.7 5.2 shard_map.371
  511.8 1.9 add_convert_fusion.22
  526.3 21.2 %collective-permute-done.55 = bf16[8,64,1024]{2,1,0:T(8,128)(2,1)S(1)} collective-permute-done((bf16[8,64,1024]{2,1,0:T(8,128)(2,1)S(1)}, bf16[8,64,1024]{2,1,0:T(8,128)(2,1)S(1)}, u32[]{:S(2)}, u32[]{:S(2)}) %collective-permute-start.55) | collective-permute-done | bytes 1048608 | tf_op jit(solution)/shard_map/ppermute | solution.py:50
  550.8 20.2 %collective-permute-done.61 = bf16[8,64,1024]{2,1,0:T(8,128)(2,1)S(1)} collective-permute-done((bf16[8,64,1024]{2,1,0:T(8,128)(2,1)S(1)}, bf16[8,64,1024]{2,1,0:T(8,128)(2,1)S(1)}, u32[]{:S(2)}, u32[]{:S(2)}) %collective-permute-start.61) | collective-permute-done | bytes 1048608 | tf_op jit(solution)/shard_map/ppermute | solution.py:50
  572.7 2.0 add_convert_fusion.21
  575.9 16.7 %collective-permute-done.67 = bf16[8,64,1024]{2,1,0:T(8,128)(2,1)S(1)} collective-permute-done((bf16[8,64,1024]{2,1,0:T(8,128)(2,1)S(1)}, bf16[8,64,1024]{2,1,0:T(8,128)(2,1)S(1)}, u32[]{:S(2)}, u32[]{:S(2)}) %collective-permute-start.67) | collective-permute-done | bytes 1048608 | tf_op jit(solution)/shard_map/ppermute | solution.py:50
  600.7 16.1 %collective-permute-done.79 = bf16[8,512,128]{2,1,0:T(8,128)(2,1)S(1)} collective-permute-done((bf16[8,512,128]{2,1,0:T(8,128)(2,1)S(1)}, bf16[8,512,128]{2,1,0:T(8,128)(2,1)S(1)}, u32[]{:S(2)}, u32[]{:S(2)}) %collective-permute-start.79) | collective-permute-done | bytes 1048608 | tf_op jit(solution)/shard_map/ppermute | solution.py:50
  624.2 2.0 collective-permute-start.92
  626.4 5.6 collective-permute-done.68
  634.0 10.8 %collective-permute-done.92 = bf16[4,32,2048]{2,1,0:T(8,128)(2,1)S(1)} collective-permute-done((bf16[4,32,2048]{2,1,0:T(8,128)(2,1)S(1)}, bf16[4,32,2048]{2,1,0:T(8,128)(2,1)S(1)}, u32[]{:S(2)}, u32[]{:S(2)}) %collective-permute-start.92) | collective-permute-done | bytes 524320 | tf_op jit(solution)/shard_map/ppermute | solution.py:50
  644.9 3.0 collective-permute-start.63
  648.4 8.4 %collective-permute-done.98 = bf16[4,32,2048]{2,1,0:T(8,128)(2,1)S(1)} collective-permute-done((bf16[4,32,2048]{2,1,0:T(8,128)(2,1)S(1)}, bf16[4,32,2048]{2,1,0:T(8,128)(2,1)S(1)}, u32[]{:S(2)}, u32[]{:S(2)}) %collective-permute-start.98) | collective-permute-done | bytes 524320 | tf_op jit(solution)/shard_map/ppermute | solution.py:50
  657.2 2.1 collective-permute-start.81
  659.5 2.5 collective-permute-done.57
  662.2 5.5 collective-permute-done.63
  667.8 7.9 %collective-permute-done.69 = bf16[2,64,1024]{2,1,0:T(8,128)(2,1)S(1)} collective-permute-done((bf16[2,64,1024]{2,1,0:T(8,128)(2,1)S(1)}, bf16[2,64,1024]{2,1,0:T(8,128)(2,1)S(1)}, u32[]{:S(2)}, u32[]{:S(2)}) %collective-permute-start.69) | collective-permute-done | bytes 262176 | tf_op jit(solution)/shard_map/ppermute | solution.py:50
  675.8 6.7 collective-permute-done.75
  683.6 5.6 collective-permute-done.81
  689.9 2.7 collective-permute-start.70
  692.7 13.1 %collective-permute-done.99 = bf16[2,32,2048]{2,1,0:T(8,128)(2,1)S(1)} collective-permute-done((bf16[2,32,2048]{2,1,0:T(8,128)(2,1)S(1)}, bf16[2,32,2048]{2,1,0:T(8,128)(2,1)S(1)}, u32[]{:S(2)}, u32[]{:S(2)}) %collective-permute-start.99) | collective-permute-done | bytes 262176 | tf_op jit(solution)/shard_map/ppermute | solution.py:50
  705.9 3.0 collective-permute-start.82
  710.6 2.5 collective-permute-done.76
  (598 shorter events, 142.5 us)
Async XLA Ops:
  5.6 27.1 %collective-permute-start.35 = (bf16[1,512,128]{2,1,0:T(8,128)(2,1)S(1)}, bf16[1,512,128]{2,1,0:T(8,128)(2,1)S(1)}, u32[]{:S(2)}, u32[]{:S(2)}) collective-permute-start(bf16[1,512,128]{2,1,0:T(8,128)(2,1)S(1)} %get-tuple-element.180), channel_id=1, source_target_pairs={{0,2},{1,3},{2,0},{3,1},{4,6},{5,7},{6,4},{7,5},{8,10},{9,11},{10,... | collective-permute-start | bytes 393224 | tf_op jit(solution)/shard_map/ppermute | solution.py:50
  8.2 23.4 %collective-permute-start.29 = (bf16[1,512,128]{2,1,0:T(8,128)(2,1)S(1)}, bf16[1,512,128]{2,1,0:T(8,128)(2,1)S(1)}, u32[]{:S(2)}, u32[]{:S(2)}) collective-permute-start(bf16[1,512,128]{2,1,0:T(8,128)(2,1)S(1)} %get-tuple-element.181), channel_id=1, source_target_pairs={{0,2},{1,3},{2,0},{3,1},{4,6},{5,7},{6,4},{7,5},{8,10},{9,11},{10,... | collective-permute-start | bytes 393224 | tf_op jit(solution)/shard_map/ppermute | solution.py:50
  32.7 65.1 %collective-permute-start.48 = (bf16[2,32,2048]{2,1,0:T(8,128)(2,1)S(1)}, bf16[2,32,2048]{2,1,0:T(8,128)(2,1)S(1)}, u32[]{:S(2)}, u32[]{:S(2)}) collective-permute-start(bf16[2,32,2048]{2,1,0:T(8,128)(2,1)S(1)} %pad_maximum_fusion.23), channel_id=1, source_target_pairs={{0,2},{1,3},{2,0},{3,1},{4,6},{5,7},{6,4},{7,5},{8,10},{9,11},{10,... | collective-permute-start | bytes 786440 | tf_op jit(solution)/shard_map/ppermute | solution.py:50
  46.7 28.1 %collective-permute-start.42 = (bf16[2,32,2048]{2,1,0:T(8,128)(2,1)S(1)}, bf16[2,32,2048]{2,1,0:T(8,128)(2,1)S(1)}, u32[]{:S(2)}, u32[]{:S(2)}) collective-permute-start(bf16[2,32,2048]{2,1,0:T(8,128)(2,1)S(1)} %pad_maximum_fusion.22), channel_id=1, source_target_pairs={{0,2},{1,3},{2,0},{3,1},{4,6},{5,7},{6,4},{7,5},{8,10},{9,11},{10,... | collective-permute-start | bytes 786440 | tf_op jit(solution)/shard_map/ppermute | solution.py:50
  46.8 50.9 %collective-permute-start.30 = (bf16[2,512,128]{2,1,0:T(8,128)(2,1)S(1)}, bf16[2,512,128]{2,1,0:T(8,128)(2,1)S(1)}, u32[]{:S(2)}, u32[]{:S(2)}) collective-permute-start(bf16[2,512,128]{2,1,0:T(8,128)(2,1)S(1)} %pad_maximum_fusion.20), channel_id=1, source_target_pairs={{0,1},{1,0},{2,3},{3,2},{4,5},{5,4},{6,7},{7,6},{8,9},{9,8},{10,11... | collective-permute-start | bytes 786440 | tf_op jit(solution)/shard_map/ppermute | solution.py:50
  49.7 30.8 %collective-permute-start.12 = (bf16[2,64,1024]{2,1,0:T(8,128)(2,1)S(1)}, bf16[2,64,1024]{2,1,0:T(8,128)(2,1)S(1)}, u32[]{:S(2)}, u32[]{:S(2)}) collective-permute-start(bf16[2,64,1024]{2,1,0:T(8,128)(2,1)S(1)} %pad_maximum_fusion.17), channel_id=1, source_target_pairs={{0,2},{1,3},{2,0},{3,1},{4,6},{5,7},{6,4},{7,5},{8,10},{9,11},{10,... | collective-permute-start | bytes 786440 | tf_op jit(solution)/shard_map/ppermute | solution.py:50
  49.9 35.4 %collective-permute-start.6 = (bf16[2,64,1024]{2,1,0:T(8,128)(2,1)S(1)}, bf16[2,64,1024]{2,1,0:T(8,128)(2,1)S(1)}, u32[]{:S(2)}, u32[]{:S(2)}) collective-permute-start(bf16[2,64,1024]{2,1,0:T(8,128)(2,1)S(1)} %pad_maximum_fusion.16), channel_id=1, source_target_pairs={{0,2},{1,3},{2,0},{3,1},{4,6},{5,7},{6,4},{7,5},{8,10},{9,11},{10,... | collective-permute-start | bytes 786440 | tf_op jit(solution)/shard_map/ppermute | solution.py:50
  85.3 41.4 %collective-permute-start.13 = (bf16[4,64,1024]{2,1,0:T(8,128)(2,1)S(1)}, bf16[4,64,1024]{2,1,0:T(8,128)(2,1)S(1)}, u32[]{:S(2)}, u32[]{:S(2)}) collective-permute-start(bf16[4,64,1024]{2,1,0:T(8,128)(2,1)S(1)} %pad_maximum_fusion.9), channel_id=1, source_target_pairs={{0,1},{1,0},{2,3},{3,2},{4,5},{5,4},{6,7},{7,6},{8,9},{9,8},{10,11... | collective-permute-start | bytes 1572872 | tf_op jit(solution)/shard_map/ppermute | solution.py:50
  90.9 36.9 %collective-permute-start.7 = (bf16[4,64,1024]{2,1,0:T(8,128)(2,1)S(1)}, bf16[4,64,1024]{2,1,0:T(8,128)(2,1)S(1)}, u32[]{:S(2)}, u32[]{:S(2)}) collective-permute-start(bf16[4,64,1024]{2,1,0:T(8,128)(2,1)S(1)} %pad_maximum_fusion.8), channel_id=1, source_target_pairs={{0,1},{1,0},{2,3},{3,2},{4,5},{5,4},{6,7},{7,6},{8,9},{9,8},{10,11... | collective-permute-start | bytes 1572872 | tf_op jit(solution)/shard_map/ppermute | solution.py:50
  96.5 32.2 %collective-permute-start.25 = (bf16[4,64,1024]{2,1,0:T(8,128)(2,1)S(1)}, bf16[4,64,1024]{2,1,0:T(8,128)(2,1)S(1)}, u32[]{:S(2)}, u32[]{:S(2)}) collective-permute-start(bf16[4,64,1024]{2,1,0:T(8,128)(2,1)S(1)} %pad_maximum_fusion.11), channel_id=1, source_target_pairs={{0,16},{1,17},{2,18},{3,19},{4,20},{5,21},{6,22},{7,23},{8,24},{9,... | collective-permute-start | bytes 1572872 | tf_op jit(solution)/shard_map/ppermute | solution.py:50
  97.7 26.9 %collective-permute-start.36 = (bf16[2,512,128]{2,1,0:T(8,128)(2,1)S(1)}, bf16[2,512,128]{2,1,0:T(8,128)(2,1)S(1)}, u32[]{:S(2)}, u32[]{:S(2)}) collective-permute-start(bf16[2,512,128]{2,1,0:T(8,128)(2,1)S(1)} %pad_maximum_fusion.21), channel_id=1, source_target_pairs={{0,1},{1,0},{2,3},{3,2},{4,5},{5,4},{6,7},{7,6},{8,9},{9,8},{10,11... | collective-permute-start | bytes 786440 | tf_op jit(solution)/shard_map/ppermute | solution.py:50
  97.8 26.8 %collective-permute-start.4 = (bf16[16,128]{1,0:T(8,128)(2,1)S(1)}, bf16[16,128]{1,0:T(8,128)(2,1)S(1)}, u32[]{:S(2)}, u32[]{:S(2)}) collective-permute-start(bf16[16,128]{1,0:T(8,128)(2,1)S(1)} %concatenate.131), channel_id=1, source_target_pairs={{0,4},{1,5},{2,6},{3,7},{4,0},{5,1},{6,2},{7,3},{8,12},{9,13},{10,... | collective-permute-start | bytes 12296 | tf_op jit(solution)/shard_map/ppermute | solution.py:50
  124.6 25.0 %collective-permute-start.43 = (bf16[4,32,2048]{2,1,0:T(8,128)(2,1)S(1)}, bf16[4,32,2048]{2,1,0:T(8,128)(2,1)S(1)}, u32[]{:S(2)}, u32[]{:S(2)}) collective-permute-start(bf16[4,32,2048]{2,1,0:T(8,128)(2,1)S(1)} %pad_maximum_fusion.14), channel_id=1, source_target_pairs={{0,1},{1,0},{2,3},{3,2},{4,5},{5,4},{6,7},{7,6},{8,9},{9,8},{10,11... | collective-permute-start | bytes 1572872 | tf_op jit(solution)/shard_map/ppermute | solution.py:50
  128.8 23.8 %collective-permute-start.19 = (bf16[4,64,1024]{2,1,0:T(8,128)(2,1)S(1)}, bf16[4,64,1024]{2,1,0:T(8,128)(2,1)S(1)}, u32[]{:S(2)}, u32[]{:S(2)}) collective-permute-start(bf16[4,64,1024]{2,1,0:T(8,128)(2,1)S(1)} %pad_maximum_fusion.10), channel_id=1, source_target_pairs={{0,8},{1,9},{2,10},{3,11},{4,12},{5,13},{6,14},{7,15},{8,0},{9,1},... | collective-permute-start | bytes 1572872 | tf_op jit(solution)/shard_map/ppermute | solution.py:50
  149.6 26.1 %collective-permute-start.26 = (bf16[8,64,1024]{2,1,0:T(8,128)(2,1)S(1)}, bf16[8,64,1024]{2,1,0:T(8,128)(2,1)S(1)}, u32[]{:S(2)}, u32[]{:S(2)}) collective-permute-start(bf16[8,64,1024]{2,1,0:T(8,128)(2,1)S(1)} %pad_maximum_fusion.3.refs_0_), channel_id=1, source_target_pairs={{0,8},{1,9},{2,10},{3,11},{4,12},{5,13},{6,14},{7,15},{8,0},{9,1},... | collective-permute-start | bytes 3145736 | tf_op jit(solution)/shard_map/ppermute | solution.py:50
  150.0 25.7 %collective-permute-start.9 = (bf16[8,64,1024]{2,1,0:T(8,128)(2,1)S(1)}, bf16[8,64,1024]{2,1,0:T(8,128)(2,1)S(1)}, u32[]{:S(2)}, u32[]{:S(2)}) collective-permute-start(bf16[8,64,1024]{2,1,0:T(8,128)(2,1)S(1)} %pad_maximum_fusion.refs_0_), channel_id=1, source_target_pairs={{0,4},{1,5},{2,6},{3,7},{4,0},{5,1},{6,2},{7,3},{8,12},{9,13},{10,... | collective-permute-start | bytes 3145736 | tf_op jit(solution)/shard_map/ppermute | solution.py:50
  150.0 46.9 %collective-permute-start.8 = (bf16[8,64,1024]{2,1,0:T(8,128)(2,1)S(1)}, bf16[8,64,1024]{2,1,0:T(8,128)(2,1)S(1)}, u32[]{:S(2)}, u32[]{:S(2)}) collective-permute-start(bf16[8,64,1024]{2,1,0:T(8,128)(2,1)S(1)} %pad_maximum_fusion.refs_0_), channel_id=1, source_target_pairs={{0,8},{1,9},{2,10},{3,11},{4,12},{5,13},{6,14},{7,15},{8,0},{9,1},... | collective-permute-start | bytes 3145736 | tf_op jit(solution)/shard_map/ppermute | solution.py:50
  152.6 44.4 %collective-permute-start.15 = (bf16[8,64,1024]{2,1,0:T(8,128)(2,1)S(1)}, bf16[8,64,1024]{2,1,0:T(8,128)(2,1)S(1)}, u32[]{:S(2)}, u32[]{:S(2)}) collective-permute-start(bf16[8,64,1024]{2,1,0:T(8,128)(2,1)S(1)} %pad_maximum_fusion.1.refs_0_), channel_id=1, source_target_pairs={{0,4},{1,5},{2,6},{3,7},{4,0},{5,1},{6,2},{7,3},{8,12},{9,13},{10,... | collective-permute-start | bytes 3145736 | tf_op jit(solution)/shard_map/ppermute | solution.py:50
  152.9 46.1 %collective-permute-start.14 = (bf16[8,64,1024]{2,1,0:T(8,128)(2,1)S(1)}, bf16[8,64,1024]{2,1,0:T(8,128)(2,1)S(1)}, u32[]{:S(2)}, u32[]{:S(2)}) collective-permute-start(bf16[8,64,1024]{2,1,0:T(8,128)(2,1)S(1)} %pad_maximum_fusion.1.refs_0_), channel_id=1, source_target_pairs={{0,16},{1,17},{2,18},{3,19},{4,20},{5,21},{6,22},{7,23},{8,24},{9,... | collective-permute-start | bytes 3145736 | tf_op jit(solution)/shard_map/ppermute | solution.py:50
  175.7 23.9 %collective-permute-start.21 = (bf16[8,64,1024]{2,1,0:T(8,128)(2,1)S(1)}, bf16[8,64,1024]{2,1,0:T(8,128)(2,1)S(1)}, u32[]{:S(2)}, u32[]{:S(2)}) collective-permute-start(bf16[8,64,1024]{2,1,0:T(8,128)(2,1)S(1)} %pad_maximum_fusion.2.refs_0_), channel_id=1, source_target_pairs={{0,4},{1,5},{2,6},{3,7},{4,0},{5,1},{6,2},{7,3},{8,12},{9,13},{10,... | collective-permute-start | bytes 3145736 | tf_op jit(solution)/shard_map/ppermute | solution.py:50
  175.7 25.8 %collective-permute-start.20 = (bf16[8,64,1024]{2,1,0:T(8,128)(2,1)S(1)}, bf16[8,64,1024]{2,1,0:T(8,128)(2,1)S(1)}, u32[]{:S(2)}, u32[]{:S(2)}) collective-permute-start(bf16[8,64,1024]{2,1,0:T(8,128)(2,1)S(1)} %pad_maximum_fusion.2.refs_0_), channel_id=1, source_target_pairs={{0,16},{1,17},{2,18},{3,19},{4,20},{5,21},{6,22},{7,23},{8,24},{9,... | collective-permute-start | bytes 3145736 | tf_op jit(solution)/shard_map/ppermute | solution.py:50
  197.9 25.9 %collective-permute-start.32 = (bf16[8,512,128]{2,1,0:T(8,128)(2,1)S(1)}, bf16[8,512,128]{2,1,0:T(8,128)(2,1)}, u32[]{:S(2)}, u32[]{:S(2)}) collective-permute-start(bf16[8,512,128]{2,1,0:T(8,128)(2,1)S(1)} %pad_maximum_fusion.4.refs_0_), channel_id=1, source_target_pairs={{0,16},{1,17},{2,18},{3,19},{4,20},{5,21},{6,22},{7,23},{8,24},{9,... | collective-permute-start | bytes 3145736 | tf_op jit(solution)/shard_map/ppermute | solution.py:50
  199.0 27.1 %collective-permute-start.38 = (bf16[8,512,128]{2,1,0:T(8,128)(2,1)S(1)}, bf16[8,512,128]{2,1,0:T(8,128)(2,1)}, u32[]{:S(2)}, u32[]{:S(2)}) collective-permute-start(bf16[8,512,128]{2,1,0:T(8,128)(2,1)S(1)} %pad_maximum_fusion.5.refs_4_), channel_id=1, source_target_pairs={{0,8},{1,9},{2,10},{3,11},{4,12},{5,13},{6,14},{7,15},{8,0},{9,1},... | collective-permute-start | bytes 3145736 | tf_op jit(solution)/shard_map/ppermute | solution.py:50
  200.5 26.1 %collective-permute-start.28 = (bf16[8,64,1024]{2,1,0:T(8,128)(2,1)S(1)}, bf16[8,64,1024]{2,1,0:T(8,128)(2,1)S(1)}, u32[]{:S(2)}, u32[]{:S(2)}) collective-permute-start(bf16[8,64,1024]{2,1,0:T(8,128)(2,1)S(1)} %collective-permute-done.26.refs_1_), channel_id=1, source_target_pairs={{0,4},{1,5},{2,6},{3,7},{4,0},{5,1},{6,2},{7,3},{8,12},{9,13},{10,... | collective-permute-start | bytes 3145736 | tf_op jit(solution)/shard_map/ppermute | solution.py:50
  201.5 27.3 %collective-permute-start.10 = (bf16[8,64,1024]{2,1,0:T(8,128)(2,1)S(1)}, bf16[8,64,1024]{2,1,0:T(8,128)(2,1)S(1)}, u32[]{:S(2)}, u32[]{:S(2)}) collective-permute-start(bf16[8,64,1024]{2,1,0:T(8,128)(2,1)S(1)} %collective-permute-done.8.refs_1_), channel_id=1, source_target_pairs={{0,4},{1,5},{2,6},{3,7},{4,0},{5,1},{6,2},{7,3},{8,12},{9,13},{10,... | collective-permute-start | bytes 3145736 | tf_op jit(solution)/shard_map/ppermute | solution.py:50
  202.5 28.2 %collective-permute-start.16 = (bf16[8,64,1024]{2,1,0:T(8,128)(2,1)S(1)}, bf16[8,64,1024]{2,1,0:T(8,128)(2,1)S(1)}, u32[]{:S(2)}, u32[]{:S(2)}) collective-permute-start(bf16[8,64,1024]{2,1,0:T(8,128)(2,1)S(1)} %collective-permute-done.14.refs_1_), channel_id=1, source_target_pairs={{0,4},{1,5},{2,6},{3,7},{4,0},{5,1},{6,2},{7,3},{8,12},{9,13},{10,... | collective-permute-start | bytes 3145736 | tf_op jit(solution)/shard_map/ppermute | solution.py:50
  226.2 46.1 %collective-permute-start.39 = (bf16[8,512,128]{2,1,0:T(8,128)(2,1)S(1)}, bf16[8,512,128]{2,1,0:T(8,128)(2,1)}, u32[]{:S(2)}, u32[]{:S(2)}) collective-permute-start(bf16[8,512,128]{2,1,0:T(8,128)(2,1)S(1)} %pad_maximum_fusion.5.refs_4_), channel_id=1, source_target_pairs={{0,4},{1,5},{2,6},{3,7},{4,0},{5,1},{6,2},{7,3},{8,12},{9,13},{10,... | collective-permute-start | bytes 3145736 | tf_op jit(solution)/shard_map/ppermute | solution.py:50
  227.7 44.6 %collective-permute-start.44 = (bf16[8,32,2048]{2,1,0:T(8,128)(2,1)}, bf16[8,32,2048]{2,1,0:T(8,128)(2,1)}, u32[]{:S(2)}, u32[]{:S(2)}) collective-permute-start(bf16[8,32,2048]{2,1,0:T(8,128)(2,1)} %pad_maximum_fusion.6.refs_0_), channel_id=1, source_target_pairs={{0,16},{1,17},{2,18},{3,19},{4,20},{5,21},{6,22},{7,23},{8,24},{9,... | collective-permute-start | bytes 3145736 | tf_op jit(solution)/shard_map/ppermute | solution.py:50
  229.7 43.1 %collective-permute-start.50 = (bf16[8,32,2048]{2,1,0:T(8,128)(2,1)S(1)}, bf16[8,32,2048]{2,1,0:T(8,128)(2,1)}, u32[]{:S(2)}, u32[]{:S(2)}) collective-permute-start(bf16[8,32,2048]{2,1,0:T(8,128)(2,1)S(1)} %pad_maximum_fusion.7.refs_4_), channel_id=1, source_target_pairs={{0,8},{1,9},{2,10},{3,11},{4,12},{5,13},{6,14},{7,15},{8,0},{9,1},... | collective-permute-start | bytes 3145736 | tf_op jit(solution)/shard_map/ppermute | solution.py:50
  231.7 41.2 %collective-permute-start.34 = (bf16[8,512,128]{2,1,0:T(8,128)(2,1)}, bf16[8,512,128]{2,1,0:T(8,128)(2,1)}, u32[]{:S(2)}, u32[]{:S(2)}) collective-permute-start(bf16[8,512,128]{2,1,0:T(8,128)(2,1)} %collective-permute-done.32.refs_1_), channel_id=1, source_target_pairs={{0,4},{1,5},{2,6},{3,7},{4,0},{5,1},{6,2},{7,3},{8,12},{9,13},{10,... | collective-permute-start | bytes 3145736 | tf_op jit(solution)/shard_map/ppermute | solution.py:50
  232.7 40.6 %collective-permute-start.40 = (bf16[8,512,128]{2,1,0:T(8,128)(2,1)}, bf16[8,512,128]{2,1,0:T(8,128)(2,1)}, u32[]{:S(2)}, u32[]{:S(2)}) collective-permute-start(bf16[8,512,128]{2,1,0:T(8,128)(2,1)} %collective-permute-done.38.refs_5_), channel_id=1, source_target_pairs={{0,4},{1,5},{2,6},{3,7},{4,0},{5,1},{6,2},{7,3},{8,12},{9,13},{10,... | collective-permute-start | bytes 3145736 | tf_op jit(solution)/shard_map/ppermute | solution.py:50
  272.3 49.5 %collective-permute-start.45 = (bf16[8,32,2048]{2,1,0:T(8,128)(2,1)}, bf16[8,32,2048]{2,1,0:T(8,128)(2,1)S(1)}, u32[]{:S(2)}, u32[]{:S(2)}) collective-permute-start(bf16[8,32,2048]{2,1,0:T(8,128)(2,1)} %pad_maximum_fusion.6.refs_0_), channel_id=1, source_target_pairs={{0,4},{1,5},{2,6},{3,7},{4,0},{5,1},{6,2},{7,3},{8,12},{9,13},{10,... | collective-permute-start | bytes 3145736 | tf_op jit(solution)/shard_map/ppermute | solution.py:50
  272.3 49.5 %collective-permute-start.51 = (bf16[8,32,2048]{2,1,0:T(8,128)(2,1)S(1)}, bf16[8,32,2048]{2,1,0:T(8,128)(2,1)S(1)}, u32[]{:S(2)}, u32[]{:S(2)}) collective-permute-start(bf16[8,32,2048]{2,1,0:T(8,128)(2,1)S(1)} %pad_maximum_fusion.7.refs_4_), channel_id=1, source_target_pairs={{0,4},{1,5},{2,6},{3,7},{4,0},{5,1},{6,2},{7,3},{8,12},{9,13},{10,... | collective-permute-start | bytes 3145736 | tf_op jit(solution)/shard_map/ppermute | solution.py:50
  272.8 49.0 %collective-permute-start.46 = (bf16[8,32,2048]{2,1,0:T(8,128)(2,1)}, bf16[8,32,2048]{2,1,0:T(8,128)(2,1)S(1)}, u32[]{:S(2)}, u32[]{:S(2)}) collective-permute-start(bf16[8,32,2048]{2,1,0:T(8,128)(2,1)} %collective-permute-done.44.refs_1_), channel_id=1, source_target_pairs={{0,4},{1,5},{2,6},{3,7},{4,0},{5,1},{6,2},{7,3},{8,12},{9,13},{10,... | collective-permute-start | bytes 3145736 | tf_op jit(solution)/shard_map/ppermute | solution.py:50
  272.9 49.0 %collective-permute-start.52 = (bf16[8,32,2048]{2,1,0:T(8,128)(2,1)}, bf16[8,32,2048]{2,1,0:T(8,128)(2,1)S(1)}, u32[]{:S(2)}, u32[]{:S(2)}) collective-permute-start(bf16[8,32,2048]{2,1,0:T(8,128)(2,1)} %collective-permute-done.50.refs_5_), channel_id=1, source_target_pairs={{0,4},{1,5},{2,6},{3,7},{4,0},{5,1},{6,2},{7,3},{8,12},{9,13},{10,... | collective-permute-start | bytes 3145736 | tf_op jit(solution)/shard_map/ppermute | solution.py:50
  464.9 46.8 %collective-permute-start.54 = (bf16[8,64,1024]{2,1,0:T(8,128)(2,1)}, bf16[8,64,1024]{2,1,0:T(8,128)(2,1)}, u32[]{:S(2)}, u32[]{:S(2)}) collective-permute-start(bf16[8,64,1024]{2,1,0:T(8,128)(2,1)} %get-tuple-element.116), channel_id=1, source_target_pairs={{0,4},{1,5},{2,6},{3,7},{4,0},{5,1},{6,2},{7,3},{8,12},{9,13},{10,... | collective-permute-start | bytes 3145736 | tf_op jit(solution)/shard_map/ppermute | solution.py:50
  469.8 51.2 %collective-permute-start.53 = (bf16[8,64,1024]{2,1,0:T(8,128)(2,1)}, bf16[8,64,1024]{2,1,0:T(8,128)(2,1)}, u32[]{:S(2)}, u32[]{:S(2)}) collective-permute-start(bf16[8,64,1024]{2,1,0:T(8,128)(2,1)} %get-tuple-element.114), channel_id=1, source_target_pairs={{0,4},{1,5},{2,6},{3,7},{4,0},{5,1},{6,2},{7,3},{8,12},{9,13},{10,... | collective-permute-start | bytes 3145736 | tf_op jit(solution)/shard_map/ppermute | solution.py:50
  479.5 34.3 %collective-permute-start.60 = (bf16[8,64,1024]{2,1,0:T(8,128)(2,1)}, bf16[8,64,1024]{2,1,0:T(8,128)(2,1)}, u32[]{:S(2)}, u32[]{:S(2)}) collective-permute-start(bf16[8,64,1024]{2,1,0:T(8,128)(2,1)} %get-tuple-element.122), channel_id=1, source_target_pairs={{0,4},{1,5},{2,6},{3,7},{4,0},{5,1},{6,2},{7,3},{8,12},{9,13},{10,... | collective-permute-start | bytes 3145736 | tf_op jit(solution)/shard_map/ppermute | solution.py:50
  480.0 30.0 %collective-permute-start.105 = (f32[1,128]{1,0:T(1,128)S(1)}, f32[1,128]{1,0:T(1,128)S(1)}, u32[]{:S(2)}, u32[]{:S(2)}) collective-permute-start(f32[1,128]{1,0:T(1,128)S(1)} %slice.333), channel_id=1, source_target_pairs={{0,8},{1,9},{2,10},{3,11},{4,12},{5,13},{6,14},{7,15},{8,0},{9,1},... | collective-permute-start | bytes 1544 | tf_op jit(solution)/shard_map/ppermute | solution.py:50
  490.2 26.1 %collective-permute-start.66 = (bf16[8,64,1024]{2,1,0:T(8,128)(2,1)}, bf16[8,64,1024]{2,1,0:T(8,128)(2,1)}, u32[]{:S(2)}, u32[]{:S(2)}) collective-permute-start(bf16[8,64,1024]{2,1,0:T(8,128)(2,1)} %get-tuple-element.128), channel_id=1, source_target_pairs={{0,4},{1,5},{2,6},{3,7},{4,0},{5,1},{6,2},{7,3},{8,12},{9,13},{10,... | collective-permute-start | bytes 3145736 | tf_op jit(solution)/shard_map/ppermute | solution.py:50
  522.1 25.4 %collective-permute-start.55 = (bf16[8,64,1024]{2,1,0:T(8,128)(2,1)S(1)}, bf16[8,64,1024]{2,1,0:T(8,128)(2,1)S(1)}, u32[]{:S(2)}, u32[]{:S(2)}) collective-permute-start(bf16[8,64,1024]{2,1,0:T(8,128)(2,1)S(1)} %add_convert_fusion.22), channel_id=1, source_target_pairs={{0,8},{1,9},{2,10},{3,11},{4,12},{5,13},{6,14},{7,15},{8,0},{9,1},... | collective-permute-start | bytes 3145736 | tf_op jit(solution)/shard_map/ppermute | solution.py:50
  522.4 26.0 %collective-permute-start.91 = (bf16[8,32,2048]{2,1,0:T(8,128)(2,1)S(1)}, bf16[8,32,2048]{2,1,0:T(8,128)(2,1)S(1)}, u32[]{:S(2)}, u32[]{:S(2)}) collective-permute-start(bf16[8,32,2048]{2,1,0:T(8,128)(2,1)S(1)} %add_convert_fusion.4), channel_id=1, source_target_pairs={{0,16},{1,17},{2,18},{3,19},{4,20},{5,21},{6,22},{7,23},{8,24},{9,... | collective-permute-start | bytes 3145736 | tf_op jit(solution)/shard_map/ppermute | solution.py:50
  524.1 46.8 %collective-permute-start.61 = (bf16[8,64,1024]{2,1,0:T(8,128)(2,1)S(1)}, bf16[8,64,1024]{2,1,0:T(8,128)(2,1)S(1)}, u32[]{:S(2)}, u32[]{:S(2)}) collective-permute-start(bf16[8,64,1024]{2,1,0:T(8,128)(2,1)S(1)} %add_convert_fusion.19), channel_id=1, source_target_pairs={{0,16},{1,17},{2,18},{3,19},{4,20},{5,21},{6,22},{7,23},{8,24},{9,... | collective-permute-start | bytes 3145736 | tf_op jit(solution)/shard_map/ppermute | solution.py:50
  525.5 49.8 %collective-permute-start.71 = (bf16[8,64,1024]{2,1,0:T(8,128)(2,1)S(1)}, bf16[8,64,1024]{2,1,0:T(8,128)(2,1)S(1)}, u32[]{:S(2)}, u32[]{:S(2)}) collective-permute-start(bf16[8,64,1024]{2,1,0:T(8,128)(2,1)S(1)} %copy-done.86), channel_id=1, source_target_pairs={{0,4},{1,5},{2,6},{3,7},{4,0},{5,1},{6,2},{7,3},{8,12},{9,13},{10,... | collective-permute-start | bytes 3145736 | tf_op jit(solution)/shard_map/ppermute | solution.py:50
  526.1 68.1 %collective-permute-start.95 = (bf16[8,32,2048]{2,1,0:T(8,128)(2,1)S(1)}, bf16[8,32,2048]{2,1,0:T(8,128)(2,1)S(1)}, u32[]{:S(2)}, u32[]{:S(2)}) collective-permute-start(bf16[8,32,2048]{2,1,0:T(8,128)(2,1)S(1)} %copy-done.84), channel_id=1, source_target_pairs={{0,4},{1,5},{2,6},{3,7},{4,0},{5,1},{6,2},{7,3},{8,12},{9,13},{10,... | collective-permute-start | bytes 3145736 | tf_op jit(solution)/shard_map/ppermute | solution.py:50
  547.5 45.0 %collective-permute-start.67 = (bf16[8,64,1024]{2,1,0:T(8,128)(2,1)S(1)}, bf16[8,64,1024]{2,1,0:T(8,128)(2,1)S(1)}, u32[]{:S(2)}, u32[]{:S(2)}) collective-permute-start(bf16[8,64,1024]{2,1,0:T(8,128)(2,1)S(1)} %add_convert_fusion.16), channel_id=1, source_target_pairs={{0,16},{1,17},{2,18},{3,19},{4,20},{5,21},{6,22},{7,23},{8,24},{9,... | collective-permute-start | bytes 3145736 | tf_op jit(solution)/shard_map/ppermute | solution.py:50
  548.5 46.3 %collective-permute-start.73 = (bf16[8,64,1024]{2,1,0:T(8,128)(2,1)S(1)}, bf16[8,64,1024]{2,1,0:T(8,128)(2,1)S(1)}, u32[]{:S(2)}, u32[]{:S(2)}) collective-permute-start(bf16[8,64,1024]{2,1,0:T(8,128)(2,1)S(1)} %add_convert_fusion.13), channel_id=1, source_target_pairs={{0,8},{1,9},{2,10},{3,11},{4,12},{5,13},{6,14},{7,15},{8,0},{9,1},... | collective-permute-start | bytes 3145736 | tf_op jit(solution)/shard_map/ppermute | solution.py:50
  570.9 26.3 %collective-permute-start.97 = (bf16[8,32,2048]{2,1,0:T(8,128)(2,1)S(1)}, bf16[8,32,2048]{2,1,0:T(8,128)(2,1)S(1)}, u32[]{:S(2)}, u32[]{:S(2)}) collective-permute-start(bf16[8,32,2048]{2,1,0:T(8,128)(2,1)S(1)} %add_convert_fusion.1), channel_id=1, source_target_pairs={{0,8},{1,9},{2,10},{3,11},{4,12},{5,13},{6,14},{7,15},{8,0},{9,1},... | collective-permute-start | bytes 3145736 | tf_op jit(solution)/shard_map/ppermute | solution.py:50
  575.8 23.8 %collective-permute-start.77 = (bf16[8,512,128]{2,1,0:T(8,128)(2,1)S(1)}, bf16[8,512,128]{2,1,0:T(8,128)(2,1)S(1)}, u32[]{:S(2)}, u32[]{:S(2)}) collective-permute-start(bf16[8,512,128]{2,1,0:T(8,128)(2,1)S(1)} %copy-done.82), channel_id=1, source_target_pairs={{0,4},{1,5},{2,6},{3,7},{4,0},{5,1},{6,2},{7,3},{8,12},{9,13},{10,... | collective-permute-start | bytes 3145736 | tf_op jit(solution)/shard_map/ppermute | solution.py:50
  592.5 24.3 %collective-permute-start.79 = (bf16[8,512,128]{2,1,0:T(8,128)(2,1)S(1)}, bf16[8,512,128]{2,1,0:T(8,128)(2,1)S(1)}, u32[]{:S(2)}, u32[]{:S(2)}) collective-permute-start(bf16[8,512,128]{2,1,0:T(8,128)(2,1)S(1)} %add_convert_fusion.10), channel_id=1, source_target_pairs={{0,16},{1,17},{2,18},{3,19},{4,20},{5,21},{6,22},{7,23},{8,24},{9,... | collective-permute-start | bytes 3145736 | tf_op jit(solution)/shard_map/ppermute | solution.py:50
  594.8 24.1 %collective-permute-start.83 = (bf16[8,512,128]{2,1,0:T(8,128)(2,1)S(1)}, bf16[8,512,128]{2,1,0:T(8,128)(2,1)S(1)}, u32[]{:S(2)}, u32[]{:S(2)}) collective-permute-start(bf16[8,512,128]{2,1,0:T(8,128)(2,1)S(1)} %copy-done.80), channel_id=1, source_target_pairs={{0,4},{1,5},{2,6},{3,7},{4,0},{5,1},{6,2},{7,3},{8,12},{9,13},{10,... | collective-permute-start | bytes 3145736 | tf_op jit(solution)/shard_map/ppermute | solution.py:50
  594.8 26.0 %collective-permute-start.85 = (bf16[8,512,128]{2,1,0:T(8,128)(2,1)S(1)}, bf16[8,512,128]{2,1,0:T(8,128)(2,1)S(1)}, u32[]{:S(2)}, u32[]{:S(2)}) collective-permute-start(bf16[8,512,128]{2,1,0:T(8,128)(2,1)S(1)} %add_convert_fusion.7), channel_id=1, source_target_pairs={{0,8},{1,9},{2,10},{3,11},{4,12},{5,13},{6,14},{7,15},{8,0},{9,1},... | collective-permute-start | bytes 3145736 | tf_op jit(solution)/shard_map/ppermute | solution.py:50
  597.3 25.6 %collective-permute-start.56 = (bf16[4,64,1024]{2,1,0:T(8,128)(2,1)S(1)}, bf16[4,64,1024]{2,1,0:T(8,128)(2,1)S(1)}, u32[]{:S(2)}, u32[]{:S(2)}) collective-permute-start(bf16[4,64,1024]{2,1,0:T(8,128)(2,1)S(1)} %slice.350), channel_id=1, source_target_pairs={{0,1},{1,0},{2,3},{3,2},{4,5},{5,4},{6,7},{7,6},{8,9},{9,8},{10,11... | collective-permute-start | bytes 1572872 | tf_op jit(solution)/shard_map/ppermute | solution.py:50
  599.7 24.6 %collective-permute-start.62 = (bf16[4,64,1024]{2,1,0:T(8,128)(2,1)S(1)}, bf16[4,64,1024]{2,1,0:T(8,128)(2,1)S(1)}, u32[]{:S(2)}, u32[]{:S(2)}) collective-permute-start(bf16[4,64,1024]{2,1,0:T(8,128)(2,1)S(1)} %slice.357), channel_id=1, source_target_pairs={{0,1},{1,0},{2,3},{3,2},{4,5},{5,4},{6,7},{7,6},{8,9},{9,8},{10,11... | collective-permute-start | bytes 1572872 | tf_op jit(solution)/shard_map/ppermute | solution.py:50
  618.9 26.0 %collective-permute-start.74 = (bf16[4,64,1024]{2,1,0:T(8,128)(2,1)S(1)}, bf16[4,64,1024]{2,1,0:T(8,128)(2,1)S(1)}, u32[]{:S(2)}, u32[]{:S(2)}) collective-permute-start(bf16[4,64,1024]{2,1,0:T(8,128)(2,1)S(1)} %slice.373), channel_id=1, source_target_pairs={{0,16},{1,17},{2,18},{3,19},{4,20},{5,21},{6,22},{7,23},{8,24},{9,... | collective-permute-start | bytes 1572872 | tf_op jit(solution)/shard_map/ppermute | solution.py:50
  620.8 27.4 %collective-permute-start.80 = (bf16[4,512,128]{2,1,0:T(8,128)(2,1)S(1)}, bf16[4,512,128]{2,1,0:T(8,128)(2,1)S(1)}, u32[]{:S(2)}, u32[]{:S(2)}) collective-permute-start(bf16[4,512,128]{2,1,0:T(8,128)(2,1)S(1)} %slice.382), channel_id=1, source_target_pairs={{0,8},{1,9},{2,10},{3,11},{4,12},{5,13},{6,14},{7,15},{8,0},{9,1},... | collective-permute-start | bytes 1572872 | tf_op jit(solution)/shard_map/ppermute | solution.py:50
  622.9 34.3 %collective-permute-start.86 = (bf16[4,512,128]{2,1,0:T(8,128)(2,1)S(1)}, bf16[4,512,128]{2,1,0:T(8,128)(2,1)S(1)}, u32[]{:S(2)}, u32[]{:S(2)}) collective-permute-start(bf16[4,512,128]{2,1,0:T(8,128)(2,1)S(1)} %slice.388), channel_id=1, source_target_pairs={{0,16},{1,17},{2,18},{3,19},{4,20},{5,21},{6,22},{7,23},{8,24},{9,... | collective-permute-start | bytes 1572872 | tf_op jit(solution)/shard_map/ppermute | solution.py:50
  632.0 24.8 %collective-permute-start.98 = (bf16[4,32,2048]{2,1,0:T(8,128)(2,1)S(1)}, bf16[4,32,2048]{2,1,0:T(8,128)(2,1)S(1)}, u32[]{:S(2)}, u32[]{:S(2)}) collective-permute-start(bf16[4,32,2048]{2,1,0:T(8,128)(2,1)S(1)} %slice.400), channel_id=1, source_target_pairs={{0,1},{1,0},{2,3},{3,2},{4,5},{5,4},{6,7},{7,6},{8,9},{9,8},{10,11... | collective-permute-start | bytes 1572872 | tf_op jit(solution)/shard_map/ppermute | solution.py:50
  648.1 27.6 %collective-permute-start.69 = (bf16[2,64,1024]{2,1,0:T(8,128)(2,1)S(1)}, bf16[2,64,1024]{2,1,0:T(8,128)(2,1)S(1)}, u32[]{:S(2)}, u32[]{:S(2)}) collective-permute-start(bf16[2,64,1024]{2,1,0:T(8,128)(2,1)S(1)} %slice.367), channel_id=1, source_target_pairs={{0,1},{1,0},{2,3},{3,2},{4,5},{5,4},{6,7},{7,6},{8,9},{9,8},{10,11... | collective-permute-start | bytes 786440 | tf_op jit(solution)/shard_map/ppermute | solution.py:50
  656.8 25.6 %collective-permute-start.75 = (bf16[2,64,1024]{2,1,0:T(8,128)(2,1)S(1)}, bf16[2,64,1024]{2,1,0:T(8,128)(2,1)S(1)}, u32[]{:S(2)}, u32[]{:S(2)}) collective-permute-start(bf16[2,64,1024]{2,1,0:T(8,128)(2,1)S(1)} %slice.375), channel_id=1, source_target_pairs={{0,1},{1,0},{2,3},{3,2},{4,5},{5,4},{6,7},{7,6},{8,9},{9,8},{10,11... | collective-permute-start | bytes 786440 | tf_op jit(solution)/shard_map/ppermute | solution.py:50
  657.2 31.9 %collective-permute-start.81 = (bf16[2,512,128]{2,1,0:T(8,128)(2,1)S(1)}, bf16[2,512,128]{2,1,0:T(8,128)(2,1)S(1)}, u32[]{:S(2)}, u32[]{:S(2)}) collective-permute-start(bf16[2,512,128]{2,1,0:T(8,128)(2,1)S(1)} %slice.384), channel_id=1, source_target_pairs={{0,1},{1,0},{2,3},{3,2},{4,5},{5,4},{6,7},{7,6},{8,9},{9,8},{10,11... | collective-permute-start | bytes 786440 | tf_op jit(solution)/shard_map/ppermute | solution.py:50
  662.1 43.8 %collective-permute-start.87 = (bf16[2,512,128]{2,1,0:T(8,128)(2,1)S(1)}, bf16[2,512,128]{2,1,0:T(8,128)(2,1)S(1)}, u32[]{:S(2)}, u32[]{:S(2)}) collective-permute-start(bf16[2,512,128]{2,1,0:T(8,128)(2,1)S(1)} %slice.390), channel_id=1, source_target_pairs={{0,1},{1,0},{2,3},{3,2},{4,5},{5,4},{6,7},{7,6},{8,9},{9,8},{10,11... | collective-permute-start | bytes 786440 | tf_op jit(solution)/shard_map/ppermute | solution.py:50
  675.7 30.1 %collective-permute-start.99 = (bf16[2,32,2048]{2,1,0:T(8,128)(2,1)S(1)}, bf16[2,32,2048]{2,1,0:T(8,128)(2,1)S(1)}, u32[]{:S(2)}, u32[]{:S(2)}) collective-permute-start(bf16[2,32,2048]{2,1,0:T(8,128)(2,1)S(1)} %slice.402), channel_id=1, source_target_pairs={{0,2},{1,3},{2,0},{3,1},{4,6},{5,7},{6,4},{7,5},{8,10},{9,11},{10,... | collective-permute-start | bytes 786440 | tf_op jit(solution)/shard_map/ppermute | solution.py:50
  682.5 26.6 %collective-permute-start.58 = (bf16[1,64,1024]{2,1,0:T(8,128)(2,1)S(1)}, bf16[1,64,1024]{2,1,0:T(8,128)(2,1)S(1)}, u32[]{:S(2)}, u32[]{:S(2)}) collective-permute-start(bf16[1,64,1024]{2,1,0:T(8,128)(2,1)S(1)} %slice.354), channel_id=1, source_target_pairs={{0,16},{1,17},{2,18},{3,19},{4,20},{5,21},{6,22},{7,23},{8,24},{9,... | collective-permute-start | bytes 393224 | tf_op jit(solution)/shard_map/ppermute | solution.py:50
  (187 other events, 2379.7 us)

commit v2 on v1

v2 whole, which is shorter than its diff:
```python
import functools

import jax
import jax.numpy as jnp
from jax import lax
from jax.experimental import pallas as pl
from jax.experimental.pallas import tpu as pltpu
from jax.sharding import PartitionSpec as P

NH = 8
STEP = 5
AXES = ("grp", "hd")

MIB = 1 << 20
F32, LOW = jnp.float32, jnp.bfloat16
VMEM = pl.BlockSpec(memory_space=pltpu.VMEM)
SMEM = pl.BlockSpec(memory_space=pltpu.SMEM)


ANY = pl.BlockSpec(memory_space=pl.ANY)


def adamw(weight, grad, first_old, second_old, learn_rate, decay):
    first_new = 0.5 * first_old + 0.5 * grad
    second_new = 0.5 * second_old + 0.5 * grad * grad
    correction = 1.0 - 0.5**STEP
    normed_step = first_new / correction / (jnp.sqrt(second_new / correction) + 1e-08)
    return (first_new, second_new, weight - learn_rate * (normed_step + decay * weight))


def log2(n):
    return n.bit_length() - 1


def outer_bits(groups, depth):
    first, last = log2(depth) + 1, log2(depth) + log2(groups)
    middle = (first + last) // 2
    return list(range(first, middle)), list(range(middle, last))


def swap(block, bit, total):
    return lax.ppermute(block, AXES, [(j, j ^ (1 << bit)) for j in range(total)])


def spread_of(order, core, total):
    bits = list(order) + [core]
    return tuple(sum(((p >> t) & 1) << b for t, b in enumerate(bits)) for p in range(total))


def added(a, b):
    return (a.astype(F32) + b.astype(F32)).astype(LOW)


def device_index():
    return lax.axis_index("grp") * lax.axis_size("hd") + lax.axis_index("hd")


def gather_steps(shard, order, core, total):
    held = shard
    for bit in order[:-1]:
        (came,) = yield [functools.partial(swap, held, bit, total)]
        held = jnp.concatenate([held, came], axis=0)
    (came,) = yield [functools.partial(swap, held, order[-1], total)]
    first, second = yield [functools.partial(swap, held, core, total), functools.partial(swap, came, core, total)]
    return [held, came, first, second]


def scatter_steps(mine, theirs, x_bit, y_bit, core, total):
    (came,) = yield [functools.partial(swap, theirs, core, total)]
    half = mine.shape[1] // 2
    away = [added(mine[k, half:], came[k, half:]) for k in range(2)]
    held = [added(mine[k, :half], came[k, :half]) for k in range(2)]
    came = yield [functools.partial(swap, block, bit, total) for block, bit in zip(away, (y_bit, x_bit))]
    half //= 2
    away = [added(held[k][half:], came[k][half:]) for k in range(2)]
    held = [added(held[k][:half], came[k][:half]) for k in range(2)]
    came = yield [functools.partial(swap, block, bit, total) for block, bit in zip(away, (x_bit, y_bit))]
    both = jnp.stack([added(held[k], came[k]) for k in range(2)], axis=1)
    (came,) = yield [functools.partial(lax.all_to_all, both, "hd", 0, 0, tiled=True)]
    return jnp.sum(came.astype(F32), axis=0)


class Chain:
    def __init__(self, steps):
        self.steps, self.result, self.under_way = steps, None, None
        self.wanted = next(steps)

    def start(self):
        if self.under_way is None:
            self.under_way = [exchange() for exchange in self.wanted]

    def advance(self, came):
        self.under_way = None
        try:
            self.wanted = self.steps.send(came)
        except StopIteration as stop:
            self.wanted, self.result = [], stop.value


def in_round(chains, compute=None, *beside, longer=()):
    chains = [chain for chain in chains if chain.wanted]
    for chain in chains:
        chain.start()
    ending = [chain for chain in chains if chain not in longer]
    done = compute() if compute else ()
    came, done, beside = lax.optimization_barrier(([chain.under_way for chain in ending], done, beside))
    for chain, blocks in zip(ending, came):
        chain.advance(blocks)
    return beside[0] if beside else done


def place_blocks(refs, spread, dst, rows, sem):
    if spread is None:
        pltpu.make_async_copy(refs[0].at[:, rows], dst, sem).start()
        return
    me, each = device_index(), len(spread) // 4
    for p, mask in enumerate(spread):
        pltpu.make_async_copy(refs[p // each].at[p % each, rows], dst.at[me ^ mask], sem).start()


def cut_blocks(halves, refs, depth, sems, masks=range(32)):
    me = device_index()
    for mask in masks:
        owner = me ^ mask
        place = mask // (2 * depth)
        for half, src_of, rows in halves:
            group = place if half == 0 else place // 2 + place % 2 * 2
            dst = refs[mask // depth % 2].at[half, group * depth + (owner & (depth - 1))]
            dst = dst if rows is None else dst.at[rows]
            pltpu.make_async_copy(src_of(owner), dst, sems.at[mask // depth % 2]).start()


def await_whole(refs, sems):
    for at, ref in enumerate(refs):
        pltpu.make_async_copy(ref, ref, sems.at[at]).wait()


def blocks_of(shape):
    return [jax.ShapeDtypeStruct((2, 16, *shape), LOW)] * 2


BLOCK = 512
PARTS = 4
CALLS = 2


def pack_kernel(attn_in, attn_out, w_out, w_in, cross, own, cross_out, own_out, mlp):
    rows = attn_in.shape[1]
    for at, (to, to_out) in enumerate(((cross, cross_out), (own, own_out))):
        for m in range(3):
            to[0, m * rows : (m + 1) * rows, :] = attn_in[3 * at + m].astype(LOW)
        to_out[0] = attn_out[at].astype(LOW)
    width = w_out.shape[1] // PARTS
    for c in range(PARTS):
        mlp[c * rows : (c + 1) * rows, :] = w_out[:, c * width : (c + 1) * width].astype(LOW)
    mlp[PARTS * rows :, :] = w_in[...].T.astype(LOW)


def pack(attn_in_t, attn_out_t, w_out_t, w_in):
    rows, width = attn_in_t.shape[1:]
    return pl.pallas_call(
        pack_kernel,
        out_shape=[jax.ShapeDtypeStruct((1, 3 * rows, width), LOW)] * 2
        + [jax.ShapeDtypeStruct((1, rows, width), LOW)] * 2
        + [jax.ShapeDtypeStruct((PARTS * rows + w_in.shape[1], width), LOW)],
        in_specs=[VMEM] * 4,
        out_specs=[VMEM] * 5,
        compiler_params=pltpu.CompilerParams(vmem_limit_bytes=16 * MIB),
    )(attn_in_t, attn_out_t, w_out_t, w_in)


def from_all(own):
    total = lax.axis_size("grp") * lax.axis_size("hd")
    return lax.all_to_all(jnp.broadcast_to(own[None], (total, *own.shape)), AXES, 0, 0, tiled=True)


def gather_gains(gains):
    rows = gains.shape[0]
    every = from_all(gains.astype(LOW).reshape(-1)).astype(F32)
    return jnp.swapaxes(every.reshape(every.shape[0], rows, -1), 0, 1).reshape(rows, -1)


def scatter_gains(grads):
    total = lax.axis_size("grp") * lax.axis_size("hd")
    rows = grads.shape[0]
    blocks = jnp.swapaxes(grads.reshape(rows, total, -1), 0, 1).reshape(total, -1)
    came = lax.all_to_all(blocks, AXES, 0, 0, tiled=True)
    return jnp.sum(came, axis=0).reshape(rows, -1)


def dot_nn(a, b):
    return lax.dot_general(a, b, (((1,), (0,)), ((), ())), preferred_element_type=F32)


def dot_nt(a, b):
    return lax.dot_general(a, b, (((1,), (1,)), ((), ())), preferred_element_type=F32)


def dot_tn(a, b):
    return lax.dot_general(a, b, (((0,), (0,)), ((), ())), preferred_element_type=F32)


def unit_rows(rows):
    inverse = lax.rsqrt(jnp.mean(rows * rows, axis=-1, keepdims=True) + 1e-06)
    return rows * inverse, inverse


def norm_grad(rows, gain, upstream):
    unit, inverse = unit_rows(rows)
    scaled = upstream * gain
    inner = jnp.mean(scaled * unit, axis=-1, keepdims=True)
    return (scaled - unit * inner) * inverse, jnp.sum(upstream * unit, axis=0, keepdims=True)


def head_scores(query, key, count, scale):
    scores = dot_nt(query, key) * scale
    if count is not None:
        place = lax.broadcasted_iota(jnp.int32, scores.shape, 1)
        scores = jnp.where(place < count, scores, -1e30)
    return scores


def matrix(weights):
    return weights[...].reshape(-1, weights.shape[2])


def attend_kernel(cross, images, size, spreads, *refs):
    if cross:
        counts, gains, source, target, *refs = refs
    else:
        gains, target, *refs = refs
        counts, source = None, target
    *pieces, q_out, k_out, v_out, context_out, sum_out, log_out, whole, weights, sems, out_sem = refs
    rows = weights.shape[2]
    count = len(pieces) // 2
    for m in (1, 2, 0):
        place_blocks(pieces[:count], spreads[0], weights.at[m], pl.ds(m * rows, rows), sems.at[m])
    place_blocks(pieces[count:], spreads[1], weights.at[3], slice(None), sems.at[3])

    def arrived(m):
        pltpu.make_async_copy(weights.at[m], weights.at[m], sems.at[m]).wait()
        return matrix(weights.at[m])

    key_gain, query_gain = (0, 1) if cross else (2, 2)
    rows = source[...].astype(F32)
    normal = (unit_rows(rows)[0] * gains[key_gain : key_gain + 1, :]).astype(LOW)
    k_out[...] = dot_nt(normal, arrived(1)).astype(LOW)
    v_out[...] = dot_nt(normal, arrived(2)).astype(LOW)
    if cross:
        rows = target[...].astype(F32)
        normal = (unit_rows(rows)[0] * gains[query_gain : query_gain + 1, :]).astype(LOW)
    q_out[...] = dot_nt(normal, arrived(0)).astype(LOW)
    out_weights = arrived(3)
    keep = pltpu.make_async_copy(weights, whole, out_sem)
    keep.start()
    width = q_out.shape[1] // NH
    scale = width ** (-0.5)

    def one_image(image, carry):
        span = pl.ds(pl.multiple_of(image * size, size), size)
        count = counts[image] if cross else None
        for h in range(NH):
            part = slice(h * width, (h + 1) * width)
            scores = head_scores(q_out[span, part], k_out[span, part], count, scale)
            highest = jnp.max(scores, axis=-1, keepdims=True)
            exponent = jnp.exp(scores - highest)
            row_total = jnp.sum(exponent, axis=-1, keepdims=True)
            probs = (exponent * (1.0 / row_total)).astype(LOW)
            context_out[span, part] = dot_nn(probs, v_out[span, part]).astype(LOW)
            log_out[span, h : h + 1] = highest + jnp.log(row_total)
        return carry

    lax.fori_loop(0, images, one_image, 0)
    sum_out[...] = target[...].astype(F32) + dot_nt(context_out[...], out_weights)
    keep.wait()


def attend_block(gains, source, target, counts, pieces, spreads, images):
    cross = source is not None
    rows, width = target.shape
    low = jax.ShapeDtypeStruct((rows, width), LOW)
    weights = (4, 32, width // 32, width)
    head = (counts, gains, source, target) if cross else (gains, target)
    return pl.pallas_call(
        functools.partial(attend_kernel, cross, images, rows // images, spreads),
        out_shape=[low] * 4
        + [jax.ShapeDtypeStruct(shape, F32) for shape in ((rows, width), (rows, NH))]
        + [jax.ShapeDtypeStruct(weights, LOW)],
        in_specs=([SMEM] if cross else []) + [VMEM] * (3 if cross else 2) + [ANY] * len(pieces),
        out_specs=[VMEM] * 6 + [ANY],
        scratch_shapes=[pltpu.VMEM(weights, LOW), pltpu.SemaphoreType.DMA((4,)), pltpu.SemaphoreType.DMA],
        compiler_params=pltpu.CompilerParams(vmem_limit_bytes=48 * MIB),
        cost_estimate=pl.CostEstimate(
            flops=8 * rows * width * width + 4 * rows * width * (rows // images),
            bytes_accessed=12 * rows * width + 8 * width * width,
            transcendentals=rows * NH * (rows // images),
        ),
    )(*head, *pieces)


def fetch(whole, members, scratch, sems):
    copies = []
    for at, (m, to) in enumerate(zip(members, scratch)):
        copies.append(pltpu.make_async_copy(whole.at[m], to, sems.at[at]))
        copies[-1].start()
    return copies


def scores_grad_kernel(cross, images, size, *refs):
    if cross:
        counts, *refs = refs
    (upstream, q_in, k_in, v_in, context_in, log_in, whole, dq, dk, dv, dc, wo_v, sems) = refs
    (copy,) = fetch(whole, (3,), (wo_v,), sems)
    up_low = upstream[...].astype(LOW)
    copy.wait()
    dc[...] = dot_nn(up_low, matrix(wo_v)).astype(LOW)
    width = q_in.shape[1] // NH
    scale = width ** (-0.5)

    def one_image(image, carry):
        span = pl.ds(pl.multiple_of(image * size, size), size)
        count = counts[image] if cross else None
        for h in range(NH):
            part = slice(h * width, (h + 1) * width)
            query, key, value, grad = q_in[span, part], k_in[span, part], v_in[span, part], dc[span, part]
            probs = jnp.exp(head_scores(query, key, count, scale) - log_in[span, h : h + 1])
            prob_grad = dot_nt(grad, value)
            dv[span, part] = dot_tn(probs.astype(LOW), grad).astype(LOW)
            inner = jnp.sum(grad.astype(F32) * context_in[span, part].astype(F32), axis=-1, keepdims=True)
            score_grad = probs * (prob_grad - inner)
            score_grad = score_grad.astype(LOW)
            dq[span, part] = (dot_nn(score_grad, key) * scale).astype(LOW)
            dk[span, part] = (dot_tn(score_grad, query) * scale).astype(LOW)
        return carry

    lax.fori_loop(0, images, one_image, 0)


def scores_grad(counts, upstream, saved, whole, images):
    cross = counts is not None
    rows, width = upstream.shape
    return pl.pallas_call(
        functools.partial(scores_grad_kernel, cross, images, rows // images),
        out_shape=[jax.ShapeDtypeStruct((rows, width), LOW)] * 3,
        in_specs=([SMEM] if cross else []) + [VMEM] * 6 + [ANY],
        out_specs=[VMEM] * 3,
        scratch_shapes=[
            pltpu.VMEM((rows, width), LOW),
            pltpu.VMEM(whole.shape[1:], LOW),
            pltpu.SemaphoreType.DMA((1,)),
        ],
        compiler_params=pltpu.CompilerParams(vmem_limit_bytes=48 * MIB),
        cost_estimate=pl.CostEstimate(
            flops=2 * rows * width * width + 10 * rows * width * (rows // images),
            bytes_accessed=18 * rows * width + 4 * width * width,
            transcendentals=rows * NH * (rows // images),
        ),
    )(*([counts] if cross else []), upstream, *saved, whole)


def matrix_shares(count, rows):
    shares = []
    for m in range(count // 2 * 2):
        shares.append((m % 2, m, 0, rows, m // 2 * rows))
    if count % 2:
        for half in range(2):
            shares.append((half, count - 1, half * rows // 2, rows // 2, count // 2 * rows))
    return shares


def matrix_blocks(sums, count, rows):
    parts = [[] for _ in range(count)]
    for half, m, _, length, at in matrix_shares(count, rows):
        parts[m].append(sums[half, at : at + length])
    return [part[0] if len(part) == 1 else jnp.concatenate(part, axis=0) for part in parts]


def matrix_grad_kernel(cross, depth, *refs):
    if cross:
        gains, source, target, *refs = refs
    else:
        gains, target, *refs = refs
    upstream, context, dq, dk, dv, *refs = refs
    *outs, grads, sems = refs
    key_gain, query_gain = (0, 1) if cross else (2, 2)
    width = target.shape[1]

    def finish(m, grad):
        grads[m] = grad.astype(LOW)
        if depth is None:
            pltpu.make_async_copy(grads.at[m], outs[m], sems.at[m]).start()
            return
        rows = width // 32

        def part(first, count):
            return lambda owner: grads.at[m, pl.ds(pl.multiple_of(owner * rows + first, count), count), :]

        halves = [
            (half, part(first, count), pl.ds(at, count)) for half, m_at, first, count, at in matrix_shares(grads.shape[0], rows) if m_at == m
        ]
        cut_blocks(halves, outs, depth, sems)

    rows = target[...].astype(F32)
    normal = (unit_rows(rows)[0] * gains[query_gain : query_gain + 1, :]).astype(LOW)
    finish(0, dot_tn(dq[...], normal))
    if cross:
        rows = source[...].astype(F32)
        normal = (unit_rows(rows)[0] * gains[key_gain : key_gain + 1, :]).astype(LOW)
    finish(1, dot_tn(dk[...], normal))
    finish(2, dot_tn(dv[...], normal))
    finish(3, dot_tn(upstream[...].astype(LOW), context[...]))
    await_whole(outs, sems)


def matrix_grads(gains, source, target, upstream, context, score_grads, depth):
    cross = source is not None
    rows, width = target.shape
    head = (gains, source, target) if cross else (gains, target)
    count = 4
    if depth is None:
        out_shape = [jax.ShapeDtypeStruct((width, width), LOW)] * count
    else:
        out_shape = blocks_of((count * width // 64, width))
    return pl.pallas_call(
        functools.partial(matrix_grad_kernel, cross, depth),
        out_shape=out_shape,
        in_specs=[VMEM] * (len(head) + 5),
        out_specs=[ANY] * len(out_shape),
        scratch_shapes=[pltpu.VMEM((count, width, width), LOW), pltpu.SemaphoreType.DMA((len(out_shape),))],
        compiler_params=pltpu.CompilerParams(vmem_limit_bytes=48 * MIB),
        cost_estimate=pl.CostEstimate(
            flops=2 * count * rows * width * width,
            bytes_accessed=16 * rows * width + 2 * count * width * width,
            transcendentals=rows,
        ),
    )(*head, upstream, context, *score_grads)


def project_grad_kernel(cross, *refs):
    if cross:
        gains, source, target, *refs = refs
    else:
        gains, target, *refs = refs
    (upstream, dq, dk, dv, whole, *refs) = refs
    outs = 2 if cross else 1
    grads_out, gain_outs = refs[:outs], refs[outs : 2 * outs]
    (wq_v, wk_v, wv_v, sems) = refs[2 * outs :]
    copies = fetch(whole, (0, 1, 2), (wq_v, wk_v, wv_v), sems)
    key_gain, query_gain = (0, 1) if cross else (2, 2)
    rows = target[...].astype(F32)
    gain = gains[query_gain : query_gain + 1, :]
    copies[0].wait()
    back = dot_nn(dq[...], matrix(wq_v))
    copies[1].wait()
    copies[2].wait()
    if cross:
        extra, gain_grad = norm_grad(rows, gain, back)
        grads_out[0][...] = upstream[...] + extra
        gain_outs[0][...] = gain_grad
        rows = source[...].astype(F32)
        gain = gains[key_gain : key_gain + 1, :]
        back = dot_nn(dk[...], matrix(wk_v))
    else:
        back += dot_nn(dk[...], matrix(wk_v))
    back += dot_nn(dv[...], matrix(wv_v))
    extra, gain_grad = norm_grad(rows, gain, back)
    if cross:
        grads_out[1][...] = extra
    else:
        grads_out[0][...] = upstream[...] + extra
    gain_outs[-1][...] = gain_grad


def project_grad(gains, source, target, upstream, score_grads, whole):
    cross = source is not None
    rows, width = target.shape
    outs = 2 if cross else 1
    head = (gains, source, target) if cross else (gains, target)
    result = pl.pallas_call(
        functools.partial(project_grad_kernel, cross),
        out_shape=[jax.ShapeDtypeStruct((rows, width), F32)] * outs + [jax.ShapeDtypeStruct((1, width), F32)] * outs,
        in_specs=[VMEM] * (len(head) + 4) + [ANY],
        out_specs=[VMEM] * (2 * outs),
        scratch_shapes=[pltpu.VMEM(whole.shape[1:], LOW)] * 3
        + [pltpu.SemaphoreType.DMA((3,))],
        compiler_params=pltpu.CompilerParams(vmem_limit_bytes=48 * MIB),
        cost_estimate=pl.CostEstimate(
            flops=6 * rows * width * width, bytes_accessed=20 * rows * width + 6 * width * width, transcendentals=rows
        ),
    )(*head, upstream, *score_grads, whole)
    return result[:outs], result[outs:]


def fetch_bands(bands, copies, sems):
    for at, (first, to) in enumerate(copies):
        pltpu.make_async_copy(bands.at[:, pl.ds(first, to.shape[1])], to, sems.at[at]).start()

    def wait():
        for at, (_, to) in enumerate(copies):
            pltpu.make_async_copy(to, to, sems.at[at]).wait()

    return wait


def mlp_forward_kernel(call, depth, second, cotangent, *refs):
    if call == 0:
        gain_row, bands, normal, partial, hidden_grad, *refs = refs
    else:
        normal, skip, bands, out, hidden_grad, *refs = refs
    *outs, cot_t, total, lower_v, lift_v, grad_v, sems, send_sems = refs
    step = pl.program_id(0)
    parts, last_step = PARTS // CALLS, pl.num_programs(0) - 1

    @pl.when(step == 0)
    def first():
        rows = lower_v.shape[2]
        copies = [((call * parts + c) * rows, lower_v.at[c]) for c in range(parts)]
        wait = fetch_bands(bands, copies, sems)
        count, units = lift_v.shape[:2]
        lift = pltpu.make_async_copy(
            bands.at[pl.ds(call * count, count), pl.ds(PARTS * rows, units)], lift_v, sems.at[parts]
        )
        lift.start()
        if call == 0:
            normal[...] = (unit_rows(second[...])[0] * gain_row[...]).astype(LOW)
        cot_t[...] = cotangent[...].T
        total[...] = second[...]
        lift.wait()
        wait()

    units = lift_v.shape[1]
    lift = lift_v[pl.ds(step * (BLOCK // units), BLOCK // units)].reshape(BLOCK, -1)
    share = lower_v.shape[3] // BLOCK
    span = pl.ds(pl.multiple_of(step % share * BLOCK, BLOCK), BLOCK)
    lower = lower_v[step // share, :, :, span].reshape(-1, BLOCK)
    hidden = dot_nt(normal[...], lift)
    square = hidden * hidden
    root = 0.7978845608028654
    tanh = jnp.tanh(root * hidden * (1.0 + 0.044715 * square))
    half = 0.5 * (1.0 + tanh)
    active = (hidden * half).astype(LOW)
    slope = half + 0.5 * hidden * (1.0 - tanh * tanh) * (root * (1.0 + 3 * 0.044715 * square))
    grad_v[:, pl.ds(pl.multiple_of(step * BLOCK, BLOCK), BLOCK)] = dot_nn(cot_t[...], active).astype(LOW)
    total[...] += dot_nt(active, lower)
    hidden_grad[...] = (dot_nn(cotangent[...], lower) * slope).astype(LOW)

    for half in range(2):
        size = grad_v.shape[1] // 2

        @pl.when(step == (half + 1) * size // BLOCK - 1)
        def send():
            columns = pl.ds(half * size, size)
            if depth is None:
                pltpu.make_async_copy(grad_v.at[:, columns], outs[0].at[:, columns], send_sems.at[0]).start()
                return
            rows = grad_v.shape[0] // 32
            src_of = lambda owner: grad_v.at[pl.ds(pl.multiple_of(owner * rows, rows), rows), columns]
            cut_blocks([(half, src_of, None)], outs, depth, send_sems)

    @pl.when(step == last_step)
    def last():
        if call == 0:
            partial[...] = total[...]
        else:
            out[...] = (total[...] + skip[...].astype(F32)).astype(LOW)
        await_whole(outs, send_sems)


def mlp_forward(call, second, cotangent, others, bands, hidden, depth):
    rows, width = second.shape
    units, parts = hidden // CALLS, PARTS // CALLS
    whole = lambda shape: pl.BlockSpec(shape, lambda f: (0, 0), pipeline_mode=pl.Buffered(1))
    once = lambda shape: pl.BlockSpec(shape, lambda f: (0, 0))
    low = jax.ShapeDtypeStruct((rows, width), LOW)
    if depth is None:
        outs = [jax.ShapeDtypeStruct((width, units), LOW)]
    else:
        outs = blocks_of((width // 32, units // 2))
    return pl.pallas_call(
        functools.partial(mlp_forward_kernel, call, depth),
        grid=(units // BLOCK,),
        out_shape=[low]
        + [jax.ShapeDtypeStruct((rows, width), F32)] * (call == 0)
        + [jax.ShapeDtypeStruct((rows, units), LOW)]
        + outs,
        in_specs=[whole((rows, width))] * 2 + [whole(other.shape) for other in others] + [ANY],
        out_specs=[once((rows, width))] * (2 if call == 0 else 1)
        + [pl.BlockSpec((rows, BLOCK), lambda f: (0, f))]
        + [ANY] * len(outs),
        scratch_shapes=[
            pltpu.VMEM((width, rows), LOW),
            pltpu.VMEM((rows, width), F32),
            pltpu.VMEM((parts, 32, width // 32, units // parts), LOW),
            pltpu.VMEM((32 // CALLS, hidden // 32, width), LOW),
            pltpu.VMEM((width, units), LOW),
            pltpu.SemaphoreType.DMA((parts + 1,)),
            pltpu.SemaphoreType.DMA((len(outs),)),
        ],
        compiler_params=pltpu.CompilerParams(vmem_limit_bytes=56 * MIB),
        cost_estimate=pl.CostEstimate(
            flops=8 * rows * width * units,
            bytes_accessed=6 * width * units + 12 * rows * width + 2 * rows * units,
            transcendentals=rows * units,
        ),
    )(second, cotangent, *others, bands)


def mlp_backward_kernel(depth, gain_row, second, cotangent, normal, hidden_grad0, hidden_grad1, bands, *refs):
    second_grad, gain_grad, *refs = refs
    *outs, normal_t, back, lift_v, grad_v, sem, send_sems = refs
    step = pl.program_id(0)
    steps = pl.num_programs(0)

    @pl.when(step == 0)
    def first():
        units = lift_v.shape[1]
        lift = pltpu.make_async_copy(bands.at[:, pl.ds(bands.shape[1] - units, units)], lift_v, sem)
        lift.start()
        normal_t[...] = normal[...].T
        back[...] = jnp.zeros_like(back)
        lift.wait()

    units = lift_v.shape[1]
    share = BLOCK // units
    lift = lift_v[pl.ds(step * share, share)].reshape(BLOCK, -1)
    hidden_grad = jnp.where(step < steps // 2, hidden_grad0[...], hidden_grad1[...])
    grad_v[step] = dot_nn(normal_t[...], hidden_grad).astype(LOW)
    back[...] += dot_nn(hidden_grad, lift)

    if depth is None:
        start = pl.multiple_of(step * BLOCK, BLOCK)
        pltpu.make_async_copy(grad_v.at[step], outs[0].at[:, pl.ds(start, BLOCK)], send_sems.at[0]).start()
    else:
        me = device_index()
        for group in range(32 // share):

            @pl.when(step == (me // share) ^ group)
            def send():
                size = grad_v.shape[1] // 2

                def part(half):
                    return lambda owner: grad_v.at[
                        step, pl.ds(half * size, size), pl.ds(pl.multiple_of(owner % share * units, units), units)
                    ]

                halves = [(half, part(half), None) for half in range(2)]
                cut_blocks(halves, outs, depth, send_sems, range(group * share, (group + 1) * share))

    @pl.when(step == steps - 1)
    def last():
        extra, gains = norm_grad(second[...], gain_row[...], back[...])
        second_grad[...] = cotangent[...].astype(F32) + extra
        gain_grad[...] = gains
        await_whole(outs, send_sems)


def mlp_backward(gain_row, second, cotangent, normal, hidden_grads, bands, hidden, depth):
    rows, width = second.shape
    whole = lambda shape: pl.BlockSpec(shape, lambda f: (0, 0), pipeline_mode=pl.Buffered(1))
    once = lambda shape: pl.BlockSpec(shape, lambda f: (0, 0))
    half = hidden // BLOCK // 2
    if depth is None:
        outs = [jax.ShapeDtypeStruct((width, hidden), LOW)]
    else:
        outs = blocks_of((width // 2, hidden // 32))
    return pl.pallas_call(
        functools.partial(mlp_backward_kernel, depth),
        grid=(hidden // BLOCK,),
        out_shape=[jax.ShapeDtypeStruct((rows, width), F32), jax.ShapeDtypeStruct((1, width), F32)] + outs,
        in_specs=[whole((1, width))]
        + [whole((rows, width))] * 3
        + [
            pl.BlockSpec((rows, BLOCK), lambda f: (0, jnp.minimum(f, half - 1))),
            pl.BlockSpec((rows, BLOCK), lambda f: (0, jnp.maximum(f - half, 0))),
            ANY,
        ],
        out_specs=[once((rows, width)), once((1, width))] + [ANY] * len(outs),
        scratch_shapes=[
            pltpu.VMEM((width, rows), LOW),
            pltpu.VMEM((rows, width), F32),
            pltpu.VMEM((32, hidden // 32, width), LOW),
            pltpu.VMEM((hidden // BLOCK, width, BLOCK), LOW),
            pltpu.SemaphoreType.DMA,
            pltpu.SemaphoreType.DMA((len(outs),)),
        ],
        compiler_params=pltpu.CompilerParams(vmem_limit_bytes=56 * MIB),
        cost_estimate=pl.CostEstimate(
            flops=4 * rows * width * hidden,
            bytes_accessed=4 * width * hidden + 12 * rows * width + 2 * rows * hidden,
            transcendentals=0,
        ),
    )(gain_row, second, cotangent, normal, *hidden_grads, bands)


def local(
    pixels,
    latents,
    skip,
    counts,
    cotangent,
    attn_in,
    attn_out,
    w_in,
    w_out,
    gains,
    attn_in_first,
    attn_in_second,
    attn_out_first,
    attn_out_second,
    w_in_first,
    w_in_second,
    w_out_first,
    w_out_second,
    gains_first,
    gains_second,
):
    groups, depth = lax.axis_size("grp"), lax.axis_size("hd")
    total, core = groups * depth, log2(depth)
    fast = total == 32 and depth == 4
    images, size, width = latents.shape
    hidden = w_out.shape[0]
    flat = lambda rows: rows.reshape(-1, width)
    whole = lambda rows: rows.reshape(images, -1, width)
    pixel_rows, latent_rows, cot_rows = flat(pixels), flat(latents), flat(cotangent)
    attn_in_t, attn_out_t, w_out_t = jnp.swapaxes(attn_in, 1, 2), jnp.swapaxes(attn_out, 1, 2), w_out.T
    own_counts = lax.dynamic_slice_in_dim(counts, lax.axis_index("hd") * images, images)
    cut = depth if fast else None

    def cross_forward(pieces, spreads):
        return attend_block(gain_rows, pixel_rows, latent_rows, own_counts, pieces, spreads, images)

    def self_forward(pieces, spreads):
        return attend_block(gain_rows, None, first_sum, None, pieces, spreads, images)

    if fast:
        (x_bit,), (y_bit,) = outer_bits(groups, depth)
        *shards, mlp_shard = pack(attn_in_t, attn_out_t, w_out_t, w_in)
        orders = ((1, 0, x_bit, y_bit), (1, 0, y_bit, x_bit), (x_bit, y_bit, 1, 0), (y_bit, x_bit, 1, 0))
        spreads = [spread_of(order, core, total) for order in orders]
        chains = [Chain(gather_steps(shard, order, core, total)) for shard, order in zip(shards, orders)]
        in_round(chains)
        mlp_shard = in_round(chains, None, mlp_shard)
        bands = lax.all_gather(mlp_shard, AXES, axis=0)
        gain_rows = in_round(chains, lambda: gather_gains(gains))
        while any(chain.wanted for chain in chains):
            in_round(chains)
        *saved, first_sum, logs, weights = cross_forward(chains[0].result + chains[2].result, spreads[::2])
        *saved2, second_sum, logs2, weights2 = self_forward(chains[1].result + chains[3].result, spreads[1::2])
    else:
        every = lambda shard: lax.all_gather(shard.astype(LOW), AXES, axis=0, tiled=True).reshape(32, -1, shard.shape[1])
        inward = lambda m: jnp.concatenate([every(attn_in_t[3 * m + k]) for k in range(3)], axis=1)
        gain_rows = gather_gains(gains)
        lower = every(w_out_t)
        lift = lax.all_gather(w_in.astype(LOW), AXES, axis=1, tiled=True).T.reshape(32, -1, width)
        bands = jnp.concatenate([*jnp.split(lower, PARTS, axis=2), lift], axis=1)
        *saved, first_sum, logs, weights = cross_forward([inward(0), every(attn_out_t[0])], (None, None))
        *saved2, second_sum, logs2, weights2 = self_forward([inward(1), every(attn_out_t[1])], (None, None))

    normal, partial, hidden_grad0, *lower_grad0 = mlp_forward(
        0, second_sum, cot_rows, (gain_rows[3:],), bands, hidden, cut
    )

    def mlp_second():
        return mlp_forward(1, partial, cot_rows, (normal, flat(skip)), bands, hidden, cut)

    def mlp_back():
        return mlp_backward(
            gain_rows[3:], second_sum, cot_rows, normal, (hidden_grad0, hidden_grad1), bands, hidden, cut
        )

    def self_scores():
        return scores_grad(None, second_grad, (*saved2, logs2), weights2, images)

    def self_matrices():
        return matrix_grads(gain_rows, None, first_sum, second_grad, saved2[3], score_grads2, cut)

    def self_project():
        return project_grad(gain_rows, None, first_sum, second_grad, score_grads2, weights2)

    def cross_scores():
        return scores_grad(own_counts, first_grad, (*saved, logs), weights, images)

    def cross_matrices():
        return matrix_grads(gain_rows, pixel_rows, latent_rows, first_grad, saved[3], score_grads, cut)

    def cross_project():
        return project_grad(gain_rows, pixel_rows, latent_rows, first_grad, score_grads, weights)

    if fast:
        scatter = lambda blocks: Chain(scatter_steps(*blocks, x_bit, y_bit, core, total))
        live = [scatter(lower_grad0)]
        latents_out, hidden_grad1, *lower_grad1 = in_round(live, mlp_second)
        live.append(scatter(lower_grad1))
        second_grad, gain3_grad, *lift_grad = in_round(live, mlp_back)
        live.append(scatter(lift_grad))
        score_grads2 = in_round(live, self_scores)
        live.append(scatter(in_round(live, self_matrices)))
        (first_grad,), (gain2_grad,) = in_round(live, self_project)
        score_grads = in_round(live, cross_scores)
        live.append(scatter(in_round(live, cross_matrices)))
        in_round(live, longer=live[:4])
        (latents_grad, pixels_grad), (gain1_grad, gain0_grad) = in_round(live, cross_project)
        gains_grad = jnp.concatenate([gain0_grad, gain1_grad, gain2_grad, gain3_grad], axis=0)
        gains_sum = scatter_gains(gains_grad)
        while any(chain.wanted for chain in live):
            in_round(live)
        lower0, lower1, lift_sum, own, cross = [chain.result for chain in live]
        lower_sum = jnp.concatenate([*lower0, *lower1], axis=1)
        lift_sum = jnp.concatenate([*lift_sum], axis=0)
        sums, sums2 = [matrix_blocks(block, 4, attn_in.shape[2]) for block in (cross, own)]
    else:
        latents_out, hidden_grad1, lower_grad1 = mlp_second()
        second_grad, gain3_grad, lift_grad = mlp_back()
        score_grads2 = self_scores()
        grads2 = self_matrices()
        (first_grad,), (gain2_grad,) = self_project()
        score_grads = cross_scores()
        grads = cross_matrices()
        (latents_grad, pixels_grad), (gain1_grad, gain0_grad) = cross_project()
        gains_grad = jnp.concatenate([gain0_grad, gain1_grad, gain2_grad, gain3_grad], axis=0)
        gains_sum = scatter_gains(gains_grad)
        sum_of = lambda grad, along: lax.psum_scatter(grad, AXES, scatter_dimension=along, tiled=True)
        sums = [sum_of(g, 0) for g in grads]
        sums2 = [sum_of(g, 0) for g in grads2]
        lift_sum = sum_of(lift_grad, 1)
        lower_sum = sum_of(jnp.concatenate([*lower_grad0, lower_grad1], axis=1), 0)
    mixing_sum = jnp.swapaxes(jnp.stack([*sums[:3], *sums2[:3]]), 1, 2).astype(F32)
    outward_sum = jnp.swapaxes(jnp.stack([sums[3], sums2[3]]), 1, 2).astype(F32)
    mix = adamw(attn_in, mixing_sum, attn_in_first, attn_in_second, 0.05, 0.1)
    out = adamw(attn_out, outward_sum, attn_out_first, attn_out_second, 0.3, 0.1)
    lift_new = adamw(w_in, lift_sum.astype(F32), w_in_first, w_in_second, 0.05, 0.1)
    lower_new = adamw(w_out, lower_sum.T.astype(F32), w_out_first, w_out_second, 0.03, 0.1)
    gain_first, gain_second, gain_new = adamw(
        gains, gains_sum, gains_first, gains_second, 0.4, 0.0
    )
    return (
        whole(latents_out),
        whole(pixels_grad),
        whole(latents_grad),
        *mix,
        *out,
        *lift_new,
        *lower_new,
        gain_first,
        gain_second[:3],
        gain_second[3],
        gain_new,
    )


def solution(mesh):
    return jax.shard_map(
        local,
        mesh=mesh,
        in_specs=(
            P(("grp", "hd"), None, None),
            P(("grp", "hd"), None, None),
            P(("grp", "hd"), None, None),
            P("grp"),
            P(("grp", "hd"), None, None),
            P(None, None, ("grp", "hd")),
            P(None, None, ("grp", "hd")),
            P(None, ("grp", "hd")),
            P(None, ("grp", "hd")),
            P(None, ("grp", "hd")),
            P(None, None, ("grp", "hd")),
            P(None, None, ("grp", "hd")),
            P(None, None, ("grp", "hd")),
            P(None, None, ("grp", "hd")),
            P(None, ("grp", "hd")),
            P(None, ("grp", "hd")),
            P(None, ("grp", "hd")),
            P(None, ("grp", "hd")),
            P(None, ("grp", "hd")),
            P(None, ("grp", "hd")),
        ),
        out_specs=(
            P(("grp", "hd"), None, None),
            P(("grp", "hd"), None, None),
            P(("grp", "hd"), None, None),
            P(None, None, ("grp", "hd")),
            P(None, None, ("grp", "hd")),
            P(None, None, ("grp", "hd")),
            P(None, None, ("grp", "hd")),
            P(None, None, ("grp", "hd")),
            P(None, None, ("grp", "hd")),
            P(None, ("grp", "hd")),
            P(None, ("grp", "hd")),
            P(None, ("grp", "hd")),
            P(None, ("grp", "hd")),
            P(None, ("grp", "hd")),
            P(None, ("grp", "hd")),
            P(None, ("grp", "hd")),
            P(None, ("grp", "hd")),
            P(("grp", "hd")),
            P(None, ("grp", "hd")),
        ),
        check_vma=False,
    )
```

time: 727 us -> 552 us (0.76)
  waiting for transfers between devices: 326 us -> 152 us
  local copies, waits for them, and re-layouts: 65.2 us -> 34.7 us
  other arithmetic: 29.3 us -> 57.1 us
  Pallas kernels: 212 us -> 199 us
  between operations: 3.46 us -> 15.6 us
    ppermute x106 -> x49, waiting for transfers between devices: 326 us -> 132 us  [swap(): return lax.ppermute(block, AXES, [(j, j ^ 1 << bit) for j in range(total)])]
    ppermute x106 -> x49, starting transfers between devices: 85.4 us -> 46.7 us  [swap(): return lax.ppermute(block, AXES, [(j, j ^ 1 << bit) for j in range(total)])]
    unnamed x294 -> x146, local copies, waits for them, and re-layouts: 62.5 us -> 24.7 us
    all_to_all x0 -> x7, starting transfers between devices: none -> 36.7 us  [the longest x5 24.6 us: start(): self.under_way = [exchange() for exchange in self.wanted]]
    all_to_all x0 -> x7, waiting for transfers between devices: none -> 20.3 us  [the longest x5 19 us: start(): self.under_way = [exchange() for exchange in self.wanted]]
    pallas_call x15 -> x10, Pallas kernels: 177 us -> 159 us  [the longest x2 49.7 us: mlp_forward(): pl.pallas_call(functools.partial(mlp_forward_kernel, call, depth), grid=(...]
    another operation x0 -> x15, other arithmetic: none -> 10.6 us  [scatter_steps(): both = jnp.stack([added(held[k], came[k]) for k in range(2)], axis=1)]
    convert_element_type x41 -> x16, other arithmetic: 19.7 us -> 30 us  [the longest x15 30 us: added(): return (a.astype(F32) + b.astype(F32)).astype(LOW)]
  transfers between devices with their start and end apart: 106 -> 57, of which waited for: 37 -> 26; matrix products, arithmetic and copies ran while one was open for 4% -> 11% of each run, Pallas kernels for 12% -> 32%
where the time goes in v2:
time: 552 us; the launch traced here: 542 us
  Pallas kernels  199 us (36%)
  waiting for transfers between devices  152 us (28%)
  starting transfers between devices  83.4 us (15%)
  other arithmetic  57.1 us (10%)
  local copies, waits for them, and re-layouts  34.7 us (6%)
  between operations  15.6 us (3%)
    ppermute x49, waiting for transfers between devices, swap(): return lax.ppermute(block, AXES, [(j, j ^ 1 << bit) for j in range(total)])  132 us
    pallas_call x2, Pallas kernels, mlp_forward(): pl.pallas_call(functools.partial(mlp_forward_kernel, call, depth), grid=(...  49.7 us
    ppermute x49, starting transfers between devices, swap(): return lax.ppermute(block, AXES, [(j, j ^ 1 << bit) for j in range(total)])  46.7 us
    pallas_call x2, Pallas kernels, attend_block(): pl.pallas_call(functools.partial(attend_kernel, cross, images, rows // im...  40.5 us
    pallas_call x2, Pallas kernels, scores_grad(): pl.pallas_call(functools.partial(scores_grad_kernel, cross, images, rows...  31.8 us
    convert_element_type x15, other arithmetic, added(): return (a.astype(F32) + b.astype(F32)).astype(LOW)  30 us
    pallas_call x2, Pallas kernels, project_grad(): pl.pallas_call(functools.partial(project_grad_kernel, cross), out_shape=[...  27.7 us
    pallas_call x1, Pallas kernels, mlp_backward(): pl.pallas_call(functools.partial(mlp_backward_kernel, depth), grid=(hidde...  24.9 us
  transfers between devices with their start and end apart: 57, of which 26 were waited for; matrix products, arithmetic and copies ran while one was open for 11% of the time, Pallas kernels for 32%

profile of v2, /device:TPU:0, one launch (start us, length us, event | category | flops | bytes accessed | tf_op | source)
XLA Modules:
  0.0 542.0 jit_solution(16316239152926224476)
XLA Ops:
  12.3 4.0 collective-permute-start
  16.4 1.8 collective-permute-start.2
  18.2 1.5 collective-permute-start.3
  20.7 1.8 collective-permute-done.3
  22.5 8.1 %collective-permute-done = bf16[1,96,1024]{2,1,0:T(8,128)(2,1)S(1)} collective-permute-done((bf16[1,96,1024]{2,1,0:T(8,128)(2,1)S(1)}, bf16[1,96,1024]{2,1,0:T(8,128)(2,1)S(1)}, u32[]{:S(2)}, u32[]{:S(2)}) %collective-permute-start) | collective-permute-done | bytes 196640 | tf_op jit(solution)/shard_map/ppermute | solution.py:42
  30.5 3.4 collective-permute-done.1
  36.2 1.6 collective-permute-start.6
  37.8 1.6 collective-permute-start.7
  39.4 1.8 collective-permute-done.6
  41.2 1.7 collective-permute-done.7
  42.9 3.2 collective-permute-done.4
  46.1 6.7 %collective-permute-done.5 = bf16[2,96,1024]{2,1,0:T(8,128)(2,1)S(1)} collective-permute-done((bf16[2,96,1024]{2,1,0:T(8,128)(2,1)S(1)}, bf16[2,96,1024]{2,1,0:T(8,128)(2,1)S(1)}, u32[]{:S(2)}, u32[]{:S(2)}) %collective-permute-start.5) | collective-permute-done | bytes 393248 | tf_op jit(solution)/shard_map/ppermute | solution.py:42
  53.5 6.7 %all-to-all-start = ((bf16[32,1,128]{2,1,0:T(2,128)(2,1)}), bf16[32,1,128]{2,1,0:T(2,128)(2,1)}, u32[]{:S(2)}, u32[]{:S(2)}) async-start(bf16[32,1,128]{2,1,0:T(2,128)(2,1)} %broadcast_in_dim.8), calls=%async_computation | async-start | bytes 32768 | tf_op jit(solution)/shard_map/all_to_all | solution.py:174
  61.9 1.7 collective-permute-start.8
  71.1 1.8 collective-permute-start.11
  75.2 21.1 %collective-permute-done.10 = bf16[4,32,1024]{2,1,0:T(8,128)(2,1)S(1)} collective-permute-done((bf16[4,32,1024]{2,1,0:T(8,128)(2,1)S(1)}, bf16[4,32,1024]{2,1,0:T(8,128)(2,1)S(1)}, u32[]{:S(2)}, u32[]{:S(2)}) %collective-permute-start.10) | collective-permute-done | bytes 262176 | tf_op jit(solution)/shard_map/ppermute | solution.py:42
  96.2 5.7 %collective-permute-done.11 = bf16[4,32,1024]{2,1,0:T(8,128)(2,1)S(1)} collective-permute-done((bf16[4,32,1024]{2,1,0:T(8,128)(2,1)S(1)}, bf16[4,32,1024]{2,1,0:T(8,128)(2,1)S(1)}, u32[]{:S(2)}, u32[]{:S(2)}) %collective-permute-start.11) | collective-permute-done | bytes 262176 | tf_op jit(solution)/shard_map/ppermute | solution.py:42
  106.4 2.1 collective-permute-start.15
  108.5 19.8 %collective-permute-done.14.refs_9_ = bf16[8,32,1024]{2,1,0:T(8,128)(2,1)S(1)} collective-permute-done((bf16[8,32,1024]{2,1,0:T(8,128)(2,1)S(1)}, bf16[8,32,1024]{2,1,0:T(8,128)(2,1)S(1)}, u32[]{:S(2)}, u32[]{:S(2)}) %collective-permute-start.14) | collective-permute-done | bytes 524320 | tf_op jit(solution)/shard_map/ppermute | solution.py:42
  128.3 18.5 %collective-permute-done.15.refs_7_ = bf16[8,32,1024]{2,1,0:T(8,128)(2,1)S(1)} collective-permute-done((bf16[8,32,1024]{2,1,0:T(8,128)(2,1)S(1)}, bf16[8,32,1024]{2,1,0:T(8,128)(2,1)S(1)}, u32[]{:S(2)}, u32[]{:S(2)}) %collective-permute-start.15) | collective-permute-done | bytes 524320 | tf_op jit(solution)/shard_map/ppermute | solution.py:42
  146.8 2.7 collective-permute-done.13.refs_3_
  150.0 3.4 collective-permute-done.22.refs_8_
  157.0 2.2 collective-permute-done.23.refs_9_
  159.2 1.9 collective-permute-done.19.refs_5_
  161.2 20.4 %shard_map.340 = (bf16[768,1024]{1,0:T(8,128)(2,1)S(1)}, bf16[768,1024]{1,0:T(8,128)(2,1)S(1)}, bf16[768,1024]{1,0:T(8,128)(2,1)}, bf16[768,1024]{1,0:T(8,128)(2...) custom-call(s32[3]{0:T(128)S(1)} %dynamic_slice.3.refs_0_, ...), custom_call_target="tpu_custom_call" | custom-call | flops 7247757312 | bytes 17825792 | tf_op jit(solution)/shard_map/pallas_call | solution.py:284
  184.7 20.1 %shard_map.341 = (bf16[768,1024]{1,0:T(8,128)(2,1)S(1)}, bf16[768,1024]{1,0:T(8,128)(2,1)S(1)}, bf16[768,1024]{1,0:T(8,128)(2,1)}, bf16[768,1024]{1,0:T(8,128)(2...) custom-call(f32[4,1024]{1,0:T(4,128)S(1)} %reshape.239.refs_1_.refs_0_, ...), custom_call_target="tpu_custom_call" | custom-call | flops 7247757312 | bytes 17825792 | tf_op jit(solution)/shard_map/pallas_call | solution.py:284
  207.2 24.7 %shard_map.342 = (bf16[768,1024]{1,0:T(8,128)(2,1)}, f32[768,1024]{1,0:T(8,128)}, bf16[768,2048]{1,0:T(8,128)(2,1)}, bf16[2,16,32,1024]{3,2,1,0:T(8,128)(2,1)}, bf16[2,16,32,1024]{3,2,1,0:T(8,128)(2,1)}) custom-call(f32[768,1024]{1,0:T(8,128)} %get-tuple-element.176.second, bf16[768,1024]{1,0:T(8,128)(2,1)} %bitcast.213, f32[1,1024]{1,0:T(1,128)} %slice.292.refs_0_.gain_row, ...), custom_call_target="tpu_custom_call" | custom-call | flops 12884901888 | bytes 25165824 | tf_op jit(solution)/shard_map/pallas_call | solution.py:579
  232.2 25.0 %shard_map.343 = (bf16[768,1024]{1,0:T(8,128)(2,1)}, bf16[768,2048]{1,0:T(8,128)(2,1)}, bf16[2,16,32,1024]{3,2,1,0:T(8,128)(2,1)}, bf16[2,16,32,1024]{3,2,1,0:T(8,128)(2,1)}) custom-call(f32[768,1024]{1,0:T(8,128)} %get-tuple-element.179.second, bf16[768,1024]{1,0:T(8,128)(2,1)} %bitcast.214, bf16[768,1024]{1,0:T(8,128)(2,1)} %get-tuple-element.180.refs_0_.normal, ...), custom_call_target="tpu_custom_call" | custom-call | flops 12884901888 | bytes 25165824 | tf_op jit(solution)/shard_map/pallas_call | solution.py:579
  257.6 1.9 add_convert_fusion.22
  260.9 1.6 collective-permute-start.26
  262.5 24.9 %shard_map.344 = (f32[768,1024]{1,0:T(8,128)}, f32[1,1024]{1,0:T(1,128)}, bf16[2,16,512,128]{3,2,1,0:T(8,128)(2,1)}, bf16[2,16,512,128]{3,2,1,0:T(8,128)(2,1)}) custom-call(f32[1,1024]{1,0:T(1,128)} %slice.292.refs_0_.gain_row, f32[768,1024]{1,0:T(8,128)} %get-tuple-element.176.second, bf16[768,1024]{1,0:T(8,128)(2,1)} %bitcast.215, ...), custom_call_target="tpu_custom_call" | custom-call | flops 12884901888 | bytes 32505856 | tf_op jit(solution)/shard_map/pallas_call | solution.py:666
  288.2 2.0 add_convert_fusion.18
  292.3 1.7 collective-permute-start.29
  294.0 16.1 %shard_map.345 = (bf16[768,1024]{1,0:T(8,128)(2,1)S(1)}, bf16[768,1024]{1,0:T(8,128)(2,1)S(1)}, bf16[768,1024]{1,0:T(8,128)(2,1)S(1)}) custom-call(f32[768,1024]{1,0:T(8,128)} %get-tuple-element.200.refs_0_.refs_2_, bf16[768,1024]{1,0:T(8,128)(2,1)} %copy-done.7, bf16[768,1024]{1,0:T(8,128)(2,1)} %copy-done.8, bf16[768,1024]{1,0:T(8,128)(2,1)} %get-tuple-element.203.refs_3_, ...), custom_call_target="tpu_custom_call" | custom-call | flops 3623878656 | bytes 18350080 | tf_op jit(solution)/shard_map/pallas_call | solution.py:342
  313.0 4.6 all-to-all-start.1
  317.7 5.4 %add_convert_fusion.8 = (bf16[1,8,512,128]{3,2,1,0:T(8,128)(2,1)}, bf16[1,8,512,128]{3,2,1,0:T(8,128)(2,1)}, bf16[8,512,128]{2,1,0:T(8,128)(2,1)}, bf16[8,512,128]{2,1,0:T(8,128)(2,1)}) fusion(bf16[2,16,512,128]{3,2,1,0:T(8,128)(2,1)} %collective-permute-done.32, bf16[2,16,512,128]{3,2,1,0:T(8,128)(2,1)} %get-tuple-element.214), kind=kLoop, calls=%fused_computation.11 | loop fusion | flops 8388608 | bytes 12582912 | tf_op jit(solution)/shard_map/convert_element_type | solution.py:51
  324.4 1.5 collective-permute-start.33
  326.0 1.5 collective-permute-start.34
  327.5 11.6 %shard_map.346 = (bf16[2,16,64,1024]{3,2,1,0:T(8,128)(2,1)}, bf16[2,16,64,1024]{3,2,1,0:T(8,128)(2,1)}) custom-call(f32[4,1024]{1,0:T(4,128)S(1)} %reshape.239.refs_1_.refs_0_, f32[768,1024]{1,0:T(8,128)} %get-tuple-element.171.refs_1_, f32[768,1024]{1,0:T(8,128)} %get-tuple-element.200.refs_0_.refs_2_, bf16[768,1024]{1,0:T(8,128)(2,1)S(1)} %copy-done.6, ...), custom_call_target="tpu_custom_call" | custom-call | flops 6442450944 | bytes 20971520 | tf_op jit(solution)/shard_map/pallas_call | solution.py:424
  339.1 14.3 %collective-permute-done.33 = bf16[4,32,1024]{2,1,0:T(8,128)(2,1)S(1)} collective-permute-done((bf16[4,32,1024]{2,1,0:T(8,128)(2,1)S(1)}, bf16[4,32,1024]{2,1,0:T(8,128)(2,1)S(1)}, u32[]{:S(2)}, u32[]{:S(2)}) %collective-permute-start.33) | collective-permute-done | bytes 262176 | tf_op jit(solution)/shard_map/ppermute | solution.py:42
  357.6 5.0 all-to-all-start.2
  366.1 1.5 collective-permute-start.38
  367.6 13.3 %shard_map.347 = (f32[768,1024]{1,0:T(8,128)}, f32[1,1024]{1,0:T(1,128)S(1)}) custom-call(f32[4,1024]{1,0:T(4,128)S(1)} %reshape.239.refs_1_.refs_0_, f32[768,1024]{1,0:T(8,128)} %get-tuple-element.171.refs_1_, f32[768,1024]{1,0:T(8,128)} %get-tuple-element.200.refs_0_.refs_2_, bf16[768,1024]{1,0:T(8,128)(2,1)S(1)} %get-tuple-element.216.refs_4_.refs_3_, ...), custom_call_target="tpu_custom_call" | custom-call | flops 4831838208 | bytes 22020096 | tf_op jit(solution)/shard_map/pallas_call | solution.py:479
  381.8 1.6 fusion.26
  385.9 5.1 all-to-all-start.3
  391.0 5.4 add_convert_fusion.4
  398.3 15.7 %shard_map.348 = (bf16[768,1024]{1,0:T(8,128)(2,1)S(1)}, bf16[768,1024]{1,0:T(8,128)(2,1)S(1)}, bf16[768,1024]{1,0:T(8,128)(2,1)S(1)}) custom-call(s32[3]{0:T(128)S(1)} %copy-done.25, f32[768,1024]{1,0:T(8,128)} %get-tuple-element.232.refs_1_.refs_3_, bf16[768,1024]{1,0:T(8,128)(2,1)} %copy-done.12, bf16[768,1024]{1,0:T(8,128)(2,1)} %copy-done.13, ...), custom_call_target="tpu_custom_call" | custom-call | flops 3623878656 | bytes 18350080 | tf_op jit(solution)/shard_map/pallas_call | solution.py:342
  417.6 2.9 collective-permute-done.40
  422.9 1.5 collective-permute-start.42
  428.1 11.9 %shard_map.349 = (bf16[2,16,64,1024]{3,2,1,0:T(8,128)(2,1)}, bf16[2,16,64,1024]{3,2,1,0:T(8,128)(2,1)}) custom-call(f32[4,1024]{1,0:T(4,128)S(1)} %reshape.239.refs_1_.refs_0_, bf16[768,1024]{1,0:T(8,128)(2,1)S(1)} %bitcast.198, bf16[768,1024]{1,0:T(8,128)(2,1)S(1)} %bitcast.201, f32[768,1024]{1,0:T(8,128)} %get-tuple-element.232.refs_1_.refs_3_, ...), custom_call_target="tpu_custom_call" | custom-call | flops 6442450944 | bytes 20971520 | tf_op jit(solution)/shard_map/pallas_call | solution.py:424
  443.2 5.1 all-to-all-start.4
  448.3 5.8 %add_convert_fusion = (bf16[1,8,64,1024]{3,2,1,0:T(8,128)(2,1)}, bf16[1,8,64,1024]{3,2,1,0:T(8,128)(2,1)}, bf16[8,64,1024]{2,1,0:T(8,128)(2,1)}, bf16[8,64,1024]{2,1,0:T(8,128)(2,1)}) fusion(bf16[2,16,64,1024]{3,2,1,0:T(8,128)(2,1)} %collective-permute-done.44, bf16[2,16,64,1024]{3,2,1,0:T(8,128)(2,1)} %get-tuple-element.251), kind=kLoop, calls=%fused_computation.3 | loop fusion | flops 8388608 | bytes 12582912 | tf_op jit(solution)/shard_map/convert_element_type | solution.py:51
  457.1 14.3 %shard_map.350 = (f32[768,1024]{1,0:T(8,128)}, f32[768,1024]{1,0:T(8,128)}, f32[1,1024]{1,0:T(1,128)S(1)}, f32[1,1024]{1,0:T(1,128)S(1)}) custom-call(f32[4,1024]{1,0:T(4,128)S(1)} %reshape.239.refs_1_.refs_0_, bf16[768,1024]{1,0:T(8,128)(2,1)S(1)} %bitcast.199, bf16[768,1024]{1,0:T(8,128)(2,1)S(1)} %bitcast.202, ...), custom_call_target="tpu_custom_call" | custom-call | flops 4831838208 | bytes 22020096 | tf_op jit(solution)/shard_map/pallas_call | solution.py:479
  471.5 3.1 all-to-all-done.4
  474.5 5.0 collective-permute-done.45
  482.5 2.2 fusion.7
  487.7 5.4 all-to-all-start.6
  493.1 1.6 collective-permute-done.47
  494.7 2.8 collective-permute-done.48
  501.7 4.9 all-to-all-start.5
  508.0 1.5 convert_reduce_fusion
  513.9 16.0 %all-to-all-done.5 = bf16[4,2,64,1024]{3,2,1,0:T(8,128)(2,1)S(1)} async-done(((bf16[4,2,64,1024]{3,2,1,0:T(8,128)(2,1)}), bf16[4,2,64,1024]{3,2,1,0:T(8,128)(2,1)S(1)}, u32[]{:S(2)}, u32[]{:S(2)}) %all-to-all-start.5) | async-done | bytes 1048608 | tf_op jit(solution)/shard_map/all_to_all | solution.py:90
  530.8 1.9 multiply_subtract_fusion.3
  532.8 1.8 multiply_subtract_fusion
  (289 shorter events, 88.7 us)
Async XLA Ops:
  7.2 200.0 %all-gather.3.cloned.1.call-start = ((), (), s32[]{:S(2)}) async-start(), calls=%async_computation.7 | async-start | bytes 17301504 | tf_op jit(solution)/shard_map/all_gather | solution.py:743
  11.4 41.4 %copy-start.60 = (f32[4,32]{1,0:T(4,128)S(1)}, f32[4,32]{1,0:T(4,128)}, u32[]{:S(2)}) copy-start(f32[4,32]{1,0:T(4,128)} %param.29) | copy-start | bytes 1540
  12.3 18.2 %collective-permute-start = (bf16[1,96,1024]{2,1,0:T(8,128)(2,1)S(1)}, bf16[1,96,1024]{2,1,0:T(8,128)(2,1)S(1)}, u32[]{:S(2)}, u32[]{:S(2)}) collective-permute-start(bf16[1,96,1024]{2,1,0:T(8,128)(2,1)S(1)} %get-tuple-element.145), channel_id=1, source_target_pairs={{0,2},{1,3},{2,0},{3,1},{4,6},{5,7},{6,4},{7,5},{8,10},{9,11},{10,... | collective-permute-start | bytes 589832 | tf_op jit(solution)/shard_map/ppermute | solution.py:42
  16.4 17.5 %collective-permute-start.1 = (bf16[1,96,1024]{2,1,0:T(8,128)(2,1)S(1)}, bf16[1,96,1024]{2,1,0:T(8,128)(2,1)S(1)}, u32[]{:S(2)}, u32[]{:S(2)}) collective-permute-start(bf16[1,96,1024]{2,1,0:T(8,128)(2,1)S(1)} %get-tuple-element.146), channel_id=1, source_target_pairs={{0,2},{1,3},{2,0},{3,1},{4,6},{5,7},{6,4},{7,5},{8,10},{9,11},{10,... | collective-permute-start | bytes 589832 | tf_op jit(solution)/shard_map/ppermute | solution.py:42
  16.4 4.3 collective-permute-start.2
  18.2 4.3 collective-permute-start.3
  34.0 12.1 %collective-permute-start.4 = (bf16[2,96,1024]{2,1,0:T(8,128)(2,1)S(1)}, bf16[2,96,1024]{2,1,0:T(8,128)(2,1)S(1)}, u32[]{:S(2)}, u32[]{:S(2)}) collective-permute-start(bf16[2,96,1024]{2,1,0:T(8,128)(2,1)S(1)} %pad_maximum_fusion.8), channel_id=1, source_target_pairs={{0,1},{1,0},{2,3},{3,2},{4,5},{5,4},{6,7},{7,6},{8,9},{9,8},{10,11... | collective-permute-start | bytes 1179656 | tf_op jit(solution)/shard_map/ppermute | solution.py:42
  34.8 18.0 %collective-permute-start.5 = (bf16[2,96,1024]{2,1,0:T(8,128)(2,1)S(1)}, bf16[2,96,1024]{2,1,0:T(8,128)(2,1)S(1)}, u32[]{:S(2)}, u32[]{:S(2)}) collective-permute-start(bf16[2,96,1024]{2,1,0:T(8,128)(2,1)S(1)} %pad_maximum_fusion.9), channel_id=1, source_target_pairs={{0,1},{1,0},{2,3},{3,2},{4,5},{5,4},{6,7},{7,6},{8,9},{9,8},{10,11... | collective-permute-start | bytes 1179656 | tf_op jit(solution)/shard_map/ppermute | solution.py:42
  36.2 5.0 collective-permute-start.6
  37.8 5.0 collective-permute-start.7
  53.5 13.7 %all-to-all-start = ((bf16[32,1,128]{2,1,0:T(2,128)(2,1)}), bf16[32,1,128]{2,1,0:T(2,128)(2,1)}, u32[]{:S(2)}, u32[]{:S(2)}) async-start(bf16[32,1,128]{2,1,0:T(2,128)(2,1)} %broadcast_in_dim.8), calls=%async_computation | async-start | bytes 32768 | tf_op jit(solution)/shard_map/all_to_all | solution.py:174
  61.9 40.0 %collective-permute-start.8 = (bf16[4,96,1024]{2,1,0:T(8,128)(2,1)}, bf16[4,96,1024]{2,1,0:T(8,128)(2,1)S(1)}, u32[]{:S(2)}, u32[]{:S(2)}) collective-permute-start(bf16[4,96,1024]{2,1,0:T(8,128)(2,1)} %pad_maximum_fusion.3), channel_id=1, source_target_pairs={{0,8},{1,9},{2,10},{3,11},{4,12},{5,13},{6,14},{7,15},{8,0},{9,1},... | collective-permute-start | bytes 2359304 | tf_op jit(solution)/shard_map/ppermute | solution.py:42
  64.6 37.4 %collective-permute-start.9 = (bf16[4,96,1024]{2,1,0:T(8,128)(2,1)}, bf16[4,96,1024]{2,1,0:T(8,128)(2,1)S(1)}, u32[]{:S(2)}, u32[]{:S(2)}) collective-permute-start(bf16[4,96,1024]{2,1,0:T(8,128)(2,1)} %pad_maximum_fusion.4), channel_id=1, source_target_pairs={{0,16},{1,17},{2,18},{3,19},{4,20},{5,21},{6,22},{7,23},{8,24},{9,... | collective-permute-start | bytes 2359304 | tf_op jit(solution)/shard_map/ppermute | solution.py:42
  68.9 27.3 %collective-permute-start.10 = (bf16[4,32,1024]{2,1,0:T(8,128)(2,1)S(1)}, bf16[4,32,1024]{2,1,0:T(8,128)(2,1)S(1)}, u32[]{:S(2)}, u32[]{:S(2)}) collective-permute-start(bf16[4,32,1024]{2,1,0:T(8,128)(2,1)S(1)} %pad_maximum_fusion.10), channel_id=1, source_target_pairs={{0,2},{1,3},{2,0},{3,1},{4,6},{5,7},{6,4},{7,5},{8,10},{9,11},{10,... | collective-permute-start | bytes 786440 | tf_op jit(solution)/shard_map/ppermute | solution.py:42
  71.1 30.8 %collective-permute-start.11 = (bf16[4,32,1024]{2,1,0:T(8,128)(2,1)S(1)}, bf16[4,32,1024]{2,1,0:T(8,128)(2,1)S(1)}, u32[]{:S(2)}, u32[]{:S(2)}) collective-permute-start(bf16[4,32,1024]{2,1,0:T(8,128)(2,1)S(1)} %pad_maximum_fusion.11), channel_id=1, source_target_pairs={{0,2},{1,3},{2,0},{3,1},{4,6},{5,7},{6,4},{7,5},{8,10},{9,11},{10,... | collective-permute-start | bytes 786440 | tf_op jit(solution)/shard_map/ppermute | solution.py:42
  75.2 31.1 %copy-start.54 = (bf16[2,32,1024]{2,1,0:T(8,128)(2,1)S(1)}, bf16[2,32,1024]{2,1,0:T(8,128)(2,1)}, u32[]{:S(2)}) copy-start(bf16[2,32,1024]{2,1,0:T(8,128)(2,1)} %copy-done.53) | copy-start | bytes 393220
  102.9 52.2 %copy-start.67 = (s32[12]{0:T(128)S(1)}, s32[12]{0:T(128)}, u32[]{:S(2)}) copy-start(s32[12]{0:T(128)} %param.23) | copy-start | bytes 148
  102.9 43.9 %collective-permute-start.12 = (bf16[8,96,1024]{2,1,0:T(8,128)(2,1)}, bf16[8,96,1024]{2,1,0:T(8,128)(2,1)}, u32[]{:S(2)}, u32[]{:S(2)}) collective-permute-start(bf16[8,96,1024]{2,1,0:T(8,128)(2,1)} %constant_dynamic-update-slice_fusion.refs_4_), channel_id=1, source_target_pairs={{0,16},{1,17},{2,18},{3,19},{4,20},{5,21},{6,22},{7,23},{8,24},{9,... | collective-permute-start | bytes 4718600 | tf_op jit(solution)/shard_map/ppermute | solution.py:42
  105.0 44.5 %collective-permute-start.13 = (bf16[8,96,1024]{2,1,0:T(8,128)(2,1)}, bf16[8,96,1024]{2,1,0:T(8,128)(2,1)}, u32[]{:S(2)}, u32[]{:S(2)}) collective-permute-start(bf16[8,96,1024]{2,1,0:T(8,128)(2,1)} %constant_dynamic-update-slice_fusion.4.refs_2_), channel_id=1, source_target_pairs={{0,8},{1,9},{2,10},{3,11},{4,12},{5,13},{6,14},{7,15},{8,0},{9,1},... | collective-permute-start | bytes 4718600 | tf_op jit(solution)/shard_map/ppermute | solution.py:42
  106.3 22.0 %collective-permute-start.14 = (bf16[8,32,1024]{2,1,0:T(8,128)(2,1)S(1)}, bf16[8,32,1024]{2,1,0:T(8,128)(2,1)S(1)}, u32[]{:S(2)}, u32[]{:S(2)}) collective-permute-start(bf16[8,32,1024]{2,1,0:T(8,128)(2,1)S(1)} %constant_dynamic-update-slice_fusion.8.refs_8_), channel_id=1, source_target_pairs={{0,1},{1,0},{2,3},{3,2},{4,5},{5,4},{6,7},{7,6},{8,9},{9,8},{10,11... | collective-permute-start | bytes 1572872 | tf_op jit(solution)/shard_map/ppermute | solution.py:42
  106.4 40.4 %collective-permute-start.15 = (bf16[8,32,1024]{2,1,0:T(8,128)(2,1)S(1)}, bf16[8,32,1024]{2,1,0:T(8,128)(2,1)S(1)}, u32[]{:S(2)}, u32[]{:S(2)}) collective-permute-start(bf16[8,32,1024]{2,1,0:T(8,128)(2,1)S(1)} %constant_dynamic-update-slice_fusion.12.refs_6_), channel_id=1, source_target_pairs={{0,1},{1,0},{2,3},{3,2},{4,5},{5,4},{6,7},{7,6},{8,9},{9,8},{10,11... | collective-permute-start | bytes 1572872 | tf_op jit(solution)/shard_map/ppermute | solution.py:42
  108.5 45.1 %collective-permute-start.16 = (bf16[8,96,1024]{2,1,0:T(8,128)(2,1)S(1)}, bf16[8,96,1024]{2,1,0:T(8,128)(2,1)S(1)}, u32[]{:S(2)}, u32[]{:S(2)}) collective-permute-start(bf16[8,96,1024]{2,1,0:T(8,128)(2,1)S(1)} %copy-done.59), channel_id=1, source_target_pairs={{0,4},{1,5},{2,6},{3,7},{4,0},{5,1},{6,2},{7,3},{8,12},{9,13},{10,... | collective-permute-start | bytes 4718600 | tf_op jit(solution)/shard_map/ppermute | solution.py:42
  128.3 27.5 %collective-permute-start.18 = (bf16[8,96,1024]{2,1,0:T(8,128)(2,1)}, bf16[8,96,1024]{2,1,0:T(8,128)(2,1)}, u32[]{:S(2)}, u32[]{:S(2)}) collective-permute-start(bf16[8,96,1024]{2,1,0:T(8,128)(2,1)} %constant_dynamic-update-slice_fusion.4.refs_2_), channel_id=1, source_target_pairs={{0,4},{1,5},{2,6},{3,7},{4,0},{5,1},{6,2},{7,3},{8,12},{9,13},{10,... | collective-permute-start | bytes 4718600 | tf_op jit(solution)/shard_map/ppermute | solution.py:42
  146.8 3.2 collective-permute-start.20
  149.5 9.7 %collective-permute-start.17 = (bf16[8,96,1024]{2,1,0:T(8,128)(2,1)}, bf16[8,96,1024]{2,1,0:T(8,128)(2,1)}, u32[]{:S(2)}, u32[]{:S(2)}) collective-permute-start(bf16[8,96,1024]{2,1,0:T(8,128)(2,1)} %collective-permute-done.12.refs_5_), channel_id=1, source_target_pairs={{0,4},{1,5},{2,6},{3,7},{4,0},{5,1},{6,2},{7,3},{8,12},{9,13},{10,... | collective-permute-start | bytes 4718600 | tf_op jit(solution)/shard_map/ppermute | solution.py:42
  149.5 11.7 %collective-permute-start.19 = (bf16[8,96,1024]{2,1,0:T(8,128)(2,1)}, bf16[8,96,1024]{2,1,0:T(8,128)(2,1)}, u32[]{:S(2)}, u32[]{:S(2)}) collective-permute-start(bf16[8,96,1024]{2,1,0:T(8,128)(2,1)} %collective-permute-done.13.refs_3_), channel_id=1, source_target_pairs={{0,4},{1,5},{2,6},{3,7},{4,0},{5,1},{6,2},{7,3},{8,12},{9,13},{10,... | collective-permute-start | bytes 4718600 | tf_op jit(solution)/shard_map/ppermute | solution.py:42
  150.0 3.4 collective-permute-start.22
  153.4 3.5 collective-permute-start.21
  154.7 4.5 collective-permute-start.23
  155.2 26.4 %copy-start.24 = (s32[3]{0:T(128)}, s32[3]{0:T(128)S(1)}, u32[]{:S(2)}) copy-start(s32[3]{0:T(128)S(1)} %dynamic_slice.3.refs_0_) | copy-start | bytes 40
  232.0 25.2 %collective-permute-start.24 = (bf16[2,16,32,1024]{3,2,1,0:T(8,128)(2,1)}, bf16[2,16,32,1024]{3,2,1,0:T(8,128)(2,1)S(1)}, u32[]{:S(2)}, u32[]{:S(2)}) collective-permute-start(bf16[2,16,32,1024]{3,2,1,0:T(8,128)(2,1)} %get-tuple-element.178), channel_id=1, source_target_pairs={{0,4},{1,5},{2,6},{3,7},{4,0},{5,1},{6,2},{7,3},{8,12},{9,13},{10,... | collective-permute-start | bytes 6291464 | tf_op jit(solution)/shard_map/ppermute | solution.py:42
  232.2 25.4 %copy-start.32 = (bf16[2,16,32,1024]{3,2,1,0:T(8,128)(2,1)S(1)}, bf16[2,16,32,1024]{3,2,1,0:T(8,128)(2,1)}, u32[]{:S(2)}) copy-start(bf16[2,16,32,1024]{3,2,1,0:T(8,128)(2,1)} %get-tuple-element.186) | copy-start | bytes 6291460
  257.2 30.3 %collective-permute-start.27 = (bf16[2,16,32,1024]{3,2,1,0:T(8,128)(2,1)}, bf16[2,16,32,1024]{3,2,1,0:T(8,128)(2,1)S(1)}, u32[]{:S(2)}, u32[]{:S(2)}) collective-permute-start(bf16[2,16,32,1024]{3,2,1,0:T(8,128)(2,1)} %get-tuple-element.188), channel_id=1, source_target_pairs={{0,4},{1,5},{2,6},{3,7},{4,0},{5,1},{6,2},{7,3},{8,12},{9,13},{10,... | collective-permute-start | bytes 6291464 | tf_op jit(solution)/shard_map/ppermute | solution.py:42
  259.5 32.7 %copy-start.35 = (bf16[1,8,32,1024]{3,2,1,0:T(8,128)(2,1)}, bf16[1,8,32,1024]{3,2,1,0:T(8,128)(2,1)S(1)}, u32[]{:S(2)}) copy-start(bf16[1,8,32,1024]{3,2,1,0:T(8,128)(2,1)S(1)} %get-tuple-element.302) | copy-start | bytes 1572868
  259.5 28.0 %collective-permute-start.25 = (bf16[8,32,1024]{2,1,0:T(8,128)(2,1)}, bf16[8,32,1024]{2,1,0:T(8,128)(2,1)S(1)}, u32[]{:S(2)}, u32[]{:S(2)}) collective-permute-start(bf16[8,32,1024]{2,1,0:T(8,128)(2,1)} %get-tuple-element.304), channel_id=1, source_target_pairs={{0,16},{1,17},{2,18},{3,19},{4,20},{5,21},{6,22},{7,23},{8,24},{9,... | collective-permute-start | bytes 1572872 | tf_op jit(solution)/shard_map/ppermute | solution.py:42
  260.9 26.5 %collective-permute-start.26 = (bf16[8,32,1024]{2,1,0:T(8,128)(2,1)S(1)}, bf16[8,32,1024]{2,1,0:T(8,128)(2,1)S(1)}, u32[]{:S(2)}, u32[]{:S(2)}) collective-permute-start(bf16[8,32,1024]{2,1,0:T(8,128)(2,1)S(1)} %get-tuple-element.303), channel_id=1, source_target_pairs={{0,8},{1,9},{2,10},{3,11},{4,12},{5,13},{6,14},{7,15},{8,0},{9,1},... | collective-permute-start | bytes 1572872 | tf_op jit(solution)/shard_map/ppermute | solution.py:42
  262.5 25.7 %copy-start.31 = (bf16[2,16,32,1024]{3,2,1,0:T(8,128)(2,1)S(1)}, bf16[2,16,32,1024]{3,2,1,0:T(8,128)(2,1)}, u32[]{:S(2)}) copy-start(bf16[2,16,32,1024]{3,2,1,0:T(8,128)(2,1)} %get-tuple-element.197) | copy-start | bytes 6291460
  287.5 23.7 %collective-permute-start.32 = (bf16[2,16,512,128]{3,2,1,0:T(8,128)(2,1)}, bf16[2,16,512,128]{3,2,1,0:T(8,128)(2,1)}, u32[]{:S(2)}, u32[]{:S(2)}) collective-permute-start(bf16[2,16,512,128]{3,2,1,0:T(8,128)(2,1)} %get-tuple-element.199), channel_id=1, source_target_pairs={{0,4},{1,5},{2,6},{3,7},{4,0},{5,1},{6,2},{7,3},{8,12},{9,13},{10,... | collective-permute-start | bytes 12582920 | tf_op jit(solution)/shard_map/ppermute | solution.py:42
  287.7 23.5 %collective-permute-start.28 = (bf16[4,32,1024]{2,1,0:T(8,128)(2,1)S(1)}, bf16[4,32,1024]{2,1,0:T(8,128)(2,1)S(1)}, u32[]{:S(2)}, u32[]{:S(2)}) collective-permute-start(bf16[4,32,1024]{2,1,0:T(8,128)(2,1)S(1)} %fusion.37), channel_id=1, source_target_pairs={{0,8},{1,9},{2,10},{3,11},{4,12},{5,13},{6,14},{7,15},{8,0},{9,1},... | collective-permute-start | bytes 786440 | tf_op jit(solution)/shard_map/ppermute | solution.py:42
  290.2 21.0 %collective-permute-start.30 = (bf16[8,32,1024]{2,1,0:T(8,128)(2,1)S(1)}, bf16[8,32,1024]{2,1,0:T(8,128)(2,1)S(1)}, u32[]{:S(2)}, u32[]{:S(2)}) collective-permute-start(bf16[8,32,1024]{2,1,0:T(8,128)(2,1)S(1)} %get-tuple-element.301), channel_id=1, source_target_pairs={{0,16},{1,17},{2,18},{3,19},{4,20},{5,21},{6,22},{7,23},{8,24},{9,... | collective-permute-start | bytes 1572872 | tf_op jit(solution)/shard_map/ppermute | solution.py:42
  290.8 20.5 %collective-permute-start.31 = (bf16[8,32,1024]{2,1,0:T(8,128)(2,1)S(1)}, bf16[8,32,1024]{2,1,0:T(8,128)(2,1)S(1)}, u32[]{:S(2)}, u32[]{:S(2)}) collective-permute-start(bf16[8,32,1024]{2,1,0:T(8,128)(2,1)S(1)} %get-tuple-element.300), channel_id=1, source_target_pairs={{0,8},{1,9},{2,10},{3,11},{4,12},{5,13},{6,14},{7,15},{8,0},{9,1},... | collective-permute-start | bytes 1572872 | tf_op jit(solution)/shard_map/ppermute | solution.py:42
  292.3 18.9 %collective-permute-start.29 = (bf16[4,32,1024]{2,1,0:T(8,128)(2,1)S(1)}, bf16[4,32,1024]{2,1,0:T(8,128)(2,1)S(1)}, u32[]{:S(2)}, u32[]{:S(2)}) collective-permute-start(bf16[4,32,1024]{2,1,0:T(8,128)(2,1)S(1)} %fusion.36), channel_id=1, source_target_pairs={{0,16},{1,17},{2,18},{3,19},{4,20},{5,21},{6,22},{7,23},{8,24},{9,... | collective-permute-start | bytes 786440 | tf_op jit(solution)/shard_map/ppermute | solution.py:42
  313.0 41.1 %all-to-all-start.1 = ((bf16[4,2,32,1024]{3,2,1,0:T(8,128)(2,1)}), bf16[4,2,32,1024]{3,2,1,0:T(8,128)(2,1)}, u32[]{:S(2)}, u32[]{:S(2)}) async-start(bf16[4,2,32,1024]{3,2,1,0:T(8,128)(2,1)} %copy.42), calls=%async_computation.1 | async-start | bytes 1048576 | tf_op jit(solution)/shard_map/all_to_all | solution.py:90
  323.1 31.0 %collective-permute-start.35 = (bf16[8,512,128]{2,1,0:T(8,128)(2,1)}, bf16[8,512,128]{2,1,0:T(8,128)(2,1)}, u32[]{:S(2)}, u32[]{:S(2)}) collective-permute-start(bf16[8,512,128]{2,1,0:T(8,128)(2,1)} %get-tuple-element.297), channel_id=1, source_target_pairs={{0,16},{1,17},{2,18},{3,19},{4,20},{5,21},{6,22},{7,23},{8,24},{9,... | collective-permute-start | bytes 3145736 | tf_op jit(solution)/shard_map/ppermute | solution.py:42
  323.7 30.4 %collective-permute-start.36 = (bf16[8,512,128]{2,1,0:T(8,128)(2,1)}, bf16[8,512,128]{2,1,0:T(8,128)(2,1)}, u32[]{:S(2)}, u32[]{:S(2)}) collective-permute-start(bf16[8,512,128]{2,1,0:T(8,128)(2,1)} %get-tuple-element.296), channel_id=1, source_target_pairs={{0,8},{1,9},{2,10},{3,11},{4,12},{5,13},{6,14},{7,15},{8,0},{9,1},... | collective-permute-start | bytes 3145736 | tf_op jit(solution)/shard_map/ppermute | solution.py:42
  324.4 29.0 %collective-permute-start.33 = (bf16[4,32,1024]{2,1,0:T(8,128)(2,1)S(1)}, bf16[4,32,1024]{2,1,0:T(8,128)(2,1)S(1)}, u32[]{:S(2)}, u32[]{:S(2)}) collective-permute-start(bf16[4,32,1024]{2,1,0:T(8,128)(2,1)S(1)} %fusion.34), channel_id=1, source_target_pairs={{0,8},{1,9},{2,10},{3,11},{4,12},{5,13},{6,14},{7,15},{8,0},{9,1},... | collective-permute-start | bytes 786440 | tf_op jit(solution)/shard_map/ppermute | solution.py:42
  326.0 28.2 %collective-permute-start.34 = (bf16[4,32,1024]{2,1,0:T(8,128)(2,1)S(1)}, bf16[4,32,1024]{2,1,0:T(8,128)(2,1)}, u32[]{:S(2)}, u32[]{:S(2)}) collective-permute-start(bf16[4,32,1024]{2,1,0:T(8,128)(2,1)S(1)} %fusion.33), channel_id=1, source_target_pairs={{0,16},{1,17},{2,18},{3,19},{4,20},{5,21},{6,22},{7,23},{8,24},{9,... | collective-permute-start | bytes 786440 | tf_op jit(solution)/shard_map/ppermute | solution.py:42
  354.2 27.6 %collective-permute-start.39 = (bf16[2,16,64,1024]{3,2,1,0:T(8,128)(2,1)}, bf16[2,16,64,1024]{3,2,1,0:T(8,128)(2,1)}, u32[]{:S(2)}, u32[]{:S(2)}) collective-permute-start(bf16[2,16,64,1024]{3,2,1,0:T(8,128)(2,1)} %get-tuple-element.226), channel_id=1, source_target_pairs={{0,4},{1,5},{2,6},{3,7},{4,0},{5,1},{6,2},{7,3},{8,12},{9,13},{10,... | collective-permute-start | bytes 12582920 | tf_op jit(solution)/shard_map/ppermute | solution.py:42
  357.6 24.2 %all-to-all-start.2 = ((bf16[4,2,32,1024]{3,2,1,0:T(8,128)(2,1)}), bf16[4,2,32,1024]{3,2,1,0:T(8,128)(2,1)}, u32[]{:S(2)}, u32[]{:S(2)}) async-start(bf16[4,2,32,1024]{3,2,1,0:T(8,128)(2,1)} %copy.43), calls=%async_computation.2 | async-start | bytes 1048576 | tf_op jit(solution)/shard_map/all_to_all | solution.py:90
  364.1 16.9 %collective-permute-start.37 = (bf16[4,512,128]{2,1,0:T(8,128)(2,1)S(1)}, bf16[4,512,128]{2,1,0:T(8,128)(2,1)S(1)}, u32[]{:S(2)}, u32[]{:S(2)}) collective-permute-start(bf16[4,512,128]{2,1,0:T(8,128)(2,1)S(1)} %fusion.17), channel_id=1, source_target_pairs={{0,8},{1,9},{2,10},{3,11},{4,12},{5,13},{6,14},{7,15},{8,0},{9,1},... | collective-permute-start | bytes 1572872 | tf_op jit(solution)/shard_map/ppermute | solution.py:42
  366.1 15.7 %collective-permute-start.38 = (bf16[4,512,128]{2,1,0:T(8,128)(2,1)S(1)}, bf16[4,512,128]{2,1,0:T(8,128)(2,1)}, u32[]{:S(2)}, u32[]{:S(2)}) collective-permute-start(bf16[4,512,128]{2,1,0:T(8,128)(2,1)S(1)} %fusion.16), channel_id=1, source_target_pairs={{0,16},{1,17},{2,18},{3,19},{4,20},{5,21},{6,22},{7,23},{8,24},{9,... | collective-permute-start | bytes 1572872 | tf_op jit(solution)/shard_map/ppermute | solution.py:42
  385.9 35.6 %all-to-all-start.3 = ((bf16[4,2,512,128]{3,2,1,0:T(8,128)(2,1)}), bf16[4,2,512,128]{3,2,1,0:T(8,128)(2,1)}, u32[]{:S(2)}, u32[]{:S(2)}) async-start(bf16[4,2,512,128]{3,2,1,0:T(8,128)(2,1)} %copy.44), calls=%async_computation.3 | async-start | bytes 2097152 | tf_op jit(solution)/shard_map/all_to_all | solution.py:90
  396.3 24.2 %collective-permute-start.40 = (bf16[8,64,1024]{2,1,0:T(8,128)(2,1)S(1)}, bf16[8,64,1024]{2,1,0:T(8,128)(2,1)S(1)}, u32[]{:S(2)}, u32[]{:S(2)}) collective-permute-start(bf16[8,64,1024]{2,1,0:T(8,128)(2,1)S(1)} %get-tuple-element.292), channel_id=1, source_target_pairs={{0,16},{1,17},{2,18},{3,19},{4,20},{5,21},{6,22},{7,23},{8,24},{9,... | collective-permute-start | bytes 3145736 | tf_op jit(solution)/shard_map/ppermute | solution.py:42
  396.9 24.6 %collective-permute-start.41 = (bf16[8,64,1024]{2,1,0:T(8,128)(2,1)S(1)}, bf16[8,64,1024]{2,1,0:T(8,128)(2,1)}, u32[]{:S(2)}, u32[]{:S(2)}) collective-permute-start(bf16[8,64,1024]{2,1,0:T(8,128)(2,1)S(1)} %get-tuple-element.291), channel_id=1, source_target_pairs={{0,8},{1,9},{2,10},{3,11},{4,12},{5,13},{6,14},{7,15},{8,0},{9,1},... | collective-permute-start | bytes 3145736 | tf_op jit(solution)/shard_map/ppermute | solution.py:42
  422.9 17.2 %collective-permute-start.42 = (bf16[4,64,1024]{2,1,0:T(8,128)(2,1)S(1)}, bf16[4,64,1024]{2,1,0:T(8,128)(2,1)S(1)}, u32[]{:S(2)}, u32[]{:S(2)}) collective-permute-start(bf16[4,64,1024]{2,1,0:T(8,128)(2,1)S(1)} %fusion.12), channel_id=1, source_target_pairs={{0,8},{1,9},{2,10},{3,11},{4,12},{5,13},{6,14},{7,15},{8,0},{9,1},... | collective-permute-start | bytes 1572872 | tf_op jit(solution)/shard_map/ppermute | solution.py:42
  425.8 14.3 %collective-permute-start.43 = (bf16[4,64,1024]{2,1,0:T(8,128)(2,1)S(1)}, bf16[4,64,1024]{2,1,0:T(8,128)(2,1)S(1)}, u32[]{:S(2)}, u32[]{:S(2)}) collective-permute-start(bf16[4,64,1024]{2,1,0:T(8,128)(2,1)S(1)} %fusion.11), channel_id=1, source_target_pairs={{0,16},{1,17},{2,18},{3,19},{4,20},{5,21},{6,22},{7,23},{8,24},{9,... | collective-permute-start | bytes 1572872 | tf_op jit(solution)/shard_map/ppermute | solution.py:42
  440.1 8.2 %collective-permute-start.44 = (bf16[2,16,64,1024]{3,2,1,0:T(8,128)(2,1)}, bf16[2,16,64,1024]{3,2,1,0:T(8,128)(2,1)}, u32[]{:S(2)}, u32[]{:S(2)}) collective-permute-start(bf16[2,16,64,1024]{3,2,1,0:T(8,128)(2,1)} %get-tuple-element.252), channel_id=1, source_target_pairs={{0,4},{1,5},{2,6},{3,7},{4,0},{5,1},{6,2},{7,3},{8,12},{9,13},{10,... | collective-permute-start | bytes 12582920 | tf_op jit(solution)/shard_map/ppermute | solution.py:42
  443.2 31.3 %all-to-all-start.4 = ((bf16[4,2,64,1024]{3,2,1,0:T(8,128)(2,1)}), bf16[4,2,64,1024]{3,2,1,0:T(8,128)(2,1)}, u32[]{:S(2)}, u32[]{:S(2)}) async-start(bf16[4,2,64,1024]{3,2,1,0:T(8,128)(2,1)} %copy.45), calls=%async_computation.4 | async-start | bytes 2097152 | tf_op jit(solution)/shard_map/all_to_all | solution.py:90
  454.2 25.4 %collective-permute-start.45 = (bf16[8,64,1024]{2,1,0:T(8,128)(2,1)}, bf16[8,64,1024]{2,1,0:T(8,128)(2,1)}, u32[]{:S(2)}, u32[]{:S(2)}) collective-permute-start(bf16[8,64,1024]{2,1,0:T(8,128)(2,1)} %get-tuple-element.289), channel_id=1, source_target_pairs={{0,16},{1,17},{2,18},{3,19},{4,20},{5,21},{6,22},{7,23},{8,24},{9,... | collective-permute-start | bytes 3145736 | tf_op jit(solution)/shard_map/ppermute | solution.py:42
  455.4 25.1 %collective-permute-start.46 = (bf16[8,64,1024]{2,1,0:T(8,128)(2,1)}, bf16[8,64,1024]{2,1,0:T(8,128)(2,1)}, u32[]{:S(2)}, u32[]{:S(2)}) collective-permute-start(bf16[8,64,1024]{2,1,0:T(8,128)(2,1)} %get-tuple-element.288), channel_id=1, source_target_pairs={{0,8},{1,9},{2,10},{3,11},{4,12},{5,13},{6,14},{7,15},{8,0},{9,1},... | collective-permute-start | bytes 3145736 | tf_op jit(solution)/shard_map/ppermute | solution.py:42
  481.9 12.8 %collective-permute-start.47 = (bf16[4,64,1024]{2,1,0:T(8,128)(2,1)S(1)}, bf16[4,64,1024]{2,1,0:T(8,128)(2,1)}, u32[]{:S(2)}, u32[]{:S(2)}) collective-permute-start(bf16[4,64,1024]{2,1,0:T(8,128)(2,1)S(1)} %fusion.8), channel_id=1, source_target_pairs={{0,8},{1,9},{2,10},{3,11},{4,12},{5,13},{6,14},{7,15},{8,0},{9,1},... | collective-permute-start | bytes 1572872 | tf_op jit(solution)/shard_map/ppermute | solution.py:42
  484.7 12.7 %collective-permute-start.48 = (bf16[4,64,1024]{2,1,0:T(8,128)(2,1)}, bf16[4,64,1024]{2,1,0:T(8,128)(2,1)}, u32[]{:S(2)}, u32[]{:S(2)}) collective-permute-start(bf16[4,64,1024]{2,1,0:T(8,128)(2,1)} %fusion.7), channel_id=1, source_target_pairs={{0,16},{1,17},{2,18},{3,19},{4,20},{5,21},{6,22},{7,23},{8,24},{9,... | collective-permute-start | bytes 1572872 | tf_op jit(solution)/shard_map/ppermute | solution.py:42
  487.7 14.0 %all-to-all-start.6 = ((f32[32,1,128]{2,1,0:T(1,128)}), f32[32,1,128]{2,1,0:T(1,128)S(1)}, u32[]{:S(2)}, u32[]{:S(2)}) async-start(f32[32,1,128]{2,1,0:T(1,128)} %bitcast.62), calls=%async_computation.6 | async-start | bytes 32768 | tf_op jit(solution)/shard_map/all_to_all | solution.py:187
  501.7 28.2 %all-to-all-start.5 = ((bf16[4,2,64,1024]{3,2,1,0:T(8,128)(2,1)}), bf16[4,2,64,1024]{3,2,1,0:T(8,128)(2,1)S(1)}, u32[]{:S(2)}, u32[]{:S(2)}) async-start(bf16[4,2,64,1024]{3,2,1,0:T(8,128)(2,1)} %copy.46), calls=%async_computation.5 | async-start | bytes 2097152 | tf_op jit(solution)/shard_map/all_to_all | solution.py:90
  (61 other events, 354.2 us)
Sparse Core Ops, SparseCore 0:
  52.9 148.7 all-gather.2
